TPU v7x, 32 devices: a whole 2x2x4 slice. The times are simulated.
32 devices in a mesh: row: 4 (over z), col: 8 (over y, x, core).
Axes of the slice: x: 2, y: 2, z: 4, core: 2. Of those that a mesh axis runs over, the one named last changes fastest.
Arguments:
- protocols: float32 [20, 4096], P(None, ('row', 'col')), may hold values from -6 to 6
- w_in: float32 [20, 256], replicated, may hold values from -1.25 to 1.25
- b_in: float32 [256], replicated, may hold values from -3 to 3
- w_out: float32 [256, 64], replicated, may hold values from -0.21875 to 0.21875
- solved: float32 [32, 4096], P(None, ('row', 'col')), may hold values from -0.5 to 0.5
- probes: float32 [32, 4096], P(None, ('row', 'col')), may hold values from -6 to 6
- window_blocks: int32 [4], replicated, may hold values from 0 to 7
Outputs:
- col_grad: float32 [64, 4096], P(None, ('row', 'col'))
- grad_in: float32 [20, 256], replicated
- grad_bias: float32 [256], replicated
- grad_out: float32 [256, 64], replicated
Inputs may be any that keep to these rules, and one draw needn't show every extreme that they name: Window block r is the 128 protocols held at index r of row and index window_blocks[r] of col.
All inputs are finite; a program needn't handle non-finite values.
Results may differ from a plain program's by a relative error of at most 0.0003.
Values sent between devices are 32-bit elements; how exact they have to be, the bound alone decides.
No kernel may reach another device: no remote copies, remote signals or barrier semaphores. Data moves between devices by JAX's collectives and lax.ppermute only.
A program may use at most 64 MiB of HBM per device.

v0:
```python
import jax
import jax.numpy as jnp
from jax import lax
from jax.sharding import PartitionSpec as P

HIGHEST = lax.Precision.HIGHEST


def spread(value, axis, source):
    kept = jnp.where(lax.axis_index(axis) == source, value, 0).astype(value.dtype)
    return lax.psum(kept, axis)


def tile_pass(first_feat, first_vec, second_feat, second_vec):
    first_norm = jnp.sum(first_feat * first_feat, 0)
    second_norm = jnp.sum(second_feat * second_feat, 0)
    cross = jnp.einsum("fi,fj->ij", first_feat, second_feat, precision=HIGHEST)
    kern = jnp.exp(-0.5 * (first_norm[:, None] + second_norm[None, :] - 2.0 * cross))
    weigh = jnp.einsum("qi,qj->ij", first_vec, second_vec, precision=HIGHEST) * kern
    first_grad = (
        jnp.einsum("fj,ij->fi", second_feat, weigh, precision=HIGHEST)
        - first_feat * jnp.sum(weigh, 1)[None, :]
    )
    second_grad = (
        jnp.einsum("fi,ij->fj", first_feat, weigh, precision=HIGHEST)
        - second_feat * jnp.sum(weigh, 0)[None, :]
    )
    return (first_grad, second_grad)


def blocked(first_feat, first_vec, second_feat, second_vec):
    width = second_feat.shape[1]
    block_width = 1024 if width % 1024 == 0 else width
    if block_width == width:
        return tile_pass(first_feat, first_vec, second_feat, second_vec)
    count = width // block_width
    split_feat = second_feat.reshape(second_feat.shape[0], count, block_width).transpose(1, 0, 2)
    split_vec = second_vec.reshape(second_vec.shape[0], count, block_width).transpose(1, 0, 2)

    def partial_pass(running, pair):
        first_part, second_part = tile_pass(first_feat, first_vec, pair[0], pair[1])
        return (running + first_part, second_part)

    first_grad, second_parts = lax.scan(
        partial_pass, jnp.zeros_like(first_feat), (split_feat, split_vec)
    )
    return (first_grad, second_parts.transpose(1, 0, 2).reshape(second_feat.shape[0], width))


def hidden_of(w_in, b_in, inputs):
    return jnp.tanh(jnp.einsum("ph,pn->hn", w_in, inputs, precision=HIGHEST) + b_in[:, None])


def backprop(w_out, inputs, hidden, grads):
    grad_out = jnp.einsum("hn,fn->hf", hidden, grads, precision=HIGHEST)
    grad_hidden = jnp.einsum("hf,fn->hn", w_out, grads, precision=HIGHEST)
    grad_pre = grad_hidden * (1.0 - hidden * hidden)
    grad_in = jnp.einsum("pn,hn->ph", inputs, grad_pre, precision=HIGHEST)
    return (grad_in, jnp.sum(grad_pre, 1), grad_out)


def per_device(protocols, w_in, b_in, w_out, solved, probes, window_blocks):
    hidden = hidden_of(w_in, b_in, protocols)
    features = jnp.einsum("hf,hn->fn", w_out, hidden, precision=HIGHEST)
    owner_col = window_blocks[lax.axis_index("row")]
    window = (
        spread(features, "col", owner_col),
        spread(solved, "col", owner_col),
        spread(protocols, "col", owner_col),
    )
    win_inputs = None
    win_part, col_part = blocked(
        window[0],
        window[1],
        lax.all_gather(features, "row", axis=1, tiled=True),
        lax.all_gather(probes, "row", axis=1, tiled=True),
    )
    col_grad = lax.psum_scatter(col_part, "row", scatter_dimension=1, tiled=True)
    win_inputs = window[2]
    own_terms = backprop(w_out, protocols, hidden, col_grad)
    win_hidden = hidden_of(w_in, b_in, win_inputs)
    win_terms = backprop(w_out, win_inputs, win_hidden, win_part)
    terms = (own_terms[0] + win_terms[0], own_terms[1] + win_terms[1], own_terms[2] + win_terms[2])
    grad_in, grad_bias, grad_out = lax.psum((terms[0], terms[1], terms[2]), ("row", "col"))
    return (col_grad, grad_in, grad_bias, grad_out)


def solution(mesh):
    in_specs = (
        P(None, ("row", "col")),
        P(),
        P(),
        P(),
        P(None, ("row", "col")),
        P(None, ("row", "col")),
        P(),
    )
    out_specs = (P(None, ("row", "col")), P(), P(), P())
    return jax.shard_map(
        per_device, mesh=mesh, in_specs=in_specs, out_specs=out_specs, check_vma=False
    )
```

profile of v0, /device:TPU:0, one launch (start us, length us, event | category | flops | bytes accessed | tf_op | source)
XLA Modules:
  0.0 216.5 jit_solution(12877712772594497762)
XLA Ops:
  7.2 0.0 copy-start
  7.2 0.0 copy-start.5
  7.2 0.0 reduce-scatter.2.cloned.1.call-start
  7.2 0.0 copy-start.7
  7.3 0.6 copy-done.7
  7.9 0.6 dynamic_slice.3
  9.1 0.0 copy-done.5
  9.1 0.0 copy-start.2
  9.2 0.0 copy-start.3
  9.2 0.7 copy-done.2
  9.9 0.0 copy-start.6
  9.9 0.0 copy-done.3
  9.9 0.6 copy-done.6
  10.5 0.3 fusion.6
  10.9 0.0 copy-done
  10.9 0.3 broadcast_select_fusion
  11.1 26.1 %all-reduce.1 = (f32[64,128]{1,0:T(8,128)S(1)}, f32[32,128]{1,0:T(8,128)S(1)}, f32[20,128]{1,0:T(8,128)S(1)}) all-reduce(f32[64,128]{1,0:T(8,128)S(1)} %get-tuple-element.11, f32[32,128]{1,0:T(8,128)S(1)} %broadcast_select_fusion.1, f32[20,128]{1,0:T(8,128)S(1)} %broadcast_select_fusion.2), channel_id=1, replica_groups=mesh['row'=4,'col'=8] {'col'}, use_global_device_ids=true, to_apply=%region_0.1 | all-reduce | flops 14848 | bytes 118784 | tf_op jit(solution)/shard_map/psum | solution.py:11
  37.2 0.0 copy-start.4
  37.3 0.7 copy-done.4
  37.9 13.4 %all_gather.6 = f32[32,512]{1,0:T(8,128)S(1)} all-gather(f32[32,128]{1,0:T(8,128)S(1)} %copy-done.4), channel_id=1, replica_groups=mesh['row'=4,'col'=8] {'row'}, dimensions={1}, use_global_device_ids=true | all-gather | bytes 81920 | tf_op jit(solution)/shard_map/all_gather | solution.py:76
  51.4 13.4 %all_gather.7 = f32[64,512]{1,0:T(8,128)S(1)} all-gather(f32[64,128]{1,0:T(8,128)S(1)} %get-tuple-element.12), channel_id=1, replica_groups=mesh['row'=4,'col'=8] {'row'}, dimensions={1}, use_global_device_ids=true | all-gather | bytes 163840 | tf_op jit(solution)/shard_map/all_gather | solution.py:75
  64.8 0.4 fusion.10
  65.3 0.6 fusion.7
  65.8 0.9 convolution_subtract_fusion
  66.7 0.0 reduce-scatter.2.cloned.1.call-update
  66.8 0.0 all-reduce.4.cloned.1.call-start
  66.8 0.4 convolution_subtract_fusion.1
  67.2 0.3 fusion.5
  67.5 0.3 fusion.9
  67.9 17.4 %reduce-scatter.2.cloned.1.call-done = f32[64,128]{1,0:T(8,128)} async-done(((f32[64,512]{1,0:T(8,128)}), f32[64,128]{1,0:T(8,128)}) %reduce-scatter.2.cloned.1.call-update) | async-done | bytes 32784 | tf_op jit(solution)/shard_map/reduce_scatter | solution.py:78
  85.2 1.0 fusion.11
  86.2 0.8 convolution_add_fusion.2
  87.1 0.0 copy-start.1
  87.1 0.0 all-reduce.4.cloned.1.call-update
  87.1 0.7 copy-done.1
  87.8 0.3 fusion.8
  88.1 0.2 convolution_bitcast_fusion.2
  88.3 0.2 convolution_add_fusion.3
  88.5 39.1 %all-reduce = (f32[20,256]{1,0:T(8,128)}, f32[256]{0:T(256)}) all-reduce(f32[20,256]{1,0:T(8,128)S(1)} %convolution_add_fusion.3, f32[256]{0:T(256)S(1)} %add.65), channel_id=1, replica_groups=mesh['row'=4,'col'=8] {'row','col'}, use_global_device_ids=true, to_apply=%region_8.9 | all-reduce | flops 5376 | bytes 43008 | tf_op jit(solution)/shard_map/psum | solution.py:84
  127.7 80.5 %all-reduce.4.cloned.1.call-done = f32[256,64]{0,1:T(8,128)} async-done(((f32[256,64]{0,1:T(8,128)}), f32[256,64]{0,1:T(8,128)}) %all-reduce.4.cloned.1.call-update) | async-done | bytes 65552 | tf_op jit(solution)/shard_map/psum | solution.py:84
  208.2 1.5 copy.12
  (5 shorter events, 0.1 us)
Async XLA Ops:
  7.2 3.7 %copy-start = (f32[256,64]{0,1:T(8,128)S(1)}, f32[256,64]{0,1:T(8,128)}, u32[]{:S(2)}) copy-start(f32[256,64]{0,1:T(8,128)} %param.10) | copy-start | bytes 196612
  7.2 2.0 copy-start.5
  7.2 78.0 %reduce-scatter.2.cloned.1.call-start = ((), (), s32[]{:S(2)}) async-start(), calls=%async_computation.1 | async-start | bytes 163840 | tf_op jit(solution)/shard_map/reduce_scatter | solution.py:78
  7.2 0.7 copy-start.7
  9.1 0.7 copy-start.2
  9.2 0.7 copy-start.3
  9.9 0.7 copy-start.6
  37.2 0.7 copy-start.4
  66.8 141.4 %all-reduce.4.cloned.1.call-start = ((), (), s32[]{:S(2)}) async-start(), calls=%async_computation.2 | async-start | bytes 131072 | tf_op jit(solution)/shard_map/psum | solution.py:84
  87.1 0.8 copy-start.1
Sparse Core Ops, SparseCore 0:
  66.9 18.3 reduce-scatter.1
  92.3 115.8 all-reduce.3
where the time goes:
time: 218 us; the launch traced here: 216 us
  waiting for transfers between devices  97.9 us (45%)
  blocking collectives  92.1 us (42%)
  between operations  14.9 us (7%)
  matrix products  6.01 us (3%)
  local copies, waits for them, and re-layouts  5.49 us (3%)
    psum x1, waiting for transfers between devices, per_device(): lax.psum((terms[0], terms[1], terms[2]), ('row', 'col'))  80.5 us
    psum x1, blocking collectives, per_device(): lax.psum((terms[0], terms[1], terms[2]), ('row', 'col'))  39.1 us
    psum x1, blocking collectives, spread(): return lax.psum(kept, axis)  26.1 us
    reduce_scatter x1, waiting for transfers between devices, per_device(): lax.psum_scatter(col_part, 'row', scatter_dimension=1, tiled=True)  17.4 us
    all_gather x1, blocking collectives, per_device(): lax.all_gather(features, 'row', axis=1, tiled=True)  13.4 us
    all_gather x1, blocking collectives, per_device(): lax.all_gather(probes, 'row', axis=1, tiled=True)  13.4 us
    unnamed x17, local copies, waits for them, and re-layouts  4.91 us
  transfers between devices with their start and end apart: 2, of which 2 were waited for; matrix products, arithmetic and copies ran while one was open for 1% of the time, Pallas kernels for 0%

commit v1 on v0

v1 whole, which is shorter than its diff:
```python
import jax
import jax.numpy as jnp
from jax import lax
from jax.sharding import PartitionSpec as P

HIGHEST = lax.Precision.HIGHEST


def swap(value, axis, size, bit):
    return lax.ppermute(value, axis, [(i, i ^ bit) for i in range(size)])


def bits_of(size):
    return [1 << k for k in range(size.bit_length() - 1)]


def hidden_of(w_in, b_in, inputs):
    return jnp.tanh(jnp.einsum("ph,pn->hn", w_in, inputs, precision=HIGHEST) + b_in[:, None])


def weight_grads(w_in, b_in, w_out, win_in, solved, col_in, probes):
    inputs = jnp.concatenate([win_in, col_in], 1)
    hidden = hidden_of(w_in, b_in, inputs)
    features = jnp.einsum("hf,hn->fn", w_out, hidden, precision=HIGHEST)
    wide = win_in.shape[1]
    first, second = features[:, :wide], features[:, wide:]
    first_norm = jnp.sum(first * first, 0)
    second_norm = jnp.sum(second * second, 0)
    cross = jnp.einsum("fi,fj->ij", first, second, precision=HIGHEST)
    kern = jnp.exp(-0.5 * (first_norm[:, None] + second_norm[None, :] - 2.0 * cross))
    weigh = jnp.einsum("qi,qj->ij", solved, probes, precision=HIGHEST) * kern
    first_grad = jnp.einsum("fj,ij->fi", second, weigh, precision=HIGHEST) - first * jnp.sum(weigh, 1)[None, :]
    second_grad = jnp.einsum("fi,ij->fj", first, weigh, precision=HIGHEST) - second * jnp.sum(weigh, 0)[None, :]
    grads = jnp.concatenate([first_grad, second_grad], 1)
    grad_out = jnp.einsum("hn,fn->fh", hidden, grads, precision=HIGHEST)
    grad_pre = jnp.einsum("hf,fn->hn", w_out, grads, precision=HIGHEST) * (1.0 - hidden * hidden)
    grad_in = jnp.einsum("pn,hn->ph", inputs, grad_pre, precision=HIGHEST)
    return second_grad, grad_in, jnp.sum(grad_pre, 1), grad_out


def body(n_row, n_col, protocols, w_in, b_in, w_out, solved, probes, window_blocks):
    depth, vecs, own = protocols.shape[0], solved.shape[0], protocols.shape[1]
    apart = lax.axis_index("col") ^ window_blocks[lax.axis_index("row")]
    bits = bits_of(n_col)
    shared, joined = bits[:-1], bits[-1]

    def nearer(bit, mine, theirs):
        return jnp.where((apart & bit) == 0, mine, theirs)

    window = jnp.concatenate([protocols, solved])
    columns = jnp.concatenate([protocols, probes])
    for bit in shared:
        window = nearer(bit, window, swap(window, "col", n_col, bit))
    high = window.shape[0]
    got = swap(jnp.concatenate([window, columns]), "col", n_col, joined)
    window = nearer(joined, window, got[:high])
    blocks = jnp.concatenate([window, columns, got[high:]])[None]
    for bit in reversed(bits_of(n_row)):
        blocks = jnp.concatenate([blocks, swap(blocks, "row", n_row, bit)])

    def laid(start, count):
        part = blocks[:, start : start + count]
        return part.transpose(1, 0, 2).reshape(count, -1)

    win_in, win_vec = laid(0, depth), laid(depth, vecs)
    col_in = jnp.concatenate([laid(high, depth), laid(2 * high, depth)], 1)
    col_vec = jnp.concatenate([laid(high + depth, vecs), laid(2 * high + depth, vecs)], 1)
    col_grad, grad_in, grad_bias, grad_out = weight_grads(w_in, b_in, w_out, win_in, win_vec, col_in, col_vec)
    pack = jnp.concatenate([grad_out, grad_in, grad_bias[None]])
    for bit in reversed(shared):
        pack = pack + swap(pack, "col", n_col, bit)
    feats = grad_out.shape[0]
    return (col_grad[:, :own], pack[feats : feats + depth], pack[feats + depth], pack[:feats].T)


def solution(mesh):
    n_row, n_col = mesh.shape["row"], mesh.shape["col"]
    split = P(None, ("row", "col"))

    def per_device(*args):
        return body(n_row, n_col, *args)

    return jax.shard_map(
        per_device,
        mesh=mesh,
        in_specs=(split, P(), P(), P(), split, split, P()),
        out_specs=(split, P(), P(), P()),
        check_vma=False,
    )
```

time: 218 us -> 48.5 us (0.22)
  blocking collectives: 92.1 us -> 0 us
  waiting for transfers between devices: 97.9 us -> 13.3 us
  between operations: 14.9 us -> 1.53 us
  starting transfers between devices: 0.08 us -> 12 us
  matrix products: 6.01 us -> 14.1 us
  other arithmetic: 0.07 us -> 3.12 us
    psum x1 -> x0, waiting for transfers between devices: 80.5 us -> none  [per_device(): lax.psum((terms[0], terms[1], terms[2]), ('row', 'col'))]
    psum x2 -> x0, blocking collectives: 65.2 us -> none  [the longest x1 39.1 us: per_device(): lax.psum((terms[0], terms[1], terms[2]), ('row', 'col'))]
    all_gather x2 -> x0, blocking collectives: 26.8 us -> none  [the longest x1 13.4 us: per_device(): lax.all_gather(features, 'row', axis=1, tiled=True)]
    reduce_scatter x1 -> x0, waiting for transfers between devices: 17.4 us -> none  [per_device(): lax.psum_scatter(col_part, 'row', scatter_dimension=1, tiled=True)]
    ppermute x0 -> x7, waiting for transfers between devices: none -> 13.3 us  [swap(): return lax.ppermute(value, axis, [(i, i ^ bit) for i in range(size)])]
    ppermute x0 -> x7, starting transfers between devices: none -> 12 us  [swap(): return lax.ppermute(value, axis, [(i, i ^ bit) for i in range(size)])]
    dot_general x11 -> x8, matrix products: 5.37 us -> 12.6 us  [the longest x1 2.45 us: weight_grads(): cross = jnp.einsum('fi,fj->ij', first, second, precision=HIGHEST)]
    unnamed x17 -> x14, local copies, waits for them, and re-layouts: 4.91 us -> 0.08 us
  transfers between devices with their start and end apart: 2 -> 7, of which waited for: 2 -> 6; matrix products, arithmetic and copies ran while one was open for 1% -> 4% of each run, Pallas kernels for 0% -> 0%
where the time goes in v1:
time: 48.5 us; the launch traced here: 47.8 us
  matrix products  14.1 us (29%)
  waiting for transfers between devices  13.3 us (27%)
  starting transfers between devices  12 us (25%)
  local copies, waits for them, and re-layouts  3.8 us (8%)
  other arithmetic  3.12 us (6%)
  between operations  1.53 us (3%)
    ppermute x7, waiting for transfers between devices, swap(): return lax.ppermute(value, axis, [(i, i ^ bit) for i in range(size)])  13.3 us
    ppermute x7, starting transfers between devices, swap(): return lax.ppermute(value, axis, [(i, i ^ bit) for i in range(size)])  12 us
    dot_general x1, matrix products, weight_grads(): cross = jnp.einsum('fi,fj->ij', first, second, precision=HIGHEST)  2.45 us
    dot_general x1, matrix products, weight_grads(): jnp.einsum('fj,ij->fi', second, weigh, precision=HIGHEST)  2.14 us
    dot_general x1, matrix products, weight_grads(): weigh = jnp.einsum('qi,qj->ij', solved, probes, precision=HIGHEST) * kern  1.84 us
    dot_general x1, matrix products, weight_grads(): features = jnp.einsum('hf,hn->fn', w_out, hidden, precision=HIGHEST)  1.65 us
    dot_general x1, matrix products, weight_grads(): jnp.einsum('hf,fn->hn', w_out, grads, precision=HIGHEST)  1.51 us
    dot_general x1, matrix products, hidden_of(): jnp.einsum('ph,pn->hn', w_in, inputs, precision=HIGHEST) + b_in[:, None]  1.44 us
  transfers between devices with their start and end apart: 7, of which 6 were waited for; matrix products, arithmetic and copies ran while one was open for 4% of the time, Pallas kernels for 0%

profile of v1, /device:TPU:0, one launch (start us, length us, event | category | flops | bytes accessed | tf_op | source)
XLA Modules:
  0.0 47.8 jit_solution(17374519208207554960)
XLA Ops:
  0.6 0.0 copy-start
  0.6 0.0 copy-start.2
  0.7 0.0 copy-start.1
  0.7 0.8 %pad_maximum_fusion.8 = f32[52,128]{1,0:T(8,128)S(1)} fusion(f32[32,128]{1,0:T(8,128)} %param.11, f32[20,128]{1,0:T(8,128)} %param.7), kind=kLoop, calls=%fused_computation.37 | loop fusion | flops 6656 | bytes 53248 | tf_op jit(solution)/shard_map/concatenate | solution.py:50
  1.4 0.5 collective-permute-start
  1.9 1.2 %dynamic_slice.3 = s32[1]{0:T(128)} dynamic-slice(s32[4]{0:T(128)} %param.13, s32[]{:T(128)S(6)} %select_n.23), dynamic_slice_sizes={1} | dynamic-slice | bytes 12 | tf_op jit(solution)/shard_map/dynamic_slice | solution.py:43
  3.8 0.0 collective-permute-done
  3.8 0.7 %broadcast_select_fusion = f32[52,128]{1,0:T(8,128)S(1)} fusion(f32[52,128]{1,0:T(8,128)S(1)} %collective-permute-done, pred[]{:T(512)S(6)} %eq.11, f32[32,128]{1,0:T(8,128)} %param.11, f32[20,128]{1,0:T(8,128)} %param.7), kind=kLoop, calls=%fused_computation.38 | loop fusion | flops 13312 | bytes 79873 | tf_op jit(solution)/shard_map/jit(_where)/select_n | solution.py:48
  4.5 2.5 %collective-permute-start.1 = (f32[52,128]{1,0:T(8,128)S(1)}, f32[52,128]{1,0:T(8,128)S(1)}, u32[]{:S(2)}, u32[]{:S(2)}) collective-permute-start(f32[52,128]{1,0:T(8,128)S(1)} %broadcast_select_fusion), channel_id=1, source_target_pairs={{0,2},{1,3},{2,0},{3,1},{4,6},{5,7},{6,4},{7,5},{8,10},{9,11},{10,... | collective-permute-start | bytes 79880 | tf_op jit(solution)/shard_map/ppermute | solution.py:10
  7.0 2.0 %collective-permute-done.1 = f32[52,128]{1,0:T(8,128)S(1)} collective-permute-done((f32[52,128]{1,0:T(8,128)S(1)}, f32[52,128]{1,0:T(8,128)S(1)}, u32[]{:S(2)}, u32[]{:S(2)}) %collective-permute-start.1) | collective-permute-done | bytes 26656 | tf_op jit(solution)/shard_map/ppermute | solution.py:10
  9.0 0.7 %pad_maximum_fusion.7 = f32[104,128]{1,0:T(8,128)S(1)} fusion(f32[32,128]{1,0:T(8,128)} %param.12, f32[20,128]{1,0:T(8,128)} %param.7, f32[52,128]{1,0:T(8,128)S(1)} %broadcast_select_fusion.1), kind=kLoop, calls=%fused_computation.32 | loop fusion | flops 26624 | bytes 106496 | tf_op jit(solution)/shard_map/concatenate | solution.py:55
  9.7 2.0 %collective-permute-start.2 = (f32[104,128]{1,0:T(8,128)S(1)}, f32[104,128]{1,0:T(8,128)S(1)}, u32[]{:S(2)}, u32[]{:S(2)}) collective-permute-start(f32[104,128]{1,0:T(8,128)S(1)} %pad_maximum_fusion.7), channel_id=1, source_target_pairs={{0,4},{1,5},{2,6},{3,7},{4,0},{5,1},{6,2},{7,3},{8,12},{9,13},{10,... | collective-permute-start | bytes 159752 | tf_op jit(solution)/shard_map/ppermute | solution.py:10
  11.7 2.2 %collective-permute-done.2 = f32[104,128]{1,0:T(8,128)S(1)} collective-permute-done((f32[104,128]{1,0:T(8,128)S(1)}, f32[104,128]{1,0:T(8,128)S(1)}, u32[]{:S(2)}, u32[]{:S(2)}) %collective-permute-start.2) | collective-permute-done | bytes 53280 | tf_op jit(solution)/shard_map/ppermute | solution.py:10
  13.9 0.7 %maximum_bitcast_fusion = f32[1,156,128]{2,1,0:T(8,128)S(1)} fusion(f32[52,128]{1,0:T(8,128)S(1)} %get-tuple-element.13, f32[32,128]{1,0:T(8,128)} %param.12, f32[20,128]{1,0:T(8,128)} %param.7, f32[52,128]{1,0:T(8,128)S(1)} %get-tuple-element.12), kind=kLoop, calls=%fused_computation.21 | loop fusion | flops 59904 | bytes 159744 | tf_op jit(solution)/shard_map/broadcast_in_dim | solution.py:57
  14.7 3.1 %collective-permute-start.3 = (f32[1,156,128]{2,1,0:T(8,128)S(1)}, f32[1,156,128]{2,1,0:T(8,128)S(1)}, u32[]{:S(2)}, u32[]{:S(2)}) collective-permute-start(f32[1,156,128]{2,1,0:T(8,128)S(1)} %maximum_bitcast_fusion), channel_id=1, source_target_pairs={{0,16},{8,24},{16,0},{24,8},{1,17},{9,25},{17,1},{25,9},{2,18},{10... | collective-permute-start | bytes 239624 | tf_op jit(solution)/shard_map/ppermute | solution.py:10
  17.7 2.4 %collective-permute-done.3 = f32[1,156,128]{2,1,0:T(8,128)S(1)} collective-permute-done((f32[1,156,128]{2,1,0:T(8,128)S(1)}, f32[1,156,128]{2,1,0:T(8,128)S(1)}, u32[]{:S(2)}, u32[]{:S(2)}) %collective-permute-start.3) | collective-permute-done | bytes 79904 | tf_op jit(solution)/shard_map/ppermute | solution.py:10
  20.2 2.0 %collective-permute-start.4 = (f32[2,156,128]{2,1,0:T(8,128)S(1)}, f32[2,156,128]{2,1,0:T(8,128)S(1)}, u32[]{:S(2)}, u32[]{:S(2)}) collective-permute-start(f32[2,156,128]{2,1,0:T(8,128)S(1)} %pad_maximum_fusion.3), channel_id=1, source_target_pairs={{0,8},{8,0},{16,24},{24,16},{1,9},{9,1},{17,25},{25,17},{2,10},{10... | collective-permute-start | bytes 479240 | tf_op jit(solution)/shard_map/ppermute | solution.py:10
  22.1 3.4 %collective-permute-done.4 = f32[2,156,128]{2,1,0:T(8,128)S(1)} collective-permute-done((f32[2,156,128]{2,1,0:T(8,128)S(1)}, f32[2,156,128]{2,1,0:T(8,128)S(1)}, u32[]{:S(2)}, u32[]{:S(2)}) %collective-permute-start.4) | collective-permute-done | bytes 159776 | tf_op jit(solution)/shard_map/ppermute | solution.py:10
  25.8 0.0 copy-done.2
  25.8 0.0 copy-done.1
  25.8 1.4 %fusion = f32[1536,256]{1,0:T(8,128)S(1)} fusion(f32[20,1536]{1,0:T(8,128)S(1)} %constant_dynamic-update-slice_fusion, f32[20,256]{1,0:T(8,128)S(1)} %copy-done.1, f32[256]{0:T(256)S(1)} %copy-done.2), kind=kOutput, calls=%fused_computation.2 | convolution fusion | flops 94765056 | bytes 1717248 | tf_op jit(solution)/shard_map/ph,pn->hn/dot_general | solution.py:18
  27.2 0.0 copy-done
  27.3 1.6 %convolution_bitcast_fusion = f32[64,1536]{1,0:T(8,128)S(1)} fusion(f32[1536,256]{1,0:T(8,128)S(1)} %fusion, f32[256,64]{0,1:T(8,128)S(1)} %copy-done), kind=kOutput, calls=%fused_computation.3 | convolution fusion | flops 301989888 | bytes 2031616 | tf_op jit(solution)/shard_map/hf,hn->fn/dot_general | solution.py:24
  29.0 1.8 %fusion.4 = f32[512,1024]{1,0:T(8,128)S(1)} fusion(f32[32,512]{1,0:T(8,128)S(1)} %get-tuple-element.17, f32[32,512]{1,0:T(8,128)S(1)} %get-tuple-element.18, f32[4,4,8,128]{3,2,1,0:T(8,128)S(1)} %get-tuple-element.9), kind=kOutput, calls=%fused_computation.13 | convolution fusion | flops 201359360 | bytes 2293760 | tf_op jit(solution)/shard_map/qi,qj->ij/dot_general | solution.py:31
  30.9 2.5 %fusion.16 = (f32[512]{0:T(512)S(1)}, f32[1024]{0:T(1024)S(1)}, f32[512,1024]{1,0:T(8,128)S(1)}) fusion(f32[512,1024]{1,0:T(8,128)S(1)} %fusion.4, f32[64,1536]{1,0:T(8,128)S(1)} %convolution_bitcast_fusion, f32[1024]{0:T(1024)S(1)} %multiply_reduce_fusion, f32[512]{0:T(512)S(1)} %multiply_reduce_fusion.1), kind=kOutput, calls=%fused_computation.46 | convolution fusion | flops 406321664 | bytes 4599808 | tf_op jit(solution)/shard_map/fi,fj->ij/dot_general | solution.py:29
  33.3 2.1 %convolution_subtract_fusion.1 = f32[64,512]{1,0:T(8,128)S(1)} fusion(f32[512,1024]{1,0:T(8,128)S(1)} %get-tuple-element.14, f32[64,1536]{1,0:T(8,128)S(1)} %convolution_bitcast_fusion, f32[512]{0:T(512)S(1)} %get-tuple-element.4), kind=kOutput, calls=%fused_computation.6 | convolution fusion | flops 402718720 | bytes 2623488 | tf_op jit(solution)/shard_map/fj,ij->fi/dot_general | solution.py:32
  35.5 1.4 %convolution_subtract_fusion = f32[64,1024]{1,0:T(8,128)S(1)} fusion(f32[512,1024]{1,0:T(8,128)S(1)} %get-tuple-element.14, f32[64,1536]{1,0:T(8,128)S(1)} %convolution_bitcast_fusion, f32[1024]{0:T(1024)S(1)} %get-tuple-element.5), kind=kOutput, calls=%fused_computation.5 | convolution fusion | flops 402784256 | bytes 2756608 | tf_op jit(solution)/shard_map/fi,ij->fj/dot_general | solution.py:33
  36.8 0.9 %fusion.1 = f32[64,256]{1,0:T(8,128)S(1)} fusion(f32[1536,256]{1,0:T(8,128)S(1)} %fusion, f32[64,1024]{1,0:T(8,128)S(1)} %convolution_subtract_fusion, f32[64,512]{1,0:T(8,128)S(1)} %convolution_subtract_fusion.1), kind=kOutput, calls=%fused_computation.8 | convolution fusion | flops 302088192 | bytes 2031616 | tf_op jit(solution)/shard_map/hn,fn->fh/dot_general | solution.py:35
  37.8 1.5 %fusion.17 = (f32[256]{0:T(256)S(1)}, f32[1536,256]{1,0:T(8,128)S(1)}) fusion(f32[1536,256]{1,0:T(8,128)S(1)} %fusion, f32[256,64]{0,1:T(8,128)S(1)} %copy-done, f32[64,1024]{1,0:T(8,128)S(1)} %convolution_subtract_fusion, f32[64,512]{1,0:T(8,128)S(1)} %convolution_subtract_fusion.1), kind=kOutput, calls=%fused_computation.47 | convolution fusion | flops 303660800 | bytes 3605504 | tf_op jit(solution)/shard_map/hf,fn->hn/dot_general | solution.py:36
  39.3 0.7 %fusion.18 = f32[20,256]{1,0:T(8,128)S(1)} fusion(f32[20,1536]{1,0:T(8,128)S(1)} %constant_dynamic-update-slice_fusion, f32[1536,256]{1,0:T(8,128)S(1)} %get-tuple-element.16), kind=kOutput, calls=%fused_computation.48 | convolution fusion | flops 94371840 | bytes 1716224 | tf_op jit(solution)/shard_map/pn,hn->ph/dot_general | solution.py:37
  40.0 1.9 %collective-permute-start.5 = (f32[85,256]{1,0:T(8,128)S(1)}, f32[85,256]{1,0:T(8,128)S(1)}, u32[]{:S(2)}, u32[]{:S(2)}) collective-permute-start(f32[85,256]{1,0:T(8,128)S(1)} %pad_maximum_fusion.4), channel_id=1, source_target_pairs={{0,2},{1,3},{2,0},{3,1},{4,6},{5,7},{6,4},{7,5},{8,10},{9,11},{10,... | collective-permute-start | bytes 261128 | tf_op jit(solution)/shard_map/ppermute | solution.py:10
  41.9 2.7 %collective-permute-done.5 = f32[85,256]{1,0:T(8,128)S(1)} collective-permute-done((f32[85,256]{1,0:T(8,128)S(1)}, f32[85,256]{1,0:T(8,128)S(1)}, u32[]{:S(2)}, u32[]{:S(2)}) %collective-permute-start.5) | collective-permute-done | bytes 87072 | tf_op jit(solution)/shard_map/ppermute | solution.py:10
  44.6 0.1 collective-permute-start.6
  44.7 0.6 %slice.60 = f32[64,128]{1,0:T(8,128)} slice(f32[64,1024]{1,0:T(8,128)S(1)} %convolution_subtract_fusion), slice={[0:64], [0:128]} | slice | bytes 65536 | tf_op jit(solution)/shard_map/slice | solution.py:73
  45.3 0.7 %collective-permute-done.6 = f32[85,256]{1,0:T(8,128)S(1)} collective-permute-done((f32[85,256]{1,0:T(8,128)S(1)}, f32[85,256]{1,0:T(8,128)S(1)}, u32[]{:S(2)}, u32[]{:S(2)}) %collective-permute-start.6) | collective-permute-done | bytes 87072 | tf_op jit(solution)/shard_map/ppermute | solution.py:10
  46.0 0.6 %slice.62 = f32[1,256]{1,0:T(1,128)} slice(f32[85,256]{1,0:T(8,128)S(1)} %add.38), slice={[84:85], [0:256]} | slice | bytes 2048 | tf_op jit(solution)/shard_map/slice | solution.py:73
  46.6 0.6 %slice.61 = f32[20,256]{1,0:T(8,128)} slice(f32[85,256]{1,0:T(8,128)S(1)} %add.38), slice={[64:84], [0:256]} | slice | bytes 40960 | tf_op jit(solution)/shard_map/slice | solution.py:73
  47.2 0.6 %slice_bitcast_fusion = f32[256,64]{0,1:T(8,128)} fusion(f32[85,256]{1,0:T(8,128)S(1)} %add.38), kind=kLoop, calls=%fused_computation.26 | loop fusion | bytes 131072 | tf_op jit(solution)/shard_map/transpose | solution.py:73
  (23 shorter events, 0.3 us)
Async XLA Ops:
  0.6 26.6 %copy-start = (f32[256,64]{0,1:T(8,128)S(1)}, f32[256,64]{0,1:T(8,128)}, u32[]{:S(2)}) copy-start(f32[256,64]{0,1:T(8,128)} %param.10) | copy-start | bytes 196612
  0.6 25.1 %copy-start.2 = (f32[256]{0:T(256)S(1)}, f32[256]{0:T(256)}, u32[]{:S(2)}) copy-start(f32[256]{0:T(256)} %param.9) | copy-start | bytes 3076
  0.7 25.1 %copy-start.1 = (f32[20,256]{1,0:T(8,128)S(1)}, f32[20,256]{1,0:T(8,128)}, u32[]{:S(2)}) copy-start(f32[20,256]{1,0:T(8,128)} %param.8) | copy-start | bytes 61444
  1.4 2.3 %collective-permute-start = (f32[52,128]{1,0:T(8,128)S(1)}, f32[52,128]{1,0:T(8,128)S(1)}, u32[]{:S(2)}, u32[]{:S(2)}) collective-permute-start(f32[52,128]{1,0:T(8,128)S(1)} %pad_maximum_fusion.8), channel_id=1, source_target_pairs={{0,1},{1,0},{2,3},{3,2},{4,5},{5,4},{6,7},{7,6},{8,9},{9,8},{10,11... | collective-permute-start | bytes 79880 | tf_op jit(solution)/shard_map/ppermute | solution.py:10
  4.5 4.5 %collective-permute-start.1 = (f32[52,128]{1,0:T(8,128)S(1)}, f32[52,128]{1,0:T(8,128)S(1)}, u32[]{:S(2)}, u32[]{:S(2)}) collective-permute-start(f32[52,128]{1,0:T(8,128)S(1)} %broadcast_select_fusion), channel_id=1, source_target_pairs={{0,2},{1,3},{2,0},{3,1},{4,6},{5,7},{6,4},{7,5},{8,10},{9,11},{10,... | collective-permute-start | bytes 79880 | tf_op jit(solution)/shard_map/ppermute | solution.py:10
  9.7 4.2 %collective-permute-start.2 = (f32[104,128]{1,0:T(8,128)S(1)}, f32[104,128]{1,0:T(8,128)S(1)}, u32[]{:S(2)}, u32[]{:S(2)}) collective-permute-start(f32[104,128]{1,0:T(8,128)S(1)} %pad_maximum_fusion.7), channel_id=1, source_target_pairs={{0,4},{1,5},{2,6},{3,7},{4,0},{5,1},{6,2},{7,3},{8,12},{9,13},{10,... | collective-permute-start | bytes 159752 | tf_op jit(solution)/shard_map/ppermute | solution.py:10
  14.7 5.5 %collective-permute-start.3 = (f32[1,156,128]{2,1,0:T(8,128)S(1)}, f32[1,156,128]{2,1,0:T(8,128)S(1)}, u32[]{:S(2)}, u32[]{:S(2)}) collective-permute-start(f32[1,156,128]{2,1,0:T(8,128)S(1)} %maximum_bitcast_fusion), channel_id=1, source_target_pairs={{0,16},{8,24},{16,0},{24,8},{1,17},{9,25},{17,1},{25,9},{2,18},{10... | collective-permute-start | bytes 239624 | tf_op jit(solution)/shard_map/ppermute | solution.py:10
  20.2 5.4 %collective-permute-start.4 = (f32[2,156,128]{2,1,0:T(8,128)S(1)}, f32[2,156,128]{2,1,0:T(8,128)S(1)}, u32[]{:S(2)}, u32[]{:S(2)}) collective-permute-start(f32[2,156,128]{2,1,0:T(8,128)S(1)} %pad_maximum_fusion.3), channel_id=1, source_target_pairs={{0,8},{8,0},{16,24},{24,16},{1,9},{9,1},{17,25},{25,17},{2,10},{10... | collective-permute-start | bytes 479240 | tf_op jit(solution)/shard_map/ppermute | solution.py:10
  40.0 4.6 %collective-permute-start.5 = (f32[85,256]{1,0:T(8,128)S(1)}, f32[85,256]{1,0:T(8,128)S(1)}, u32[]{:S(2)}, u32[]{:S(2)}) collective-permute-start(f32[85,256]{1,0:T(8,128)S(1)} %pad_maximum_fusion.4), channel_id=1, source_target_pairs={{0,2},{1,3},{2,0},{3,1},{4,6},{5,7},{6,4},{7,5},{8,10},{9,11},{10,... | collective-permute-start | bytes 261128 | tf_op jit(solution)/shard_map/ppermute | solution.py:10
  44.6 1.4 %collective-permute-start.6 = (f32[85,256]{1,0:T(8,128)S(1)}, f32[85,256]{1,0:T(8,128)S(1)}, u32[]{:S(2)}, u32[]{:S(2)}) collective-permute-start(f32[85,256]{1,0:T(8,128)S(1)} %fusion.29), channel_id=1, source_target_pairs={{0,1},{1,0},{2,3},{3,2},{4,5},{5,4},{6,7},{7,6},{8,9},{9,8},{10,11... | collective-permute-start | bytes 261128 | tf_op jit(solution)/shard_map/ppermute | solution.py:10

commit v2 on v1

v2 whole, which is shorter than its diff:
```python
import functools

import jax
import jax.numpy as jnp
from jax import lax
from jax.experimental import pallas as pl
from jax.experimental.pallas import tpu as pltpu
from jax.sharding import PartitionSpec as P

BF, F32 = jnp.bfloat16, jnp.float32
VMEM = pltpu.VMEM


def swap(value, axis, size, bit):
    return lax.ppermute(value, axis, [(i, i ^ bit) for i in range(size)])


def bits_of(size):
    return [1 << k for k in range(size.bit_length() - 1)]


def split(value, terms=2):
    parts = []
    for _ in range(terms):
        part = value.astype(BF).astype(F32)
        parts.append(part)
        value = value - part
    return parts


def stack(parts):
    return jnp.concatenate(parts, 0).astype(BF)


def mm(a, b):
    return lax.dot_general(a, b, (((1,), (0,)), ((), ())), preferred_element_type=F32)


def mm_nt(a, b):
    return lax.dot_general(a, b, (((1,), (1,)), ((), ())), preferred_element_type=F32)


def mm_tn(a, b):
    return lax.dot_general(a, b, (((0,), (0,)), ((), ())), preferred_element_type=F32)


def each(count, step):
    if count <= 8:
        for i in range(count):
            step(i)
    else:
        lax.fori_loop(0, count, lambda i, c: (step(i), c)[1], 0)


def up(value, to):
    return -(-value // to) * to


class Sizes:
    def __init__(self, depth, vecs, hid, feats, own, n_row):
        self.depth, self.vecs, self.hid, self.feats, self.own, self.n_row = depth, vecs, hid, feats, own, n_row
        self.ins = up(depth + 1, 8)
        self.part = self.ins + vecs
        self.wide = n_row * own
        self.total = 3 * self.wide


def prepare_kernel(z, blocks_ref, protocols_ref, solved_ref, probes_ref, window_ref, columns_ref, apart_ref):
    ones = jnp.where(lax.broadcasted_iota(jnp.int32, (z.ins - z.depth, z.own), 0) == 0, 1.0, 0.0)
    inputs = jnp.concatenate([protocols_ref[...], ones], 0)
    window_ref[: z.ins] = inputs
    window_ref[z.ins :] = solved_ref[...]
    columns_ref[: z.ins] = inputs
    columns_ref[z.ins :] = probes_ref[...]
    apart = blocks_ref[lax.axis_index("row")] ^ lax.axis_index("col")
    apart_ref[...] = jnp.full(apart_ref.shape, apart, jnp.int32)


def compute_kernel(
    z, blocks_ref, w_in_ref, b_in_ref, w_out_ref, col_grad_ref, pack_ref,
    x_ref, vec_ref, h1_ref, h2_ref, hid_ref, feat_ref, wink_ref, colk_ref, winv_ref, colv_ref, winm_ref, colm_ref,
    half_ref, tot_ref,
):
    own, ins, hid, feats, vecs, wide = z.own, z.ins, z.hid, z.feats, z.vecs, z.wide
    chunk = 2 * own
    for r in range(z.n_row):
        for k in range(3):
            lanes = pl.ds(k * wide + r * own, own)
            x_ref[:, lanes] = blocks_ref[r, k * z.part : k * z.part + ins]
            vec_ref[:, lanes] = blocks_ref[r, k * z.part + ins : (k + 1) * z.part]
    w_all = jnp.concatenate(
        [w_in_ref[...], b_in_ref[...], jnp.zeros((ins - z.depth - 1, hid), F32)], 0
    )
    w1, w2, w3 = split(w_all, 3)
    w_stack = stack([w1, w1, w2, w2, w1, w3])
    o1, o2 = split(w_out_ref[...])
    out_m = jnp.concatenate([o1, o2], 1).astype(BF)
    out_k = jnp.concatenate([o1, o1, o2, o2], 1).astype(BF)
    ones = jnp.ones((16, chunk), F32)

    def forward(i):
        lanes = pl.ds(i * chunk, chunk)
        x1, x2, x3 = split(x_ref[:, lanes], 3)
        h = jnp.tanh(mm_tn(w_stack, stack([x1, x2, x1, x2, x3, x1])))
        hid_ref[:, lanes] = h
        h1 = h.astype(BF)
        h2 = (h - h1.astype(F32)).astype(BF)
        h1_ref[:, lanes], h2_ref[:, lanes] = h1, h2
        raw = mm_tn(out_m, h1) + mm_tn(out_m, h2)
        feat_ref[:, lanes] = raw[:feats] + raw[feats:]

    each(z.total // chunk, forward)

    def window(i):
        lanes = pl.ds(i * chunk, chunk)
        f1, f2 = split(feat_ref[:, lanes])
        wink_ref[lanes, :] = stack([f1, f2, f1, f2]).T
        winm_ref[:, lanes] = stack([f1, f2, ones])
        s1, s2 = split(vec_ref[:, lanes])
        winv_ref[lanes, :] = stack([s1, s2, s1, s2]).T
        exact = f1 + f2
        half_ref[lanes, :] = mm_tn(stack(split(exact * exact, 3)), jnp.full((3 * feats, own), 0.5, BF))
        tot_ref[:, lanes] = jnp.zeros((tot_ref.shape[0], chunk), F32)

    each(wide // chunk, window)

    def columns(i):
        lanes = pl.ds(wide + i * chunk, chunk)
        f1, f2 = split(feat_ref[:, lanes])
        p1, p2 = split(vec_ref[:, lanes])
        exact = f1 + f2
        half = 0.5 * jnp.sum(exact * exact, 0, keepdims=True)
        f_stack, p_stack = stack([f1, f1, f2, f2]), stack([p1, p1, p2, p2])
        m_stack = stack([f1, f2, ones])

        def against(k, raw):
            rows = pl.ds(k * wide_step, wide_step)
            norm = half_ref[rows, :]
            norm = jnp.concatenate([norm] * (chunk // own), 1)
            kern = jnp.exp(mm(wink_ref[rows, :], f_stack) - norm - half)
            weigh = kern * mm(winv_ref[rows, :], p_stack)
            g1 = weigh.astype(BF)
            g2 = (weigh - g1.astype(F32)).astype(BF)
            m = winm_ref[:, rows]
            tot_ref[:, rows] += mm_nt(m_stack, g1) + mm_nt(m_stack, g2)
            return raw + mm(m, g1) + mm(m, g2)

        wide_step = min(wide, 512)
        raw = jnp.zeros((2 * feats + 16, chunk), F32)
        if wide == wide_step:
            raw = against(0, raw)
        else:
            raw = lax.fori_loop(0, wide // wide_step, against, raw)
        feat_ref[:, lanes] = raw[:feats] + raw[feats : 2 * feats] - exact * raw[2 * feats : 2 * feats + 1]

    each(2 * wide // chunk, columns)
    col_grad_ref[...] = feat_ref[:, wide : wide + own]

    def window_grad(i):
        lanes = pl.ds(i * chunk, chunk)
        f1, f2 = split(feat_ref[:, lanes])
        raw = tot_ref[:, lanes]
        feat_ref[:, lanes] = raw[:feats] + raw[feats : 2 * feats] - (f1 + f2) * raw[2 * feats : 2 * feats + 1]

    each(wide // chunk, window_grad)

    pack_ref[...] = jnp.zeros(pack_ref.shape, F32)

    def backward(i):
        lanes = pl.ds(i * chunk, chunk)
        t1, t2 = split(feat_ref[:, lanes])
        h = hid_ref[:, lanes]
        g = mm(out_k, stack([t1, t2, t1, t2])) * (1.0 - h * h)
        t_stack = stack([t1, t2])
        raw = mm_nt(t_stack, h1_ref[:, lanes]) + mm_nt(t_stack, h2_ref[:, lanes])
        pack_ref[:feats] += raw[:feats] + raw[feats:]
        x1, x2 = split(x_ref[:, lanes])
        x_stack = stack([x1, x2])
        g1 = g.astype(BF)
        g2 = (g - g1.astype(F32)).astype(BF)
        raw = mm_nt(x_stack, g1) + mm_nt(x_stack, g2)
        pack_ref[feats:] += raw[:ins] + raw[ins:]

    each(z.total // chunk, backward)


def finish_kernel(z, mine_ref, theirs_ref, grad_in_ref, grad_bias_ref, grad_out_ref):
    both = mine_ref[...] + theirs_ref[...]
    grad_out_ref[...] = both[: z.feats].T
    grad_in_ref[...] = both[z.feats : z.feats + z.depth]
    grad_bias_ref[...] = both[z.feats + z.depth : z.feats + z.depth + 1]


def whole(count):
    return [pl.BlockSpec(memory_space=VMEM)] * count


def body(n_row, n_col, protocols, w_in, b_in, w_out, solved, probes, window_blocks):
    z = Sizes(protocols.shape[0], solved.shape[0], w_out.shape[0], w_out.shape[1], protocols.shape[1], n_row)
    bits = bits_of(n_col)
    shared, joined = bits[:-1], bits[-1]
    blk = jax.ShapeDtypeStruct((z.part, z.own), F32)
    window, columns, apart = pl.pallas_call(
        functools.partial(prepare_kernel, z),
        out_shape=(blk, blk, jax.ShapeDtypeStruct((8, z.own), jnp.int32)),
        in_specs=[pl.BlockSpec(memory_space=pltpu.SMEM)] + whole(3),
        out_specs=tuple(whole(3)),
        compiler_params=pltpu.CompilerParams(vmem_limit_bytes=2 << 20),
        name="prepare",
    )(window_blocks, protocols, solved, probes)

    def nearer(bit, mine, theirs):
        return jnp.where((apart[:1] & bit) == 0, mine, theirs)

    for bit in shared:
        window = nearer(bit, window, swap(window, "col", n_col, bit))
    got = swap(jnp.concatenate([window, columns]), "col", n_col, joined)
    window = nearer(joined, window, got[: z.part])
    blocks = jnp.concatenate([window, columns, got[z.part :]])[None]
    for bit in reversed(bits_of(n_row)):
        blocks = jnp.concatenate([blocks, swap(blocks, "row", n_row, bit)])

    feats, total, wide = z.feats, z.total, z.wide
    col_grad, pack = pl.pallas_call(
        functools.partial(compute_kernel, z),
        out_shape=(jax.ShapeDtypeStruct((feats, z.own), F32), jax.ShapeDtypeStruct((feats + z.ins, z.hid), F32)),
        in_specs=whole(4),
        out_specs=tuple(whole(2)),
        scratch_shapes=[
            VMEM((z.ins, total), F32),
            VMEM((z.vecs, total), F32),
            VMEM((z.hid, total), BF),
            VMEM((z.hid, total), BF),
            VMEM((z.hid, total), F32),
            VMEM((feats, total), F32),
            VMEM((wide, 4 * feats), BF),
            VMEM((8, 128), BF),
            VMEM((wide, 4 * z.vecs), BF),
            VMEM((8, 128), BF),
            VMEM((2 * feats + 16, wide), BF),
            VMEM((8, 128), BF),
            VMEM((wide, z.own), F32),
            VMEM((2 * feats + 16, wide), F32),
        ],
        compiler_params=pltpu.CompilerParams(vmem_limit_bytes=48 << 20),
        name="compute",
    )(blocks, w_in, b_in.reshape(1, -1), w_out)

    for bit in reversed(shared[1:]):
        pack = pack + swap(pack, "col", n_col, bit)
    grad_in, grad_bias, grad_out = pl.pallas_call(
        functools.partial(finish_kernel, z),
        out_shape=(
            jax.ShapeDtypeStruct((z.depth, z.hid), F32),
            jax.ShapeDtypeStruct((1, z.hid), F32),
            jax.ShapeDtypeStruct((z.hid, feats), F32),
        ),
        in_specs=whole(2),
        out_specs=tuple(whole(3)),
        compiler_params=pltpu.CompilerParams(vmem_limit_bytes=2 << 20),
        name="finish",
    )(pack, swap(pack, "col", n_col, shared[0]))
    return (col_grad, grad_in, grad_bias.reshape(-1), grad_out)


def solution(mesh):
    n_row, n_col = mesh.shape["row"], mesh.shape["col"]
    cut = P(None, ("row", "col"))

    def per_device(*args):
        return body(n_row, n_col, *args)

    return jax.shard_map(
        per_device,
        mesh=mesh,
        in_specs=(cut, P(), P(), P(), cut, cut, P()),
        out_specs=(cut, P(), P(), P()),
        check_vma=False,
    )
```

time: 48.5 us -> 38.3 us (0.79)
  matrix products: 14.1 us -> 0 us
  Pallas kernels: 0 us -> 5.46 us
  other arithmetic: 3.12 us -> 0.1 us
  waiting for transfers between devices: 13.3 us -> 14.6 us
  between operations: 1.53 us -> 0.72 us
  starting transfers between devices: 12 us -> 12.6 us
    dot_general x9 -> x0, matrix products: 14.1 us -> none  [the longest x1 2.45 us: weight_grads(): cross = jnp.einsum('fi,fj->ij', first, second, precision=HIGHEST)]
    pallas_call x0 -> x3, Pallas kernels: none -> 5.46 us  [the longest x1 4.28 us: body(): pl.pallas_call(functools.partial(compute_kernel, z), out_shape=(jax.Shape...]
    unnamed x14 -> x16, local copies, waits for them, and re-layouts: 0.08 us -> 4.27 us
    slice x3 -> x0, local copies, waits for them, and re-layouts: 1.79 us -> none  [the longest x1 0.62 us: body(): col_grad[:, :own]]
    ppermute x7, waiting for transfers between devices: 13.3 us -> 14.6 us  [swap(): return lax.ppermute(value, axis, [(i, i ^ bit) for i in range(size)])]
    dynamic_slice x1 -> x0, local copies, waits for them, and re-layouts: 1.24 us -> none  [body(): apart = lax.axis_index('col') ^ window_blocks[lax.axis_index('row')]]
    concatenate x2 -> x0, other arithmetic: 0.77 us -> none  [the longest x1 0.76 us: body(): window = jnp.concatenate([protocols, solved])]
    select_n x3, other arithmetic: 0.75 us -> 0.02 us  [nearer(): return jnp.where(apart[:1] & bit == 0, mine, theirs)]
  transfers between devices with their start and end apart: 7 -> 7, of which waited for: 6 -> 7; matrix products, arithmetic and copies ran while one was open for 4% -> 0% of each run, Pallas kernels for 0% -> 0%
where the time goes in v2:
time: 38.3 us; the launch traced here: 37.8 us
  waiting for transfers between devices  14.6 us (38%)
  starting transfers between devices  12.6 us (33%)
  Pallas kernels  5.46 us (14%)
  local copies, waits for them, and re-layouts  4.27 us (11%)
  between operations  0.72 us (2%)
    ppermute x7, waiting for transfers between devices, swap(): return lax.ppermute(value, axis, [(i, i ^ bit) for i in range(size)])  14.6 us
    ppermute x7, starting transfers between devices, swap(): return lax.ppermute(value, axis, [(i, i ^ bit) for i in range(size)])  12.6 us
    pallas_call x1, Pallas kernels, body(): pl.pallas_call(functools.partial(compute_kernel, z), out_shape=(jax.Shape...  4.28 us
    unnamed x16, local copies, waits for them, and re-layouts  4.27 us
  transfers between devices with their start and end apart: 7, of which 7 were waited for; matrix products, arithmetic and copies ran while one was open for 0% of the time, Pallas kernels for 0%

profile of v2, /device:TPU:0, one launch (start us, length us, event | category | flops | bytes accessed | tf_op | source)
XLA Modules:
  0.0 37.8 jit_solution(17594047262340063513)
XLA Ops:
  0.6 0.0 copy-start.1
  0.6 0.7 %copy-done.1 = f32[32,128]{1,0:T(8,128)S(1)} copy-done((f32[32,128]{1,0:T(8,128)S(1)}, f32[32,128]{1,0:T(8,128)}, u32[]{:S(2)}) %copy-start.1) | copy-done | bytes 16408
  1.4 0.0 copy-start.2
  1.4 0.7 %copy-done.2 = f32[32,128]{1,0:T(8,128)S(1)} copy-done((f32[32,128]{1,0:T(8,128)S(1)}, f32[32,128]{1,0:T(8,128)}, u32[]{:S(2)}) %copy-start.2) | copy-done | bytes 16408
  2.1 0.0 copy-start.3
  2.1 0.7 %copy-done.3 = f32[20,128]{1,0:T(8,128)S(1)} copy-done((f32[20,128]{1,0:T(8,128)S(1)}, f32[20,128]{1,0:T(8,128)}, u32[]{:S(2)}) %copy-start.3) | copy-done | bytes 10264
  2.8 0.0 copy-start.5
  2.8 0.7 %copy-done.5 = s32[4]{0:T(128)S(1)} copy-done((s32[4]{0:T(128)S(1)}, s32[4]{0:T(128)}, u32[]{:S(2)}) %copy-start.5) | copy-done | bytes 40
  3.4 0.6 %prepare.1 = (f32[56,128]{1,0:T(8,128)S(1)}, f32[56,128]{1,0:T(8,128)S(1)}, s32[8,128]{1,0:T(8,128)S(1)}) custom-call(s32[4]{0:T(128)S(1)} %copy-done.5, f32[20,128]{1,0:T(8,128)S(1)} %copy-done.3, f32[32,128]{1,0:T(8,128)S(1)} %copy-done.1, f32[32,128]{1,0:T(8,128)S(1)} %copy-done.2), custom_call_target="tpu_custom_call" | custom-call | tf_op jit(solution)/shard_map/prepare/pallas_call | solution.py:203
  4.0 0.5 %collective-permute-start = (f32[56,128]{1,0:T(8,128)S(1)}, f32[56,128]{1,0:T(8,128)S(1)}, u32[]{:S(2)}, u32[]{:S(2)}) collective-permute-start(f32[56,128]{1,0:T(8,128)S(1)} %get-tuple-element.13), channel_id=1, source_target_pairs={{0,1},{1,0},{2,3},{3,2},{4,5},{5,4},{6,7},{7,6},{8,9},{9,8},{10,11... | collective-permute-start | bytes 86024 | tf_op jit(solution)/shard_map/ppermute | solution.py:15
  4.5 0.8 %collective-permute-done = f32[56,128]{1,0:T(8,128)S(1)} collective-permute-done((f32[56,128]{1,0:T(8,128)S(1)}, f32[56,128]{1,0:T(8,128)S(1)}, u32[]{:S(2)}, u32[]{:S(2)}) %collective-permute-start) | collective-permute-done | bytes 28704 | tf_op jit(solution)/shard_map/ppermute | solution.py:15
  5.4 2.8 %collective-permute-start.1 = (f32[56,128]{1,0:T(8,128)S(1)}, f32[56,128]{1,0:T(8,128)S(1)}, u32[]{:S(2)}, u32[]{:S(2)}) collective-permute-start(f32[56,128]{1,0:T(8,128)S(1)} %broadcast_select_fusion), channel_id=1, source_target_pairs={{0,2},{1,3},{2,0},{3,1},{4,6},{5,7},{6,4},{7,5},{8,10},{9,11},{10,... | collective-permute-start | bytes 86024 | tf_op jit(solution)/shard_map/ppermute | solution.py:15
  8.2 1.8 %collective-permute-done.1 = f32[56,128]{1,0:T(8,128)S(1)} collective-permute-done((f32[56,128]{1,0:T(8,128)S(1)}, f32[56,128]{1,0:T(8,128)S(1)}, u32[]{:S(2)}, u32[]{:S(2)}) %collective-permute-start.1) | collective-permute-done | bytes 28704 | tf_op jit(solution)/shard_map/ppermute | solution.py:15
  10.1 2.1 %collective-permute-start.2 = (f32[112,128]{1,0:T(8,128)S(1)}, f32[112,128]{1,0:T(8,128)S(1)}, u32[]{:S(2)}, u32[]{:S(2)}) collective-permute-start(f32[112,128]{1,0:T(8,128)S(1)} %pad_maximum_fusion.2), channel_id=1, source_target_pairs={{0,4},{1,5},{2,6},{3,7},{4,0},{5,1},{6,2},{7,3},{8,12},{9,13},{10,... | collective-permute-start | bytes 172040 | tf_op jit(solution)/shard_map/ppermute | solution.py:15
  12.2 2.2 %collective-permute-done.2 = f32[112,128]{1,0:T(8,128)S(1)} collective-permute-done((f32[112,128]{1,0:T(8,128)S(1)}, f32[112,128]{1,0:T(8,128)S(1)}, u32[]{:S(2)}, u32[]{:S(2)}) %collective-permute-start.2) | collective-permute-done | bytes 57376 | tf_op jit(solution)/shard_map/ppermute | solution.py:15
  14.4 0.0 copy-start.6
  14.4 3.2 %collective-permute-start.3 = (f32[1,168,128]{2,1,0:T(8,128)S(1)}, f32[1,168,128]{2,1,0:T(8,128)S(1)}, u32[]{:S(2)}, u32[]{:S(2)}) collective-permute-start(f32[1,168,128]{2,1,0:T(8,128)S(1)} %maximum_bitcast_fusion), channel_id=1, source_target_pairs={{0,16},{8,24},{16,0},{24,8},{1,17},{9,25},{17,1},{25,9},{2,18},{10... | collective-permute-start | bytes 258056 | tf_op jit(solution)/shard_map/ppermute | solution.py:15
  17.5 2.5 %collective-permute-done.3 = f32[1,168,128]{2,1,0:T(8,128)S(1)} collective-permute-done((f32[1,168,128]{2,1,0:T(8,128)S(1)}, f32[1,168,128]{2,1,0:T(8,128)S(1)}, u32[]{:S(2)}, u32[]{:S(2)}) %collective-permute-start.3) | collective-permute-done | bytes 86048 | tf_op jit(solution)/shard_map/ppermute | solution.py:15
  20.0 2.0 %collective-permute-start.4 = (f32[2,168,128]{2,1,0:T(8,128)S(1)}, f32[2,168,128]{2,1,0:T(8,128)S(1)}, u32[]{:S(2)}, u32[]{:S(2)}) collective-permute-start(f32[2,168,128]{2,1,0:T(8,128)S(1)} %pad_maximum_fusion.1), channel_id=1, source_target_pairs={{0,8},{8,0},{16,24},{24,16},{1,9},{9,1},{17,25},{25,17},{2,10},{10... | collective-permute-start | bytes 516104 | tf_op jit(solution)/shard_map/ppermute | solution.py:15
  22.0 0.0 copy-done.6
  22.0 0.1 copy.11.w_out_ref
  22.1 0.0 copy-start
  22.1 3.4 %collective-permute-done.4 = f32[2,168,128]{2,1,0:T(8,128)S(1)} collective-permute-done((f32[2,168,128]{2,1,0:T(8,128)S(1)}, f32[2,168,128]{2,1,0:T(8,128)S(1)}, u32[]{:S(2)}, u32[]{:S(2)}) %collective-permute-start.4) | collective-permute-done | bytes 172064 | tf_op jit(solution)/shard_map/ppermute | solution.py:15
  25.5 0.0 copy-start.4
  25.5 0.0 copy-done
  25.6 0.7 %copy-done.4 = f32[256]{0:T(256)S(1)} copy-done((f32[256]{0:T(256)S(1)}, f32[256]{0:T(256)}, u32[]{:S(2)}) %copy-start.4) | copy-done | bytes 1048
  26.2 4.3 %compute.1 = (f32[64,128]{1,0:T(8,128)}, f32[88,256]{1,0:T(8,128)S(1)}) custom-call(f32[4,168,128]{2,1,0:T(8,128)S(1)} %pad_maximum_fusion.blocks_ref, f32[20,256]{1,0:T(8,128)S(1)} %copy-done, f32[1,256]{1,0:T(1,128)S(1)} %bitcast.10, f32[256,64]{1,0:T(8,128)S(1)} %copy.11.w_out_ref), custom_call_target="tpu_custom_call" | custom-call | tf_op jit(solution)/shard_map/compute/pallas_call | solution.py:224
  30.5 1.9 %collective-permute-start.5 = (f32[88,256]{1,0:T(8,128)S(1)}, f32[88,256]{1,0:T(8,128)S(1)}, u32[]{:S(2)}, u32[]{:S(2)}) collective-permute-start(f32[88,256]{1,0:T(8,128)S(1)} %get-tuple-element.16), channel_id=1, source_target_pairs={{0,2},{1,3},{2,0},{3,1},{4,6},{5,7},{6,4},{7,5},{8,10},{9,11},{10,... | collective-permute-start | bytes 270344 | tf_op jit(solution)/shard_map/ppermute | solution.py:15
  32.4 2.7 %collective-permute-done.5 = f32[88,256]{1,0:T(8,128)S(1)} collective-permute-done((f32[88,256]{1,0:T(8,128)S(1)}, f32[88,256]{1,0:T(8,128)S(1)}, u32[]{:S(2)}, u32[]{:S(2)}) %collective-permute-start.5) | collective-permute-done | bytes 90144 | tf_op jit(solution)/shard_map/ppermute | solution.py:15
  35.1 0.1 collective-permute-start.6
  35.2 1.3 %collective-permute-done.6.theirs_ref = f32[88,256]{1,0:T(8,128)S(1)} collective-permute-done((f32[88,256]{1,0:T(8,128)S(1)}, f32[88,256]{1,0:T(8,128)S(1)}, u32[]{:S(2)}, u32[]{:S(2)}) %collective-permute-start.6) | collective-permute-done | bytes 90144 | tf_op jit(solution)/shard_map/ppermute | solution.py:15
  36.5 0.6 %finish.1 = (f32[20,256]{1,0:T(8,128)}, f32[1,256]{1,0:T(1,128)}, f32[256,64]{1,0:T(8,128)S(1)}) custom-call(f32[88,256]{1,0:T(8,128)S(1)} %add.3.mine_ref, f32[88,256]{1,0:T(8,128)S(1)} %collective-permute-done.6.theirs_ref), custom_call_target="tpu_custom_call" | custom-call | tf_op jit(solution)/shard_map/finish/pallas_call | solution.py:251
  37.1 0.7 %copy.12 = f32[256,64]{0,1:T(8,128)} copy(f32[256,64]{1,0:T(8,128)S(1)} %get-tuple-element.23) | data formatting | bytes 131072
  (9 shorter events, 0.1 us)
Async XLA Ops:
  0.6 0.7 %copy-start.1 = (f32[32,128]{1,0:T(8,128)S(1)}, f32[32,128]{1,0:T(8,128)}, u32[]{:S(2)}) copy-start(f32[32,128]{1,0:T(8,128)} %solved_ref.1) | copy-start | bytes 49156
  1.4 0.7 %copy-start.2 = (f32[32,128]{1,0:T(8,128)S(1)}, f32[32,128]{1,0:T(8,128)}, u32[]{:S(2)}) copy-start(f32[32,128]{1,0:T(8,128)} %probes_ref.1) | copy-start | bytes 49156
  2.1 0.7 %copy-start.3 = (f32[20,128]{1,0:T(8,128)S(1)}, f32[20,128]{1,0:T(8,128)}, u32[]{:S(2)}) copy-start(f32[20,128]{1,0:T(8,128)} %protocols_ref.1) | copy-start | bytes 30724
  2.8 0.7 %copy-start.5 = (s32[4]{0:T(128)S(1)}, s32[4]{0:T(128)}, u32[]{:S(2)}) copy-start(s32[4]{0:T(128)} %blocks_ref.1) | copy-start | bytes 52
  4.0 1.4 %collective-permute-start = (f32[56,128]{1,0:T(8,128)S(1)}, f32[56,128]{1,0:T(8,128)S(1)}, u32[]{:S(2)}, u32[]{:S(2)}) collective-permute-start(f32[56,128]{1,0:T(8,128)S(1)} %get-tuple-element.13), channel_id=1, source_target_pairs={{0,1},{1,0},{2,3},{3,2},{4,5},{5,4},{6,7},{7,6},{8,9},{9,8},{10,11... | collective-permute-start | bytes 86024 | tf_op jit(solution)/shard_map/ppermute | solution.py:15
  5.4 4.7 %collective-permute-start.1 = (f32[56,128]{1,0:T(8,128)S(1)}, f32[56,128]{1,0:T(8,128)S(1)}, u32[]{:S(2)}, u32[]{:S(2)}) collective-permute-start(f32[56,128]{1,0:T(8,128)S(1)} %broadcast_select_fusion), channel_id=1, source_target_pairs={{0,2},{1,3},{2,0},{3,1},{4,6},{5,7},{6,4},{7,5},{8,10},{9,11},{10,... | collective-permute-start | bytes 86024 | tf_op jit(solution)/shard_map/ppermute | solution.py:15
  10.1 4.3 %collective-permute-start.2 = (f32[112,128]{1,0:T(8,128)S(1)}, f32[112,128]{1,0:T(8,128)S(1)}, u32[]{:S(2)}, u32[]{:S(2)}) collective-permute-start(f32[112,128]{1,0:T(8,128)S(1)} %pad_maximum_fusion.2), channel_id=1, source_target_pairs={{0,4},{1,5},{2,6},{3,7},{4,0},{5,1},{6,2},{7,3},{8,12},{9,13},{10,... | collective-permute-start | bytes 172040 | tf_op jit(solution)/shard_map/ppermute | solution.py:15
  14.4 7.7 %copy-start.6 = (f32[256,64]{0,1:T(8,128)S(1)}, f32[256,64]{0,1:T(8,128)}, u32[]{:S(2)}) copy-start(f32[256,64]{0,1:T(8,128)} %param.10) | copy-start | bytes 196612
  14.4 5.6 %collective-permute-start.3 = (f32[1,168,128]{2,1,0:T(8,128)S(1)}, f32[1,168,128]{2,1,0:T(8,128)S(1)}, u32[]{:S(2)}, u32[]{:S(2)}) collective-permute-start(f32[1,168,128]{2,1,0:T(8,128)S(1)} %maximum_bitcast_fusion), channel_id=1, source_target_pairs={{0,16},{8,24},{16,0},{24,8},{1,17},{9,25},{17,1},{25,9},{2,18},{10... | collective-permute-start | bytes 258056 | tf_op jit(solution)/shard_map/ppermute | solution.py:15
  20.0 5.5 %collective-permute-start.4 = (f32[2,168,128]{2,1,0:T(8,128)S(1)}, f32[2,168,128]{2,1,0:T(8,128)S(1)}, u32[]{:S(2)}, u32[]{:S(2)}) collective-permute-start(f32[2,168,128]{2,1,0:T(8,128)S(1)} %pad_maximum_fusion.1), channel_id=1, source_target_pairs={{0,8},{8,0},{16,24},{24,16},{1,9},{9,1},{17,25},{25,17},{2,10},{10... | collective-permute-start | bytes 516104 | tf_op jit(solution)/shard_map/ppermute | solution.py:15
  22.1 3.4 %copy-start = (f32[20,256]{1,0:T(8,128)S(1)}, f32[20,256]{1,0:T(8,128)}, u32[]{:S(2)}) copy-start(f32[20,256]{1,0:T(8,128)} %w_in_ref.1) | copy-start | bytes 61444
  25.5 0.7 %copy-start.4 = (f32[256]{0:T(256)S(1)}, f32[256]{0:T(256)}, u32[]{:S(2)}) copy-start(f32[256]{0:T(256)} %param.9) | copy-start | bytes 3076
  30.5 4.6 %collective-permute-start.5 = (f32[88,256]{1,0:T(8,128)S(1)}, f32[88,256]{1,0:T(8,128)S(1)}, u32[]{:S(2)}, u32[]{:S(2)}) collective-permute-start(f32[88,256]{1,0:T(8,128)S(1)} %get-tuple-element.16), channel_id=1, source_target_pairs={{0,2},{1,3},{2,0},{3,1},{4,6},{5,7},{6,4},{7,5},{8,10},{9,11},{10,... | collective-permute-start | bytes 270344 | tf_op jit(solution)/shard_map/ppermute | solution.py:15
  35.1 1.4 %collective-permute-start.6 = (f32[88,256]{1,0:T(8,128)S(1)}, f32[88,256]{1,0:T(8,128)S(1)}, u32[]{:S(2)}, u32[]{:S(2)}) collective-permute-start(f32[88,256]{1,0:T(8,128)S(1)} %add.3.mine_ref), channel_id=1, source_target_pairs={{0,1},{1,0},{2,3},{3,2},{4,5},{5,4},{6,7},{7,6},{8,9},{9,8},{10,11... | collective-permute-start | bytes 270344 | tf_op jit(solution)/shard_map/ppermute | solution.py:15

commit v3 on v1

v3 whole, which is shorter than its diff:
```python
import functools

import jax
import jax.numpy as jnp
from jax import lax
from jax.experimental import pallas as pl
from jax.experimental.pallas import tpu as pltpu
from jax.sharding import PartitionSpec as P

BF, F32 = jnp.bfloat16, jnp.float32
VMEM = pltpu.VMEM


def swap(value, axis, size, bit):
    return lax.ppermute(value, axis, [(i, i ^ bit) for i in range(size)])


def bits_of(size):
    return [1 << k for k in range(size.bit_length() - 1)]


def split(value, terms=2):
    parts = []
    for _ in range(terms):
        part = value.astype(BF).astype(F32)
        parts.append(part)
        value = value - part
    return parts


def stack(parts):
    return jnp.concatenate(parts, 0).astype(BF)


def mm(a, b):
    return lax.dot_general(a, b, (((1,), (0,)), ((), ())), preferred_element_type=F32)


def mm_nt(a, b):
    return lax.dot_general(a, b, (((1,), (1,)), ((), ())), preferred_element_type=F32)


def mm_tn(a, b):
    return lax.dot_general(a, b, (((0,), (0,)), ((), ())), preferred_element_type=F32)


def each(count, step):
    if count <= 4:
        for i in range(count):
            step(i)
    else:
        lax.fori_loop(0, count, lambda i, c: (step(i), c)[1], 0)


def up(value, to):
    return -(-value // to) * to


class Sizes:
    def __init__(self, depth, vecs, hid, feats, own, n_row):
        self.depth, self.vecs, self.hid, self.feats, self.own = depth, vecs, hid, feats, own
        self.ins = up(depth + 1, 8)
        self.part = self.ins + vecs
        self.groups = n_row // 2
        self.wide = self.groups * own
        self.chunk = min(2 * own, self.wide)
        self.rows = 2 * feats + 16

    def half(self):
        w = self.wide
        return dict(
            x=((self.ins, 3 * w), F32),
            h1=((self.hid, 3 * w), BF),
            h2=((self.hid, 3 * w), BF),
            m=((self.rows, 3 * w), BF),
            vec=((4 * self.vecs, 2 * w), BF),
            norm=((8, 2 * w), F32),
            wink=((w, 4 * self.feats), BF),
            winv=((w, 4 * self.vecs), BF),
            winn=((w, self.own), F32),
        )

    def sums(self):
        return dict(raw=((self.rows, 2 * self.wide), F32), tot=((self.rows, self.wide), F32))


class Refs:
    def __init__(self, names, refs):
        self.__dict__.update(zip(names, refs, strict=True))


def prepare_kernel(z, blocks_hbm, in_hbm, vec_hbm, probes_hbm, window_ref, columns_ref, apart_ref, blocks, sems):
    depth, ins = z.depth, z.ins
    moves = (
        (blocks_hbm, blocks),
        (in_hbm, window_ref.at[:depth]),
        (vec_hbm, window_ref.at[ins:]),
        (probes_hbm, columns_ref.at[ins:]),
    )
    copies = [pltpu.make_async_copy(src, dst, sems.at[i]) for i, (src, dst) in enumerate(moves)]
    for copy in copies:
        copy.start()
    for copy in copies:
        copy.wait()
    ones = jnp.where(lax.broadcasted_iota(jnp.int32, (ins - depth, z.own), 0) == 0, 1.0, 0.0)
    window_ref[depth:ins] = ones
    columns_ref[:depth] = window_ref[:depth]
    columns_ref[depth:ins] = ones
    apart_ref[...] = jnp.full(apart_ref.shape, blocks[lax.axis_index("row")] ^ lax.axis_index("col"), jnp.int32)


def pick_kernel(z, own_ref, apart_ref, far_in, far_vec, window_ref):
    depth, ins = z.depth, z.ins

    def nearer(mine, theirs):
        return jnp.where(jnp.broadcast_to(apart_ref[:1] & 1, mine.shape) == 0, mine, theirs)

    window_ref[:depth] = nearer(own_ref[:depth], far_in[...])
    window_ref[depth:ins] = own_ref[depth:ins]
    window_ref[ins:] = nearer(own_ref[ins:], far_vec[...])


def weights_kernel(z, w_in, b_in, w_out, w_stack_ref, out_m_ref, out_k_ref):
    w_all = jnp.concatenate([w_in[0], b_in[...], jnp.zeros((z.ins - z.depth - 1, z.hid), F32)], 0)
    w1, w2, w3 = split(w_all, 3)
    w_stack_ref[...] = stack([w1, w1, w2, w2, w1, w3]).T
    o1, o2 = split(w_out[...])
    out_m_ref[...] = stack([o1, o2])
    out_k_ref[...] = stack([o1, o1, o2, o2]).T


def features(z, blocks_ref, w_stack, out_m, s):
    own, ins, feats, wide, chunk, part = z.own, z.ins, z.feats, z.wide, z.chunk, z.part
    per = chunk // own

    def source(i, start, count, third):
        return jnp.concatenate(
            [blocks_ref[i * per + r, third * part + start : third * part + start + count] for r in range(per)], 1
        )

    for third in range(3):

        def one(i, third=third):
            lanes = pl.ds(third * wide + i * chunk, chunk)
            x = source(i, 0, ins, third)
            s.x[:, lanes] = x
            x1, x2, x3 = split(x, 3)
            h = jnp.tanh(mm(w_stack, stack([x1, x2, x1, x2, x3, x1])))
            h1 = h.astype(BF)
            h2 = (h - h1.astype(F32)).astype(BF)
            s.h1[:, lanes], s.h2[:, lanes] = h1, h2
            raw = mm(out_m, h1) + mm(out_m, h2)
            f1, f2 = split(raw[:feats] + raw[feats:])
            s.m[:, lanes] = stack([f1, f2, jnp.ones((16, chunk), F32)])
            exact = f1 + f2
            square = exact * exact
            v1, v2 = split(source(i, ins, z.vecs, third))
            if third == 0:
                rows = pl.ds(i * chunk, chunk)
                s.wink[rows, :] = stack([f1, f2, f1, f2]).T
                s.winv[rows, :] = stack([v1, v2, v1, v2]).T
                s.winn[rows, :] = mm_tn(stack(split(square, 3)), jnp.full((3 * feats, own), 0.5, BF))
            else:
                here = pl.ds((third - 1) * wide + i * chunk, chunk)
                s.vec[:, here] = stack([v1, v1, v2, v2])
                s.norm[:, here] = jnp.broadcast_to(0.5 * jnp.sum(square, 0, keepdims=True), (8, chunk))

        each(wide // chunk, one)


def tiles(z, win, col, raw_ref, tot_ref):
    feats, wide, chunk = z.feats, z.wide, z.chunk

    def columns(i):
        here, lanes = pl.ds(i * chunk, chunk), pl.ds(wide + i * chunk, chunk)
        m = col.m[:, lanes]
        f1, f2 = m[:feats], m[feats : 2 * feats]
        f_stack = jnp.concatenate([f1, f1, f2, f2], 0)
        vec, norm = col.vec[:, here], col.norm[:1, here]

        def windows(k):
            rows = pl.ds(k * chunk, chunk)
            far = jnp.concatenate([win.winn[rows, :]] * (chunk // z.own), 1)
            kern = jnp.exp(mm(win.wink[rows, :], f_stack) - far - norm)
            weigh = kern * mm(win.winv[rows, :], vec)
            g1 = weigh.astype(BF)
            g2 = (weigh - g1.astype(F32)).astype(BF)
            mine = win.m[:, rows]
            tot_ref[:, rows] += mm_nt(m, g1) + mm_nt(m, g2)
            raw_ref[:, here] += mm(mine, g1) + mm(mine, g2)

        each(wide // chunk, windows)

    each(2 * wide // chunk, columns)


def early_kernel(z, names, blocks_ref, w_stack_ref, out_m_ref, *outs):
    s = Refs(names, outs)
    features(z, blocks_ref, w_stack_ref[...], out_m_ref[...], s)
    s.raw[...] = jnp.zeros(s.raw.shape, F32)
    s.tot[...] = jnp.zeros(s.tot.shape, F32)
    tiles(z, s, s, s.raw, s.tot)


def late_kernel(z, names, blocks_ref, w_stack_ref, out_m_ref, out_k_ref, *refs):
    feats, wide, chunk, ins = z.feats, z.wide, z.chunk, z.ins
    n = len(names)
    a, (col_grad_ref, pack_ref), b = Refs(names, refs[:n]), refs[n : n + 2], Refs(names, refs[n + 2 : 2 * n + 2])
    raw_ref, tot_ref, grad_ref = refs[2 * n + 2 :]
    features(z, blocks_ref, w_stack_ref[...], out_m_ref[...], b)
    raw_ref[...] = a.raw[...]
    tot_ref[...] = a.tot[...]
    b.raw[...] = jnp.zeros(b.raw.shape, F32)
    b.tot[...] = jnp.zeros(b.tot.shape, F32)
    tiles(z, b, a, raw_ref, b.tot)
    tiles(z, a, b, b.raw, tot_ref)
    tiles(z, b, b, b.raw, b.tot)
    pack_ref[...] = jnp.zeros(pack_ref.shape, F32)
    out_k = out_k_ref[...]
    for k, (s, raw, tot) in enumerate(((a, raw_ref, tot_ref), (b, b.raw, b.tot))):

        def backward(i, s=s, source=None, start=0, shift=0, first=False):
            lanes = pl.ds(start + i * chunk, chunk)
            sums = source[:, pl.ds(i * chunk + shift, chunk)]
            m = s.m[:, lanes].astype(F32)
            exact = m[:feats] + m[feats : 2 * feats]
            t = sums[:feats] + sums[feats : 2 * feats] - exact * sums[2 * feats : 2 * feats + 1]
            if first:
                grad_ref[:, pl.ds(i * chunk, chunk)] = t
            t1, t2 = split(t)
            h1, h2 = s.h1[:, lanes], s.h2[:, lanes]
            h = h1.astype(F32) + h2.astype(F32)
            g = mm(out_k, stack([t1, t2, t1, t2])) * (1.0 - h * h)
            t_stack = stack([t1, t2])
            both = mm_nt(t_stack, h1) + mm_nt(t_stack, h2)
            pack_ref[:feats] += both[:feats] + both[feats:]
            x1, x2 = split(s.x[:, lanes])
            x_stack = stack([x1, x2])
            g1 = g.astype(BF)
            g2 = (g - g1.astype(F32)).astype(BF)
            both = mm_nt(x_stack, g1) + mm_nt(x_stack, g2)
            pack_ref[feats:] += both[:ins] + both[ins:]

        each(2 * wide // chunk, functools.partial(backward, source=raw, start=wide, first=k == 0))
        each(wide // chunk, functools.partial(backward, source=tot))
    col_grad_ref[...] = grad_ref[:, : z.own]


def finish_kernel(z, mine_ref, theirs_ref, grad_in_ref, grad_bias_ref, grad_out_ref):
    both = mine_ref[...] + theirs_ref[...]
    grad_out_ref[...] = both[: z.feats]
    grad_in_ref[...] = both[z.feats : z.feats + z.depth]
    grad_bias_ref[...] = both[z.feats + z.depth : z.feats + z.depth + 1]


def whole(count):
    return [pl.BlockSpec(memory_space=VMEM)] * count


def shapes(spec):
    return [jax.ShapeDtypeStruct(*v) for v in spec.values()]


def call(kernel, name, outs, operands, scratch=(), limit=4, cost=1, place=VMEM):
    return pl.pallas_call(
        kernel,
        out_shape=tuple(outs),
        in_specs=[pl.BlockSpec(memory_space=place)] * len(operands),
        out_specs=tuple(whole(len(outs))),
        scratch_shapes=list(scratch),
        compiler_params=pltpu.CompilerParams(vmem_limit_bytes=limit << 20),
        cost_estimate=pl.CostEstimate(flops=cost * 10**8, bytes_accessed=10**6, transcendentals=0),
        name=name,
    )(*operands)


def body(n_row, n_col, protocols, w_in, b_in, w_out, solved, probes, window_blocks):
    depth, own = protocols.shape
    z = Sizes(depth, solved.shape[0], w_out.shape[0], w_out.shape[1], own, n_row)
    bits = bits_of(n_col)
    shared, joined = bits[:-1], bits[-1]
    limit = 12 if n_row <= 4 else 48
    f32 = functools.partial(jax.ShapeDtypeStruct, dtype=F32)

    theirs = swap(protocols, "col", n_col, 1), swap(solved, "col", n_col, 1)
    blk = f32((z.part, own))
    window, columns, apart = call(
        functools.partial(prepare_kernel, z),
        "prepare",
        (blk, blk, jax.ShapeDtypeStruct((8, own), jnp.int32)),
        [pltpu.with_memory_space_constraint(v, pltpu.HBM) for v in (window_blocks, protocols, solved, probes)],
        [pltpu.SMEM(window_blocks.shape, jnp.int32), pltpu.SemaphoreType.DMA((4,))],
        place=pltpu.HBM,
    )
    (window,) = call(functools.partial(pick_kernel, z), "pick", (blk,), (window, apart, *theirs))

    def nearer(bit, mine, theirs):
        return jnp.where((apart[:1] & bit) == 0, mine, theirs)

    window, w_in, b_in, w_out = lax.optimization_barrier((window, w_in, b_in, w_out))
    w_stack, out_m, out_k = call(
        functools.partial(weights_kernel, z),
        "weights",
        (
            jax.ShapeDtypeStruct((z.hid, 6 * z.ins), BF),
            jax.ShapeDtypeStruct((2 * z.feats, z.hid), BF),
            jax.ShapeDtypeStruct((z.hid, 4 * z.feats), BF),
        ),
        (w_in[None], b_in.reshape(1, -1), w_out.T),
    )
    for bit in shared[1:]:
        window = nearer(bit, window, swap(window, "col", n_col, bit))
    window, w_stack, out_m, out_k = lax.optimization_barrier((window, w_stack, out_m, out_k))
    got = swap(jnp.concatenate([window, columns]), "col", n_col, joined)
    window = nearer(joined, window, got[: z.part])
    blocks = jnp.concatenate([window, columns, got[z.part :]])[None]
    for bit in reversed(bits_of(n_row)[1:]):
        blocks = jnp.concatenate([blocks, swap(blocks, "row", n_row, bit)])
    far_blocks = swap(blocks, "row", n_row, 1)

    kept = z.half() | z.sums()
    early = call(
        functools.partial(early_kernel, z, list(kept)),
        "early",
        shapes(kept),
        (blocks, w_stack, out_m),
        limit=limit,
        cost=10,
    )
    col_grad, pack = call(
        functools.partial(late_kernel, z, list(kept)),
        "late",
        (f32((z.feats, own)), f32((z.feats + z.ins, z.hid))),
        (far_blocks, w_stack, out_m, out_k, *early),
        [VMEM(*v) for v in (kept | {"r": kept["raw"], "t": kept["tot"], "g": ((z.feats, 2 * z.wide), F32)}).values()],
        limit=limit,
        cost=20,
    )
    for bit in reversed(shared[1:]):
        pack = pack + swap(pack, "col", n_col, bit)
    grad_in, grad_bias, grad_out = call(
        functools.partial(finish_kernel, z),
        "finish",
        (f32((depth, z.hid)), f32((1, z.hid)), f32((z.feats, z.hid))),
        (pack, swap(pack, "col", n_col, shared[0])),
    )
    return (col_grad, grad_in, grad_bias.reshape(-1), grad_out.T)


def solution(mesh):
    n_row, n_col = mesh.shape["row"], mesh.shape["col"]
    cut = P(None, ("row", "col"))

    def per_device(*args):
        return body(n_row, n_col, *args)

    return jax.shard_map(
        per_device,
        mesh=mesh,
        in_specs=(cut, P(), P(), P(), cut, cut, P()),
        out_specs=(cut, P(), P(), P()),
        check_vma=False,
    )
```

time: 48.5 us -> 33.6 us (0.69)
  matrix products: 14.1 us -> 0 us
  Pallas kernels: 0 us -> 7.2 us
  local copies, waits for them, and re-layouts: 3.8 us -> 0.67 us
  other arithmetic: 3.12 us -> 0.07 us
  waiting for transfers between devices: 13.3 us -> 12.1 us
  between operations: 1.53 us -> 0.69 us
  starting transfers between devices: 12 us -> 12.5 us
    dot_general x9 -> x0, matrix products: 14.1 us -> none  [the longest x1 2.45 us: weight_grads(): cross = jnp.einsum('fi,fj->ij', first, second, precision=HIGHEST)]
    pallas_call x0 -> x6, Pallas kernels: none -> 7.2 us  [call(): pl.pallas_call(kernel, out_shape=tuple(outs), in_specs=[pl.BlockSpec(memo...]
    slice x3 -> x0, local copies, waits for them, and re-layouts: 1.79 us -> none  [the longest x1 0.62 us: body(): col_grad[:, :own]]
    ppermute x7 -> x8, waiting for transfers between devices: 13.3 us -> 12.1 us  [swap(): return lax.ppermute(value, axis, [(i, i ^ bit) for i in range(size)])]
    dynamic_slice x1 -> x0, local copies, waits for them, and re-layouts: 1.24 us -> none  [body(): apart = lax.axis_index('col') ^ window_blocks[lax.axis_index('row')]]
    concatenate x2 -> x0, other arithmetic: 0.77 us -> none  [the longest x1 0.76 us: body(): window = jnp.concatenate([protocols, solved])]
    select_n x3 -> x2, other arithmetic: 0.75 us -> 0.01 us  [nearer(): return jnp.where(apart[:1] & bit == 0, mine, theirs)]
    concatenate x1, other arithmetic: 0.73 us -> 0.01 us  [body(): got = swap(jnp.concatenate([window, columns]), 'col', n_col, joined)]
  transfers between devices with their start and end apart: 7 -> 8, of which waited for: 6 -> 7; matrix products, arithmetic and copies ran while one was open for 4% -> 0% of each run, Pallas kernels for 0% -> 7%
where the time goes in v3:
time: 33.6 us; the launch traced here: 33.3 us
  starting transfers between devices  12.5 us (37%)
  waiting for transfers between devices  12.1 us (36%)
  Pallas kernels  7.2 us (21%)
  between operations  0.69 us (2%)
  local copies, waits for them, and re-layouts  0.67 us (2%)
    ppermute x8, starting transfers between devices, swap(): return lax.ppermute(value, axis, [(i, i ^ bit) for i in range(size)])  12.5 us
    ppermute x8, waiting for transfers between devices, swap(): return lax.ppermute(value, axis, [(i, i ^ bit) for i in range(size)])  12.1 us
    pallas_call x6, Pallas kernels, call(): pl.pallas_call(kernel, out_shape=tuple(outs), in_specs=[pl.BlockSpec(memo...  7.2 us
    unnamed x6, local copies, waits for them, and re-layouts  0.67 us
  transfers between devices with their start and end apart: 8, of which 7 were waited for; matrix products, arithmetic and copies ran while one was open for 0% of the time, Pallas kernels for 7%

profile of v3, /device:TPU:0, one launch (start us, length us, event | category | flops | bytes accessed | tf_op | source)
XLA Modules:
  0.0 33.3 jit_solution(14500388706246972306)
XLA Ops:
  0.6 0.5 %collective-permute-start.1 = (f32[32,128]{1,0:T(8,128)}, f32[32,128]{1,0:T(8,128)S(1)}, u32[]{:S(2)}, u32[]{:S(2)}) collective-permute-start(f32[32,128]{1,0:T(8,128)} %vec_hbm.1), channel_id=1, source_target_pairs={{0,1},{1,0},{2,3},{3,2},{4,5},{5,4},{6,7},{7,6},{8,9},{9,8},{10,11... | collective-permute-start | bytes 49160 | tf_op jit(solution)/shard_map/ppermute | solution.py:15
  1.1 0.1 collective-permute-start
  1.2 0.8 %prepare.1 = (f32[56,128]{1,0:T(8,128)S(1)}, f32[56,128]{1,0:T(8,128)S(1)}, s32[8,128]{1,0:T(8,128)S(1)}) custom-call(s32[4]{0:T(128)} %blocks_hbm.1, f32[20,128]{1,0:T(8,128)} %in_hbm.1, f32[32,128]{1,0:T(8,128)} %vec_hbm.1, f32[32,128]{1,0:T(8,128)} %probes_hbm.1), custom_call_target="tpu_custom_call" | custom-call | flops 100000000 | bytes 1000000 | tf_op jit(solution)/shard_map/prepare/pallas_call | solution.py:265
  2.0 0.5 %collective-permute-done.far_in = f32[20,128]{1,0:T(8,128)S(1)} collective-permute-done((f32[20,128]{1,0:T(8,128)}, f32[20,128]{1,0:T(8,128)S(1)}, u32[]{:S(2)}, u32[]{:S(2)}) %collective-permute-start) | collective-permute-done | bytes 10272 | tf_op jit(solution)/shard_map/ppermute | solution.py:15
  2.5 0.0 collective-permute-done.1.far_vec
  2.5 0.0 copy-start
  2.5 0.0 copy-start.1
  2.6 2.7 %collective-permute-start.2 = (f32[56,128]{1,0:T(8,128)S(1)}, f32[56,128]{1,0:T(8,128)S(1)}, u32[]{:S(2)}, u32[]{:S(2)}) collective-permute-start(f32[56,128]{1,0:T(8,128)S(1)} %pick.1), channel_id=1, source_target_pairs={{0,2},{1,3},{2,0},{3,1},{4,6},{5,7},{6,4},{7,5},{8,10},{9,11},{10,... | collective-permute-start | bytes 86024 | tf_op jit(solution)/shard_map/ppermute | solution.py:15
  5.3 0.0 copy-start.2
  5.3 0.0 copy-done
  5.3 0.0 copy-done.1
  5.3 0.7 %copy-done.2 = f32[256]{0:T(256)S(1)} copy-done((f32[256]{0:T(256)S(1)}, f32[256]{0:T(256)}, u32[]{:S(2)}) %copy-start.2) | copy-done | bytes 1048
  6.0 0.1 weights.1
  6.1 1.0 %collective-permute-done.2 = f32[56,128]{1,0:T(8,128)S(1)} collective-permute-done((f32[56,128]{1,0:T(8,128)S(1)}, f32[56,128]{1,0:T(8,128)S(1)}, u32[]{:S(2)}, u32[]{:S(2)}) %collective-permute-start.2) | collective-permute-done | bytes 28704 | tf_op jit(solution)/shard_map/ppermute | solution.py:15
  7.1 2.1 %collective-permute-start.3 = (f32[112,128]{1,0:T(8,128)S(1)}, f32[112,128]{1,0:T(8,128)S(1)}, u32[]{:S(2)}, u32[]{:S(2)}) collective-permute-start(f32[112,128]{1,0:T(8,128)S(1)} %pad_maximum_fusion.1), channel_id=1, source_target_pairs={{0,4},{1,5},{2,6},{3,7},{4,0},{5,1},{6,2},{7,3},{8,12},{9,13},{10,... | collective-permute-start | bytes 172040 | tf_op jit(solution)/shard_map/ppermute | solution.py:15
  9.3 2.2 %collective-permute-done.3 = f32[112,128]{1,0:T(8,128)S(1)} collective-permute-done((f32[112,128]{1,0:T(8,128)S(1)}, f32[112,128]{1,0:T(8,128)S(1)}, u32[]{:S(2)}, u32[]{:S(2)}) %collective-permute-start.3) | collective-permute-done | bytes 57376 | tf_op jit(solution)/shard_map/ppermute | solution.py:15
  11.4 3.2 %collective-permute-start.4 = (f32[1,168,128]{2,1,0:T(8,128)S(1)}, f32[1,168,128]{2,1,0:T(8,128)S(1)}, u32[]{:S(2)}, u32[]{:S(2)}) collective-permute-start(f32[1,168,128]{2,1,0:T(8,128)S(1)} %maximum_bitcast_fusion), channel_id=1, source_target_pairs={{0,16},{8,24},{16,0},{24,8},{1,17},{9,25},{17,1},{25,9},{2,18},{10... | collective-permute-start | bytes 258056 | tf_op jit(solution)/shard_map/ppermute | solution.py:15
  14.6 2.5 %collective-permute-done.4 = f32[1,168,128]{2,1,0:T(8,128)S(1)} collective-permute-done((f32[1,168,128]{2,1,0:T(8,128)S(1)}, f32[1,168,128]{2,1,0:T(8,128)S(1)}, u32[]{:S(2)}, u32[]{:S(2)}) %collective-permute-start.4) | collective-permute-done | bytes 86048 | tf_op jit(solution)/shard_map/ppermute | solution.py:15
  17.1 2.0 %collective-permute-start.5 = (f32[2,168,128]{2,1,0:T(8,128)S(1)}, f32[2,168,128]{2,1,0:T(8,128)S(1)}, u32[]{:S(2)}, u32[]{:S(2)}) collective-permute-start(f32[2,168,128]{2,1,0:T(8,128)S(1)} %pad_maximum_fusion.blocks_ref), channel_id=1, source_target_pairs={{0,8},{8,0},{16,24},{24,16},{1,9},{9,1},{17,25},{25,17},{2,10},{10... | collective-permute-start | bytes 516104 | tf_op jit(solution)/shard_map/ppermute | solution.py:15
  19.1 1.5 %early.1 = (f32[24,768]{1,0:T(8,128)S(1)}, bf16[256,768]{1,0:T(8,128)(2,1)S(1)}, bf16[256,768]{1,0:T(8,128)(2,1)S(1)}, bf16[144,768]{1,0:T(8,128)(2,1)S(1)}, bf1...) custom-call(f32[2,168,128]{2,1,0:T(8,128)S(1)} %pad_maximum_fusion.b, ...), custom_call_target="tpu_custom_call" | custom-call | flops 1000000000 | bytes 1000000 | tf_op jit(solution)/shard_map/early/pallas_call | solution.py:265
  20.6 2.0 %collective-permute-done.5.blocks_ref = f32[2,168,128]{2,1,0:T(8,128)S(1)} collective-permute-done((f32[2,168,128]{2,1,0:T(8,128)S(1)}, f32[2,168,128]{2,1,0:T(8,128)S(1)}, u32[]{:S(2)}, u32[]{:S(2)}) %collective-permute-start.5) | collective-permute-done | bytes 172064 | tf_op jit(solution)/shard_map/ppermute | solution.py:15
  22.5 4.1 %late.1 = (f32[64,128]{1,0:T(8,128)}, f32[88,256]{1,0:T(8,128)S(1)}) custom-call(f32[2,168,128]{2,1,0:T(8,128)S(1)} %collective-permute-done.5.blocks_ref, bf16[256,144]{1,0:T(8,128)(2,1)S(1)} %get-tuple-element.45.w_stack_ref, bf16[128,256]{1,0:T(8,128)(2,1)S(1)} %get-tuple-element.46.out_m_ref, bf16[256,256]{1,0:T(8,128)(2,1)S(1)} %get-tuple-element.47.out_k_ref, ...), custom_call_target="tpu_custom_call" | custom-call | flops 2000000000 | bytes 1000000 | tf_op jit(solution)/shard_map/late/pallas_call | solution.py:265
  26.7 1.9 %collective-permute-start.6 = (f32[88,256]{1,0:T(8,128)S(1)}, f32[88,256]{1,0:T(8,128)S(1)}, u32[]{:S(2)}, u32[]{:S(2)}) collective-permute-start(f32[88,256]{1,0:T(8,128)S(1)} %get-tuple-element.60), channel_id=1, source_target_pairs={{0,2},{1,3},{2,0},{3,1},{4,6},{5,7},{6,4},{7,5},{8,10},{9,11},{10,... | collective-permute-start | bytes 270344 | tf_op jit(solution)/shard_map/ppermute | solution.py:15
  28.6 2.7 %collective-permute-done.6 = f32[88,256]{1,0:T(8,128)S(1)} collective-permute-done((f32[88,256]{1,0:T(8,128)S(1)}, f32[88,256]{1,0:T(8,128)S(1)}, u32[]{:S(2)}, u32[]{:S(2)}) %collective-permute-start.6) | collective-permute-done | bytes 90144 | tf_op jit(solution)/shard_map/ppermute | solution.py:15
  31.3 0.1 collective-permute-start.7
  31.4 1.3 %collective-permute-done.7.theirs_ref = f32[88,256]{1,0:T(8,128)S(1)} collective-permute-done((f32[88,256]{1,0:T(8,128)S(1)}, f32[88,256]{1,0:T(8,128)S(1)}, u32[]{:S(2)}, u32[]{:S(2)}) %collective-permute-start.7) | collective-permute-done | bytes 90144 | tf_op jit(solution)/shard_map/ppermute | solution.py:15
  32.6 0.6 %finish.1 = (f32[20,256]{1,0:T(8,128)}, f32[1,256]{1,0:T(1,128)}, f32[64,256]{1,0:T(8,128)}) custom-call(f32[88,256]{1,0:T(8,128)S(1)} %add.3.mine_ref, f32[88,256]{1,0:T(8,128)S(1)} %collective-permute-done.7.theirs_ref), custom_call_target="tpu_custom_call" | custom-call | flops 100000000 | bytes 1000000 | tf_op jit(solution)/shard_map/finish/pallas_call | solution.py:265
  (8 shorter events, 0.1 us)
Async XLA Ops:
  0.6 1.9 %collective-permute-start.1 = (f32[32,128]{1,0:T(8,128)}, f32[32,128]{1,0:T(8,128)S(1)}, u32[]{:S(2)}, u32[]{:S(2)}) collective-permute-start(f32[32,128]{1,0:T(8,128)} %vec_hbm.1), channel_id=1, source_target_pairs={{0,1},{1,0},{2,3},{3,2},{4,5},{5,4},{6,7},{7,6},{8,9},{9,8},{10,11... | collective-permute-start | bytes 49160 | tf_op jit(solution)/shard_map/ppermute | solution.py:15
  1.1 1.4 %collective-permute-start = (f32[20,128]{1,0:T(8,128)}, f32[20,128]{1,0:T(8,128)S(1)}, u32[]{:S(2)}, u32[]{:S(2)}) collective-permute-start(f32[20,128]{1,0:T(8,128)} %in_hbm.1), channel_id=1, source_target_pairs={{0,1},{1,0},{2,3},{3,2},{4,5},{5,4},{6,7},{7,6},{8,9},{9,8},{10,11... | collective-permute-start | bytes 30728 | tf_op jit(solution)/shard_map/ppermute | solution.py:15
  2.5 2.7 %copy-start = (f32[256,64]{0,1:T(8,128)S(1)}, f32[256,64]{0,1:T(8,128)}, u32[]{:S(2)}) copy-start(f32[256,64]{0,1:T(8,128)} %param.10) | copy-start | bytes 196612
  2.5 2.7 %copy-start.1 = (f32[20,256]{1,0:T(8,128)S(1)}, f32[20,256]{1,0:T(8,128)}, u32[]{:S(2)}) copy-start(f32[20,256]{1,0:T(8,128)} %param.8) | copy-start | bytes 61444
  2.6 4.6 %collective-permute-start.2 = (f32[56,128]{1,0:T(8,128)S(1)}, f32[56,128]{1,0:T(8,128)S(1)}, u32[]{:S(2)}, u32[]{:S(2)}) collective-permute-start(f32[56,128]{1,0:T(8,128)S(1)} %pick.1), channel_id=1, source_target_pairs={{0,2},{1,3},{2,0},{3,1},{4,6},{5,7},{6,4},{7,5},{8,10},{9,11},{10,... | collective-permute-start | bytes 86024 | tf_op jit(solution)/shard_map/ppermute | solution.py:15
  5.3 0.7 %copy-start.2 = (f32[256]{0:T(256)S(1)}, f32[256]{0:T(256)}, u32[]{:S(2)}) copy-start(f32[256]{0:T(256)} %param.9) | copy-start | bytes 3076
  7.1 4.3 %collective-permute-start.3 = (f32[112,128]{1,0:T(8,128)S(1)}, f32[112,128]{1,0:T(8,128)S(1)}, u32[]{:S(2)}, u32[]{:S(2)}) collective-permute-start(f32[112,128]{1,0:T(8,128)S(1)} %pad_maximum_fusion.1), channel_id=1, source_target_pairs={{0,4},{1,5},{2,6},{3,7},{4,0},{5,1},{6,2},{7,3},{8,12},{9,13},{10,... | collective-permute-start | bytes 172040 | tf_op jit(solution)/shard_map/ppermute | solution.py:15
  11.4 5.6 %collective-permute-start.4 = (f32[1,168,128]{2,1,0:T(8,128)S(1)}, f32[1,168,128]{2,1,0:T(8,128)S(1)}, u32[]{:S(2)}, u32[]{:S(2)}) collective-permute-start(f32[1,168,128]{2,1,0:T(8,128)S(1)} %maximum_bitcast_fusion), channel_id=1, source_target_pairs={{0,16},{8,24},{16,0},{24,8},{1,17},{9,25},{17,1},{25,9},{2,18},{10... | collective-permute-start | bytes 258056 | tf_op jit(solution)/shard_map/ppermute | solution.py:15
  17.1 5.5 %collective-permute-start.5 = (f32[2,168,128]{2,1,0:T(8,128)S(1)}, f32[2,168,128]{2,1,0:T(8,128)S(1)}, u32[]{:S(2)}, u32[]{:S(2)}) collective-permute-start(f32[2,168,128]{2,1,0:T(8,128)S(1)} %pad_maximum_fusion.blocks_ref), channel_id=1, source_target_pairs={{0,8},{8,0},{16,24},{24,16},{1,9},{9,1},{17,25},{25,17},{2,10},{10... | collective-permute-start | bytes 516104 | tf_op jit(solution)/shard_map/ppermute | solution.py:15
  26.7 4.6 %collective-permute-start.6 = (f32[88,256]{1,0:T(8,128)S(1)}, f32[88,256]{1,0:T(8,128)S(1)}, u32[]{:S(2)}, u32[]{:S(2)}) collective-permute-start(f32[88,256]{1,0:T(8,128)S(1)} %get-tuple-element.60), channel_id=1, source_target_pairs={{0,2},{1,3},{2,0},{3,1},{4,6},{5,7},{6,4},{7,5},{8,10},{9,11},{10,... | collective-permute-start | bytes 270344 | tf_op jit(solution)/shard_map/ppermute | solution.py:15
  31.3 1.4 %collective-permute-start.7 = (f32[88,256]{1,0:T(8,128)S(1)}, f32[88,256]{1,0:T(8,128)S(1)}, u32[]{:S(2)}, u32[]{:S(2)}) collective-permute-start(f32[88,256]{1,0:T(8,128)S(1)} %add.3.mine_ref), channel_id=1, source_target_pairs={{0,1},{1,0},{2,3},{3,2},{4,5},{5,4},{6,7},{7,6},{8,9},{9,8},{10,11... | collective-permute-start | bytes 270344 | tf_op jit(solution)/shard_map/ppermute | solution.py:15

commit v4 on v3

v4 whole, which is shorter than its diff:
```python
import functools

import jax
import jax.numpy as jnp
from jax import lax
from jax.experimental import pallas as pl
from jax.experimental.pallas import tpu as pltpu
from jax.sharding import PartitionSpec as P

BF, F32 = jnp.bfloat16, jnp.float32
VMEM = pltpu.VMEM


def swap(value, axis, size, bit):
    return lax.ppermute(value, axis, [(i, i ^ bit) for i in range(size)])


def bits_of(size):
    return [1 << k for k in range(size.bit_length() - 1)]


def split(value, terms=2):
    parts = []
    for _ in range(terms):
        part = value.astype(BF).astype(F32)
        parts.append(part)
        value = value - part
    return parts


def stack(parts):
    return jnp.concatenate(parts, 0).astype(BF)


def mm(a, b):
    return lax.dot_general(a, b, (((1,), (0,)), ((), ())), preferred_element_type=F32)


def mm_nt(a, b):
    return lax.dot_general(a, b, (((1,), (1,)), ((), ())), preferred_element_type=F32)


def mm_tn(a, b):
    return lax.dot_general(a, b, (((0,), (0,)), ((), ())), preferred_element_type=F32)


def each(count, step):
    if count <= 4:
        for i in range(count):
            step(i)
    else:
        lax.fori_loop(0, count, lambda i, c: (step(i), c)[1], 0)


def flow(count, *stages):
    held = {}
    for t in range(count + len(stages) - 1):
        for depth, stage in enumerate(stages):
            k = t - depth
            if 0 <= k < count:
                held[k] = stage(k, held.get(k))


def up(value, to):
    return -(-value // to) * to


class Sizes:
    def __init__(self, depth, vecs, hid, feats, own, n_row):
        self.depth, self.vecs, self.hid, self.feats, self.own = depth, vecs, hid, feats, own
        self.ins = up(depth + 1, 8)
        self.part = self.ins + vecs
        self.wide = n_row // 2 * own
        self.cols = n_row * own
        self.rows = 2 * feats + 16
        self.win_step = min(256, self.wide)
        self.win_piece = min(256, self.win_step)
        self.col_step = min(512, self.cols)

    def network(self, lanes):
        return dict(
            x=((self.ins, lanes), F32),
            h1=((self.hid, lanes), BF),
            h2=((self.hid, lanes), BF),
            m=((self.rows, lanes), BF),
        )

    def windows(self):
        w = self.wide
        return self.network(w) | dict(
            key=((w, 4 * self.feats), BF),
            vec=((w, 4 * self.vecs), BF),
            norm=((w, self.own), F32),
            sums=((w, self.rows), F32),
        )

    def columns(self):
        c = self.cols
        return self.network(c) | dict(vec=((4 * self.vecs, c), BF), norm=((8, c), F32), sums=((self.rows, c), F32))


class Refs:
    def __init__(self, names, refs):
        self.__dict__.update(zip(names, refs, strict=True))


def prepare_kernel(z, blocks_hbm, in_hbm, vec_hbm, probes_hbm, window_ref, columns_ref, apart_ref, blocks, sems):
    depth, ins = z.depth, z.ins
    moves = (
        (blocks_hbm, blocks),
        (in_hbm, window_ref.at[:depth]),
        (vec_hbm, window_ref.at[ins:]),
        (probes_hbm, columns_ref.at[ins:]),
    )
    copies = [pltpu.make_async_copy(src, dst, sems.at[i]) for i, (src, dst) in enumerate(moves)]
    for copy in copies:
        copy.start()
    for copy in copies:
        copy.wait()
    ones = jnp.where(lax.broadcasted_iota(jnp.int32, (ins - depth, z.own), 0) == 0, 1.0, 0.0)
    window_ref[depth:ins] = ones
    columns_ref[:depth] = window_ref[:depth]
    columns_ref[depth:ins] = ones
    apart_ref[...] = jnp.full(apart_ref.shape, blocks[lax.axis_index("row")] ^ lax.axis_index("col"), jnp.int32)


def pick_kernel(z, own_ref, apart_ref, far_in, far_vec, window_ref):
    depth, ins = z.depth, z.ins

    def nearer(mine, theirs):
        return jnp.where(jnp.broadcast_to(apart_ref[:1] & 1, mine.shape) == 0, mine, theirs)

    window_ref[:depth] = nearer(own_ref[:depth], far_in[...])
    window_ref[depth:ins] = own_ref[depth:ins]
    window_ref[ins:] = nearer(own_ref[ins:], far_vec[...])


def weights_kernel(z, w_in, b_in, w_out, w_stack_ref, out_m_ref, out_k_ref):
    w_all = jnp.concatenate([w_in[0], b_in[...], jnp.zeros((z.ins - z.depth - 1, z.hid), F32)], 0)
    w1, w2, w3 = split(w_all, 3)
    w_stack_ref[...] = stack([w1, w1, w2, w2, w1, w3]).T
    o1, o2 = split(w_out[...])
    out_m_ref[...] = stack([o1, o2])
    out_k_ref[...] = stack([o1, o1, o2, o2]).T


def network(z, s, w_stack, out_m):
    def into(lanes):
        x1, x2, x3 = split(s.x[:, lanes], 3)
        return mm(w_stack, stack([x1, x2, x1, x2, x3, x1]))

    def middle(lanes, pre):
        h = jnp.tanh(pre)
        h1 = h.astype(BF)
        h2 = (h - h1.astype(F32)).astype(BF)
        s.h1[:, lanes], s.h2[:, lanes] = h1, h2
        return mm(out_m, h1) + mm(out_m, h2)

    def out(lanes, raw):
        f1, f2 = split(raw[: z.feats] + raw[z.feats :])
        s.m[:, lanes] = stack([f1, f2, jnp.ones((16, raw.shape[1]), F32)])
        exact = f1 + f2
        return 0.5 * jnp.sum(exact * exact, 0, keepdims=True)

    return into, middle, out


def window_features(z, blocks_ref, s, w_stack, out_m):
    own, part, step = z.own, z.part, z.win_step
    for r in range(z.wide // own):
        here = pl.ds(r * own, own)
        s.x[:, here] = blocks_ref[r * part : r * part + z.ins]
        v1, v2 = split(blocks_ref[r * part + z.ins : (r + 1) * part])
        s.vec[here, :] = stack([v1, v2, v1, v2]).T
    into, middle, out = network(z, s, w_stack, out_m)

    def one(i):
        rows = [pl.ds(i * step + k * z.win_piece, z.win_piece) for k in range(step // z.win_piece)]

        def last(k, raw):
            norm = out(rows[k], raw)
            s.key[rows[k], :] = jnp.concatenate([s.m[: 2 * z.feats, rows[k]]] * 2, 0).T
            s.norm[rows[k], :] = jnp.broadcast_to(norm, (own, z.win_piece)).T

        flow(len(rows), lambda k, _: into(rows[k]), lambda k, pre: middle(rows[k], pre), last)

    each(z.wide // step, one)
    s.sums[...] = jnp.zeros(s.sums.shape, F32)


def column_blocks(z, blocks_ref, s):
    for r in range(z.cols // z.own):
        here = pl.ds(r * z.own, z.own)
        s.x[:, here] = blocks_ref[r * z.part : r * z.part + z.ins]
        v1, v2 = split(blocks_ref[r * z.part + z.ins : (r + 1) * z.part])
        s.vec[:, here] = stack([v1, v1, v2, v2])


def beside(parts):
    return jnp.concatenate(parts, 1)


def tile(z, win, col):
    feats, step = z.feats, z.win_step
    single = z.wide == step

    def products(lanes, rows):
        m = col.m[: 2 * feats, lanes]
        f1, f2 = m[:feats], m[feats:]
        cross = mm(win.key[rows, :], jnp.concatenate([f1, f1, f2, f2], 0))
        return cross, mm(win.vec[rows, :], col.vec[:, lanes])

    def weighed(lanes, rows, dots):
        far = beside([win.norm[rows, :]] * (z.col_step // z.own))
        weigh = jnp.exp(dots[0] - far - col.norm[:1, lanes]) * dots[1]
        g1 = weigh.astype(BF)
        g2 = (weigh - g1.astype(F32)).astype(BF)
        both = jnp.concatenate([g1, g2], 0)
        mine = win.m[:, rows]
        part = mm_nt(both, col.m[:, lanes])
        win.sums[rows, :] += part[:step] + part[step:]
        return mm(beside([mine, mine]), both)

    def first(lanes):
        return products(lanes, pl.ds(0, step)) if single else None

    def second(lanes, dots):
        if single:
            return weighed(lanes, pl.ds(0, step), dots)

        def add(k, sums):
            rows = pl.ds(k * step, step)
            return sums + weighed(lanes, rows, products(lanes, rows))

        return lax.fori_loop(0, z.wide // step, add, jnp.zeros((z.rows, z.col_step), F32))

    return first, second


def total_of(z, m, sums):
    feats = z.feats
    m = m[: 2 * feats].astype(F32)
    return sums[:feats] + sums[feats : 2 * feats] - (m[:feats] + m[feats:]) * sums[2 * feats : 2 * feats + 1]


def backprop(z, s, out_k, pack_ref):
    def first(lanes, total):
        t1, t2 = split(total)
        t_stack = stack([t1, t2])
        g = mm(out_k, jnp.concatenate([t_stack, t_stack], 0))
        both = mm_nt(beside([t_stack, t_stack]), beside([s.h1[:, lanes], s.h2[:, lanes]]))
        pack_ref[: z.feats] += both[: z.feats] + both[z.feats :]
        return g

    def second(lanes, g):
        h = s.h1[:, lanes].astype(F32) + s.h2[:, lanes].astype(F32)
        g = g * (1.0 - h * h)
        x_stack = stack(split(s.x[:, lanes]))
        g1 = g.astype(BF)
        g2 = (g - g1.astype(F32)).astype(BF)
        both = mm_nt(beside([x_stack, x_stack]), beside([g1, g2]))
        pack_ref[z.feats :] += both[: z.ins] + both[z.ins :]

    return first, second


def window_total(z, s, rows):
    return total_of(z, s.m[:, rows], s.sums[rows, :].T)


def window_backprop(z, s, out_k, pack_ref):
    first, second = backprop(z, s, out_k, pack_ref)

    def one(i):
        rows = pl.ds(i * z.win_step, z.win_step)
        second(rows, first(rows, window_total(z, s, rows)))

    each(z.wide // z.win_step, one)


def column_steps(z):
    return [pl.ds(k * z.col_step, z.col_step) for k in range(z.cols // z.col_step)]


def column_features(z, blocks_ref, col, win, w_stack, out_m):
    column_blocks(z, blocks_ref, col)
    into, middle, out = network(z, col, w_stack, out_m)
    first, second = tile(z, win, col)
    lanes = column_steps(z)

    def third(k, raw):
        col.norm[:, lanes[k]] = jnp.broadcast_to(out(lanes[k], raw), (8, z.col_step))
        return first(lanes[k])

    def fourth(k, dots):
        col.sums[:, lanes[k]] = second(lanes[k], dots)

    flow(len(lanes), lambda k, _: into(lanes[k]), lambda k, pre: middle(lanes[k], pre), third, fourth)


def near_kernel(z, windows_ref, columns_ref, w_stack_ref, out_m_ref, *refs):
    n = len(z.windows())
    win, col = Refs(z.windows(), refs[:n]), Refs(z.columns(), refs[n:])
    w_stack, out_m = w_stack_ref[...], out_m_ref[...]
    window_features(z, windows_ref, win, w_stack, out_m)
    column_features(z, columns_ref, col, win, w_stack, out_m)


def far_kernel(z, columns_ref, w_stack_ref, out_m_ref, out_k_ref, *refs):
    n, c = len(z.windows()), len(z.columns())
    win, col = Refs(z.windows(), refs[:n]), Refs(z.columns(), refs[n : n + c])
    pack_ref, sums_ref = refs[n + c :]
    sums_ref[...] = win.sums[...]
    win.sums = sums_ref
    column_features(z, columns_ref, col, win, w_stack_ref[...], out_m_ref[...])
    pack_ref[...] = jnp.zeros(pack_ref.shape, F32)
    window_backprop(z, win, out_k_ref[...], pack_ref)


def late_kernel(z, windows_ref, w_stack_ref, out_m_ref, out_k_ref, *refs):
    c = len(z.columns())
    cols = [Refs(z.columns(), refs[:c]), Refs(z.columns(), refs[c : 2 * c])]
    early_pack_ref, col_grad_ref, pack_ref = refs[2 * c : 2 * c + 3]
    win = Refs(z.windows(), refs[2 * c + 3 :])
    pack_ref[...] = early_pack_ref[...]
    window_features(z, windows_ref, win, w_stack_ref[...], out_m_ref[...])
    out_k = out_k_ref[...]
    work = [(col, lanes) for col in cols for lanes in column_steps(z)]
    totals = []

    def total(k, dots):
        col, lanes = work[k]
        sums = col.sums[:, lanes] + tile(z, win, col)[1](lanes, dots)
        totals.append(total_of(z, col.m[:, lanes], sums))

    flow(len(work), lambda k, _: tile(z, win, work[k][0])[0](work[k][1]), total)
    col_grad_ref[...] = totals[0][:, : z.own]
    for i in range(z.wide // z.win_step):
        rows = pl.ds(i * z.win_step, z.win_step)
        work.append((win, rows))
        totals.append(window_total(z, win, rows))
    stages = [backprop(z, s, out_k, pack_ref) for s, _ in work]
    flow(len(work), lambda k, _: stages[k][0](work[k][1], totals[k]), lambda k, g: stages[k][1](work[k][1], g))


def finish_kernel(z, mine_ref, theirs_ref, own_ref, col_grad_ref, grad_in_ref, grad_bias_ref, grad_out_ref):
    col_grad_ref[...] = own_ref[...]
    both = mine_ref[...] + theirs_ref[...]
    grad_out_ref[...] = both[: z.feats]
    grad_in_ref[...] = both[z.feats : z.feats + z.depth]
    grad_bias_ref[...] = both[z.feats + z.depth : z.feats + z.depth + 1]


def whole(count):
    return [pl.BlockSpec(memory_space=VMEM)] * count


def shapes(spec):
    return [jax.ShapeDtypeStruct(*v) for v in spec.values()]


def call(kernel, name, outs, operands, scratch=(), limit=4, cost=1, place=VMEM):
    return pl.pallas_call(
        kernel,
        out_shape=tuple(outs),
        in_specs=[pl.BlockSpec(memory_space=place)] * len(operands),
        out_specs=tuple(whole(len(outs))),
        scratch_shapes=list(scratch),
        compiler_params=pltpu.CompilerParams(vmem_limit_bytes=limit << 20),
        cost_estimate=pl.CostEstimate(flops=cost * 10**8, bytes_accessed=10**6, transcendentals=0),
        name=name,
    )(*operands)


def body(n_row, n_col, protocols, w_in, b_in, w_out, solved, probes, window_blocks):
    depth, own = protocols.shape
    z = Sizes(depth, solved.shape[0], w_out.shape[0], w_out.shape[1], own, n_row)
    bits = bits_of(n_col)
    shared, joined = bits[:-1], bits[-1]
    limit = 12 if n_row <= 4 else 48
    f32 = functools.partial(jax.ShapeDtypeStruct, dtype=F32)

    theirs = swap(protocols, "col", n_col, 1), swap(solved, "col", n_col, 1)
    blk = f32((z.part, own))
    window, columns, apart = call(
        functools.partial(prepare_kernel, z),
        "prepare",
        (blk, blk, jax.ShapeDtypeStruct((8, own), jnp.int32)),
        [pltpu.with_memory_space_constraint(v, pltpu.HBM) for v in (window_blocks, protocols, solved, probes)],
        [pltpu.SMEM(window_blocks.shape, jnp.int32), pltpu.SemaphoreType.DMA((4,))],
        place=pltpu.HBM,
    )
    (window,) = call(functools.partial(pick_kernel, z), "pick", (blk,), (window, apart, *theirs))

    def nearer(bit, mine, theirs):
        return jnp.where((apart[:1] & bit) == 0, mine, theirs)

    window, w_in, b_in, w_out = lax.optimization_barrier((window, w_in, b_in, w_out))
    w_stack, out_m, out_k = call(
        functools.partial(weights_kernel, z),
        "weights",
        (
            jax.ShapeDtypeStruct((z.hid, 6 * z.ins), BF),
            jax.ShapeDtypeStruct((2 * z.feats, z.hid), BF),
            jax.ShapeDtypeStruct((z.hid, 4 * z.feats), BF),
        ),
        (w_in[None], b_in.reshape(1, -1), w_out.T),
    )
    for bit in shared[1:]:
        window = nearer(bit, window, swap(window, "col", n_col, bit))
    columns = jnp.concatenate([columns, swap(columns, "col", n_col, joined)])
    window, columns, w_stack, out_m, out_k = lax.optimization_barrier((window, columns, w_stack, out_m, out_k))
    for bit in reversed(bits_of(n_row)[1:]):
        columns = jnp.concatenate([columns, swap(columns, "row", n_row, bit)])
    far_columns = swap(columns, "row", n_row, 1)
    window = nearer(joined, window, swap(window, "col", n_col, joined))
    for bit in reversed(bits_of(n_row)[1:]):
        window = jnp.concatenate([window, swap(window, "row", n_row, bit)])
    far_window = swap(window, "row", n_row, 1)

    pack_shape = f32((z.feats + z.ins, z.hid))
    near = call(
        functools.partial(near_kernel, z),
        "near",
        (*shapes(z.windows()), *shapes(z.columns())),
        (window, columns, w_stack, out_m),
        limit=limit,
        cost=10,
    )
    windows, near = near[: len(z.windows())], near[len(z.windows()) :]
    *far, early_pack = call(
        functools.partial(far_kernel, z),
        "far",
        (*shapes(z.columns()), pack_shape),
        (far_columns, w_stack, out_m, out_k, *windows),
        [VMEM(*z.windows()["sums"])],
        limit=limit,
        cost=10,
    )
    col_grad, pack = call(
        functools.partial(late_kernel, z),
        "late",
        (f32((z.feats, own)), pack_shape),
        (far_window, w_stack, out_m, out_k, *near, *far, early_pack),
        [VMEM(*v) for v in z.windows().values()],
        limit=limit,
        cost=20,
    )
    for bit in reversed(shared[1:]):
        pack = pack + swap(pack, "col", n_col, bit)
    col_grad, grad_in, grad_bias, grad_out = call(
        functools.partial(finish_kernel, z),
        "finish",
        (f32((z.feats, own)), f32((depth, z.hid)), f32((1, z.hid)), f32((z.feats, z.hid))),
        (pack, swap(pack, "col", n_col, shared[0]), col_grad),
    )
    return (col_grad, grad_in, grad_bias.reshape(-1), grad_out.T)


def solution(mesh):
    n_row, n_col = mesh.shape["row"], mesh.shape["col"]
    cut = P(None, ("row", "col"))

    def per_device(*args):
        return body(n_row, n_col, *args)

    return jax.shard_map(
        per_device,
        mesh=mesh,
        in_specs=(cut, P(), P(), P(), cut, cut, P()),
        out_specs=(cut, P(), P(), P()),
        check_vma=False,
    )
```

time: 33.6 us -> 31.2 us (0.929)
  waiting for transfers between devices: 12.1 us -> 7.27 us
  starting transfers between devices: 12.5 us -> 15.6 us
  Pallas kernels: 7.2 us -> 6.55 us
    ppermute x8 -> x11, waiting for transfers between devices: 12.1 us -> 7.27 us  [swap(): return lax.ppermute(value, axis, [(i, i ^ bit) for i in range(size)])]
    ppermute x8 -> x11, starting transfers between devices: 12.5 us -> 15.6 us  [swap(): return lax.ppermute(value, axis, [(i, i ^ bit) for i in range(size)])]
    pallas_call x6 -> x7, Pallas kernels: 7.2 us -> 6.55 us  [call(): pl.pallas_call(kernel, out_shape=tuple(outs), in_specs=[pl.BlockSpec(memo...]
    unnamed x6 -> x7, local copies, waits for them, and re-layouts: 0.67 us -> 0.69 us
  transfers between devices with their start and end apart: 8 -> 11, of which waited for: 7 -> 5; matrix products, arithmetic and copies ran while one was open for 0% -> 0% of each run, Pallas kernels for 7% -> 12%
where the time goes in v4:
time: 31.2 us; the launch traced here: 30.9 us
  starting transfers between devices  15.6 us (50%)
  waiting for transfers between devices  7.27 us (23%)
  Pallas kernels  6.55 us (21%)
  between operations  0.76 us (2%)
  local copies, waits for them, and re-layouts  0.7 us (2%)
    ppermute x11, starting transfers between devices, swap(): return lax.ppermute(value, axis, [(i, i ^ bit) for i in range(size)])  15.6 us
    ppermute x11, waiting for transfers between devices, swap(): return lax.ppermute(value, axis, [(i, i ^ bit) for i in range(size)])  7.27 us
    pallas_call x7, Pallas kernels, call(): pl.pallas_call(kernel, out_shape=tuple(outs), in_specs=[pl.BlockSpec(memo...  6.55 us
    unnamed x7, local copies, waits for them, and re-layouts  0.69 us
  transfers between devices with their start and end apart: 11, of which 5 were waited for; matrix products, arithmetic and copies ran while one was open for 0% of the time, Pallas kernels for 12%

profile of v4, /device:TPU:0, one launch (start us, length us, event | category | flops | bytes accessed | tf_op | source)
XLA Modules:
  0.0 30.9 jit_solution(4106189784225069477)
XLA Ops:
  0.6 0.5 %collective-permute-start = (f32[20,128]{1,0:T(8,128)}, f32[20,128]{1,0:T(8,128)S(1)}, u32[]{:S(2)}, u32[]{:S(2)}) collective-permute-start(f32[20,128]{1,0:T(8,128)} %in_hbm.1), channel_id=1, source_target_pairs={{0,1},{1,0},{2,3},{3,2},{4,5},{5,4},{6,7},{7,6},{8,9},{9,8},{10,11... | collective-permute-start | bytes 30728 | tf_op jit(solution)/shard_map/ppermute | solution.py:15
  1.1 0.1 collective-permute-start.1
  1.2 0.8 %prepare.1 = (f32[56,128]{1,0:T(8,128)S(1)}, f32[56,128]{1,0:T(8,128)S(1)}, s32[8,128]{1,0:T(8,128)S(1)}) custom-call(s32[4]{0:T(128)} %blocks_hbm.1, f32[20,128]{1,0:T(8,128)} %in_hbm.1, f32[32,128]{1,0:T(8,128)} %vec_hbm.1, f32[32,128]{1,0:T(8,128)} %probes_hbm.1), custom_call_target="tpu_custom_call" | custom-call | flops 100000000 | bytes 1000000 | tf_op jit(solution)/shard_map/prepare/pallas_call | solution.py:363
  2.0 3.0 %collective-permute-start.3 = (f32[56,128]{1,0:T(8,128)S(1)}, f32[56,128]{1,0:T(8,128)S(1)}, u32[]{:S(2)}, u32[]{:S(2)}) collective-permute-start(f32[56,128]{1,0:T(8,128)S(1)} %get-tuple-element.51), channel_id=1, source_target_pairs={{0,4},{1,5},{2,6},{3,7},{4,0},{5,1},{6,2},{7,3},{8,12},{9,13},{10,... | collective-permute-start | bytes 86024 | tf_op jit(solution)/shard_map/ppermute | solution.py:15
  5.0 0.0 collective-permute-done.far_in
  5.0 0.0 collective-permute-done.1.far_vec
  5.1 0.0 copy-start
  5.1 0.0 copy-start.1
  5.1 1.6 %collective-permute-start.2 = (f32[56,128]{1,0:T(8,128)S(1)}, f32[56,128]{1,0:T(8,128)S(1)}, u32[]{:S(2)}, u32[]{:S(2)}) collective-permute-start(f32[56,128]{1,0:T(8,128)S(1)} %pick.1), channel_id=1, source_target_pairs={{0,2},{1,3},{2,0},{3,1},{4,6},{5,7},{6,4},{7,5},{8,10},{9,11},{10,... | collective-permute-start | bytes 86024 | tf_op jit(solution)/shard_map/ppermute | solution.py:15
  6.7 0.0 copy-start.2
  6.7 0.0 copy-done
  6.7 0.0 copy-done.1
  6.7 0.7 %copy-done.2 = f32[256]{0:T(256)S(1)} copy-done((f32[256]{0:T(256)S(1)}, f32[256]{0:T(256)}, u32[]{:S(2)}) %copy-start.2) | copy-done | bytes 1048
  7.3 0.1 weights.1
  7.5 0.0 collective-permute-done.3
  7.5 1.5 %collective-permute-done.2 = f32[56,128]{1,0:T(8,128)S(1)} collective-permute-done((f32[56,128]{1,0:T(8,128)S(1)}, f32[56,128]{1,0:T(8,128)S(1)}, u32[]{:S(2)}, u32[]{:S(2)}) %collective-permute-start.2) | collective-permute-done | bytes 28704 | tf_op jit(solution)/shard_map/ppermute | solution.py:15
  9.0 0.1 collective-permute-start.4
  9.2 3.0 %collective-permute-start.7 = (f32[112,128]{1,0:T(8,128)S(1)}, f32[112,128]{1,0:T(8,128)S(1)}, u32[]{:S(2)}, u32[]{:S(2)}) collective-permute-start(f32[112,128]{1,0:T(8,128)S(1)} %pad_maximum_fusion), channel_id=1, source_target_pairs={{0,16},{8,24},{16,0},{24,8},{1,17},{9,25},{17,1},{25,9},{2,18},{10... | collective-permute-start | bytes 172040 | tf_op jit(solution)/shard_map/ppermute | solution.py:15
  12.1 0.8 %collective-permute-done.4 = f32[56,128]{1,0:T(8,128)S(1)} collective-permute-done((f32[56,128]{1,0:T(8,128)S(1)}, f32[56,128]{1,0:T(8,128)S(1)}, u32[]{:S(2)}, u32[]{:S(2)}) %collective-permute-start.4) | collective-permute-done | bytes 28704 | tf_op jit(solution)/shard_map/ppermute | solution.py:15
  12.9 2.6 %collective-permute-start.5 = (f32[56,128]{1,0:T(8,128)S(1)}, f32[56,128]{1,0:T(8,128)S(1)}, u32[]{:S(2)}, u32[]{:S(2)}) collective-permute-start(f32[56,128]{1,0:T(8,128)S(1)} %broadcast_select_fusion.1), channel_id=1, source_target_pairs={{0,16},{8,24},{16,0},{24,8},{1,17},{9,25},{17,1},{25,9},{2,18},{10... | collective-permute-start | bytes 86024 | tf_op jit(solution)/shard_map/ppermute | solution.py:15
  15.5 0.0 collective-permute-done.7
  15.5 1.6 %collective-permute-start.8 = (f32[224,128]{1,0:T(8,128)S(1)}, f32[224,128]{1,0:T(8,128)S(1)}, u32[]{:S(2)}, u32[]{:S(2)}) collective-permute-start(f32[224,128]{1,0:T(8,128)S(1)} %constant_dynamic-update-slice_fusion.columns_ref), channel_id=1, source_target_pairs={{0,8},{8,0},{16,24},{24,16},{1,9},{9,1},{17,25},{25,17},{2,10},{10... | collective-permute-start | bytes 344072 | tf_op jit(solution)/shard_map/ppermute | solution.py:15
  17.2 0.6 %collective-permute-done.5 = f32[56,128]{1,0:T(8,128)S(1)} collective-permute-done((f32[56,128]{1,0:T(8,128)S(1)}, f32[56,128]{1,0:T(8,128)S(1)}, u32[]{:S(2)}, u32[]{:S(2)}) %collective-permute-start.5) | collective-permute-done | bytes 28704 | tf_op jit(solution)/shard_map/ppermute | solution.py:15
  17.8 1.5 %collective-permute-start.6 = (f32[112,128]{1,0:T(8,128)S(1)}, f32[112,128]{1,0:T(8,128)S(1)}, u32[]{:S(2)}, u32[]{:S(2)}) collective-permute-start(f32[112,128]{1,0:T(8,128)S(1)} %pad_maximum_fusion.1.windows_ref), channel_id=1, source_target_pairs={{0,8},{8,0},{16,24},{24,16},{1,9},{9,1},{17,25},{25,17},{2,10},{10... | collective-permute-start | bytes 172040 | tf_op jit(solution)/shard_map/ppermute | solution.py:15
  19.3 1.2 %near.1 = (f32[24,256]{1,0:T(8,128)S(1)}, bf16[256,256]{1,0:T(8,128)(2,1)S(1)}, bf16[256,256]{1,0:T(8,128)(2,1)S(1)}, bf16[144,256]{1,0:T(8,128)(2,1)S(1)}, bf16...) custom-call(f32[112,128]{1,0:T(8,128)S(1)} %pad_maximum_fusion.1.win, ...), custom_call_target="tpu_custom_call" | custom-call | flops 1000000000 | bytes 1000000 | tf_op jit(solution)/shard_map/near/pallas_call | solution.py:363
  20.5 0.0 collective-permute-done.8.columns_ref
  20.5 1.6 %far.1 = (f32[24,512]{1,0:T(8,128)S(1)}, bf16[256,512]{1,0:T(8,128)(2,1)S(1)}, bf16[256,512]{1,0:T(8,128)(2,1)S(1)}, bf16[144,512]{1,0:T(8,128)(2,1)S(1)}, bf16[...) custom-call(f32[224,128]{1,0:T(8,128)S(1)} %collective-permute-done.8.columns_re, ...), custom_call_target="tpu_custom_call" | custom-call | flops 1000000000 | bytes 1000000 | tf_op jit(solution)/shard_map/far/pallas_call | solution.py:363
  22.1 0.0 collective-permute-done.6.windows_ref
  22.1 2.2 %late.1 = (f32[64,128]{1,0:T(8,128)S(1)}, f32[88,256]{1,0:T(8,128)S(1)}) custom-call(f32[112,128]{1,0:T(8,128)S(1)} %collective-permute-done.6.windows_ref, bf16[256,144]{1,0:T(8,128)(2,1)S(1)} %get-tuple-element.59.w_stack_ref, bf16[128,256]{1,0:T(8,128)(2,1)S(1)} %get-tuple-element.60.out_m_ref, bf16[256,256]{1,0:T(8,128)(2,1)S(1)} %get-tuple-element.61.out_k_ref, ...), custom_call_target="tpu_custom_call" | custom-call | flops 2000000000 | bytes 1000000 | tf_op jit(solution)/shard_map/late/pallas_call | solution.py:363
  24.3 1.6 %collective-permute-start.9 = (f32[88,256]{1,0:T(8,128)S(1)}, f32[88,256]{1,0:T(8,128)S(1)}, u32[]{:S(2)}, u32[]{:S(2)}) collective-permute-start(f32[88,256]{1,0:T(8,128)S(1)} %get-tuple-element.86), channel_id=1, source_target_pairs={{0,2},{1,3},{2,0},{3,1},{4,6},{5,7},{6,4},{7,5},{8,10},{9,11},{10,... | collective-permute-start | bytes 270344 | tf_op jit(solution)/shard_map/ppermute | solution.py:15
  25.8 3.0 %collective-permute-done.9 = f32[88,256]{1,0:T(8,128)S(1)} collective-permute-done((f32[88,256]{1,0:T(8,128)S(1)}, f32[88,256]{1,0:T(8,128)S(1)}, u32[]{:S(2)}, u32[]{:S(2)}) %collective-permute-start.9) | collective-permute-done | bytes 90144 | tf_op jit(solution)/shard_map/ppermute | solution.py:15
  28.9 0.1 collective-permute-start.10
  29.0 1.3 %collective-permute-done.10.theirs_ref = f32[88,256]{1,0:T(8,128)S(1)} collective-permute-done((f32[88,256]{1,0:T(8,128)S(1)}, f32[88,256]{1,0:T(8,128)S(1)}, u32[]{:S(2)}, u32[]{:S(2)}) %collective-permute-start.10) | collective-permute-done | bytes 90144 | tf_op jit(solution)/shard_map/ppermute | solution.py:15
  30.2 0.7 %finish.1 = (f32[64,128]{1,0:T(8,128)}, f32[20,256]{1,0:T(8,128)}, f32[1,256]{1,0:T(1,128)}, f32[64,256]{1,0:T(8,128)}) custom-call(f32[88,256]{1,0:T(8,128)S(1)} %add.3.mine_ref, f32[88,256]{1,0:T(8,128)S(1)} %collective-permute-done.10.theirs_ref, f32[64,128]{1,0:T(8,128)S(1)} %get-tuple-element.87.own_ref), custom_call_target="tpu_custom_call" | custom-call | flops 100000000 | bytes 1000000 | tf_op jit(solution)/shard_map/finish/pallas_call | solution.py:363
  (9 shorter events, 0.1 us)
Async XLA Ops:
  0.6 4.4 %collective-permute-start = (f32[20,128]{1,0:T(8,128)}, f32[20,128]{1,0:T(8,128)S(1)}, u32[]{:S(2)}, u32[]{:S(2)}) collective-permute-start(f32[20,128]{1,0:T(8,128)} %in_hbm.1), channel_id=1, source_target_pairs={{0,1},{1,0},{2,3},{3,2},{4,5},{5,4},{6,7},{7,6},{8,9},{9,8},{10,11... | collective-permute-start | bytes 30728 | tf_op jit(solution)/shard_map/ppermute | solution.py:15
  1.1 3.9 %collective-permute-start.1 = (f32[32,128]{1,0:T(8,128)}, f32[32,128]{1,0:T(8,128)S(1)}, u32[]{:S(2)}, u32[]{:S(2)}) collective-permute-start(f32[32,128]{1,0:T(8,128)} %vec_hbm.1), channel_id=1, source_target_pairs={{0,1},{1,0},{2,3},{3,2},{4,5},{5,4},{6,7},{7,6},{8,9},{9,8},{10,11... | collective-permute-start | bytes 49160 | tf_op jit(solution)/shard_map/ppermute | solution.py:15
  2.0 5.5 %collective-permute-start.3 = (f32[56,128]{1,0:T(8,128)S(1)}, f32[56,128]{1,0:T(8,128)S(1)}, u32[]{:S(2)}, u32[]{:S(2)}) collective-permute-start(f32[56,128]{1,0:T(8,128)S(1)} %get-tuple-element.51), channel_id=1, source_target_pairs={{0,4},{1,5},{2,6},{3,7},{4,0},{5,1},{6,2},{7,3},{8,12},{9,13},{10,... | collective-permute-start | bytes 86024 | tf_op jit(solution)/shard_map/ppermute | solution.py:15
  5.1 1.6 %copy-start = (f32[256,64]{0,1:T(8,128)S(1)}, f32[256,64]{0,1:T(8,128)}, u32[]{:S(2)}) copy-start(f32[256,64]{0,1:T(8,128)} %param.10) | copy-start | bytes 196612
  5.1 1.6 %copy-start.1 = (f32[20,256]{1,0:T(8,128)S(1)}, f32[20,256]{1,0:T(8,128)}, u32[]{:S(2)}) copy-start(f32[20,256]{1,0:T(8,128)} %param.8) | copy-start | bytes 61444
  5.1 3.9 %collective-permute-start.2 = (f32[56,128]{1,0:T(8,128)S(1)}, f32[56,128]{1,0:T(8,128)S(1)}, u32[]{:S(2)}, u32[]{:S(2)}) collective-permute-start(f32[56,128]{1,0:T(8,128)S(1)} %pick.1), channel_id=1, source_target_pairs={{0,2},{1,3},{2,0},{3,1},{4,6},{5,7},{6,4},{7,5},{8,10},{9,11},{10,... | collective-permute-start | bytes 86024 | tf_op jit(solution)/shard_map/ppermute | solution.py:15
  6.7 0.7 %copy-start.2 = (f32[256]{0:T(256)S(1)}, f32[256]{0:T(256)}, u32[]{:S(2)}) copy-start(f32[256]{0:T(256)} %param.9) | copy-start | bytes 3076
  9.0 3.9 %collective-permute-start.4 = (f32[56,128]{1,0:T(8,128)S(1)}, f32[56,128]{1,0:T(8,128)S(1)}, u32[]{:S(2)}, u32[]{:S(2)}) collective-permute-start(f32[56,128]{1,0:T(8,128)S(1)} %broadcast_select_fusion), channel_id=1, source_target_pairs={{0,4},{1,5},{2,6},{3,7},{4,0},{5,1},{6,2},{7,3},{8,12},{9,13},{10,... | collective-permute-start | bytes 86024 | tf_op jit(solution)/shard_map/ppermute | solution.py:15
  9.2 6.3 %collective-permute-start.7 = (f32[112,128]{1,0:T(8,128)S(1)}, f32[112,128]{1,0:T(8,128)S(1)}, u32[]{:S(2)}, u32[]{:S(2)}) collective-permute-start(f32[112,128]{1,0:T(8,128)S(1)} %pad_maximum_fusion), channel_id=1, source_target_pairs={{0,16},{8,24},{16,0},{24,8},{1,17},{9,25},{17,1},{25,9},{2,18},{10... | collective-permute-start | bytes 172040 | tf_op jit(solution)/shard_map/ppermute | solution.py:15
  12.9 4.9 %collective-permute-start.5 = (f32[56,128]{1,0:T(8,128)S(1)}, f32[56,128]{1,0:T(8,128)S(1)}, u32[]{:S(2)}, u32[]{:S(2)}) collective-permute-start(f32[56,128]{1,0:T(8,128)S(1)} %broadcast_select_fusion.1), channel_id=1, source_target_pairs={{0,16},{8,24},{16,0},{24,8},{1,17},{9,25},{17,1},{25,9},{2,18},{10... | collective-permute-start | bytes 86024 | tf_op jit(solution)/shard_map/ppermute | solution.py:15
  15.5 5.0 %collective-permute-start.8 = (f32[224,128]{1,0:T(8,128)S(1)}, f32[224,128]{1,0:T(8,128)S(1)}, u32[]{:S(2)}, u32[]{:S(2)}) collective-permute-start(f32[224,128]{1,0:T(8,128)S(1)} %constant_dynamic-update-slice_fusion.columns_ref), channel_id=1, source_target_pairs={{0,8},{8,0},{16,24},{24,16},{1,9},{9,1},{17,25},{25,17},{2,10},{10... | collective-permute-start | bytes 344072 | tf_op jit(solution)/shard_map/ppermute | solution.py:15
  17.8 4.3 %collective-permute-start.6 = (f32[112,128]{1,0:T(8,128)S(1)}, f32[112,128]{1,0:T(8,128)S(1)}, u32[]{:S(2)}, u32[]{:S(2)}) collective-permute-start(f32[112,128]{1,0:T(8,128)S(1)} %pad_maximum_fusion.1.windows_ref), channel_id=1, source_target_pairs={{0,8},{8,0},{16,24},{24,16},{1,9},{9,1},{17,25},{25,17},{2,10},{10... | collective-permute-start | bytes 172040 | tf_op jit(solution)/shard_map/ppermute | solution.py:15
  24.3 4.6 %collective-permute-start.9 = (f32[88,256]{1,0:T(8,128)S(1)}, f32[88,256]{1,0:T(8,128)S(1)}, u32[]{:S(2)}, u32[]{:S(2)}) collective-permute-start(f32[88,256]{1,0:T(8,128)S(1)} %get-tuple-element.86), channel_id=1, source_target_pairs={{0,2},{1,3},{2,0},{3,1},{4,6},{5,7},{6,4},{7,5},{8,10},{9,11},{10,... | collective-permute-start | bytes 270344 | tf_op jit(solution)/shard_map/ppermute | solution.py:15
  28.9 1.4 %collective-permute-start.10 = (f32[88,256]{1,0:T(8,128)S(1)}, f32[88,256]{1,0:T(8,128)S(1)}, u32[]{:S(2)}, u32[]{:S(2)}) collective-permute-start(f32[88,256]{1,0:T(8,128)S(1)} %add.3.mine_ref), channel_id=1, source_target_pairs={{0,1},{1,0},{2,3},{3,2},{4,5},{5,4},{6,7},{7,6},{8,9},{9,8},{10,11... | collective-permute-start | bytes 270344 | tf_op jit(solution)/shard_map/ppermute | solution.py:15

commit v5 on v4

--- a/solution.py
+++ b/solution.py
@@ -74,8 +74,8 @@
         self.cols = n_row * own
         self.rows = 2 * feats + 16
         self.win_step = min(256, self.wide)
-        self.win_piece = min(256, self.win_step)
         self.col_step = min(512, self.cols)
+        self.early_step = min(256, self.cols)
 
     def network(self, lanes):
         return dict(
@@ -165,7 +165,7 @@
     return into, middle, out
 
 
-def window_features(z, blocks_ref, s, w_stack, out_m):
+def window_features(z, blocks_ref, s, w_stack, out_m, others=()):
     own, part, step = z.own, z.part, z.win_step
     for r in range(z.wide // own):
         here = pl.ds(r * own, own)
@@ -173,18 +173,16 @@
         v1, v2 = split(blocks_ref[r * part + z.ins : (r + 1) * part])
         s.vec[here, :] = stack([v1, v2, v1, v2]).T
     into, middle, out = network(z, s, w_stack, out_m)
-
-    def one(i):
-        rows = [pl.ds(i * step + k * z.win_piece, z.win_piece) for k in range(step // z.win_piece)]
-
-        def last(k, raw):
-            norm = out(rows[k], raw)
-            s.key[rows[k], :] = jnp.concatenate([s.m[: 2 * z.feats, rows[k]]] * 2, 0).T
-            s.norm[rows[k], :] = jnp.broadcast_to(norm, (own, z.win_piece)).T
-
-        flow(len(rows), lambda k, _: into(rows[k]), lambda k, pre: middle(rows[k], pre), last)
-
-    each(z.wide // step, one)
+    for i in range(z.wide // step):
+        rows = pl.ds(i * step, step)
+        value = into(rows)
+        other = others[i][0]() if others else None
+        value = middle(rows, value)
+        if others:
+            others[i][1](other)
+        norm = out(rows, value)
+        s.key[rows, :] = jnp.concatenate([s.m[: 2 * z.feats, rows]] * 2, 0).T
+        s.norm[rows, :] = jnp.broadcast_to(norm, (own, step)).T
     s.sums[...] = jnp.zeros(s.sums.shape, F32)
 
 
@@ -200,7 +198,7 @@
     return jnp.concatenate(parts, 1)
 
 
-def tile(z, win, col):
+def tile(z, win, col, width):
     feats, step = z.feats, z.win_step
     single = z.wide == step
 
@@ -211,7 +209,7 @@
         return cross, mm(win.vec[rows, :], col.vec[:, lanes])
 
     def weighed(lanes, rows, dots):
-        far = beside([win.norm[rows, :]] * (z.col_step // z.own))
+        far = beside([win.norm[rows, :]] * (width // z.own))
         weigh = jnp.exp(dots[0] - far - col.norm[:1, lanes]) * dots[1]
         g1 = weigh.astype(BF)
         g2 = (weigh - g1.astype(F32)).astype(BF)
@@ -232,7 +230,7 @@
             rows = pl.ds(k * step, step)
             return sums + weighed(lanes, rows, products(lanes, rows))
 
-        return lax.fori_loop(0, z.wide // step, add, jnp.zeros((z.rows, z.col_step), F32))
+        return lax.fori_loop(0, z.wide // step, add, jnp.zeros((z.rows, width), F32))
 
     return first, second
 
@@ -268,28 +266,18 @@
     return total_of(z, s.m[:, rows], s.sums[rows, :].T)
 
 
-def window_backprop(z, s, out_k, pack_ref):
-    first, second = backprop(z, s, out_k, pack_ref)
-
-    def one(i):
-        rows = pl.ds(i * z.win_step, z.win_step)
-        second(rows, first(rows, window_total(z, s, rows)))
-
-    each(z.wide // z.win_step, one)
-
-
-def column_steps(z):
-    return [pl.ds(k * z.col_step, z.col_step) for k in range(z.cols // z.col_step)]
+def column_steps(z, step):
+    return [pl.ds(k * step, step) for k in range(z.cols // step)]
 
 
 def column_features(z, blocks_ref, col, win, w_stack, out_m):
     column_blocks(z, blocks_ref, col)
     into, middle, out = network(z, col, w_stack, out_m)
-    first, second = tile(z, win, col)
-    lanes = column_steps(z)
+    first, second = tile(z, win, col, z.early_step)
+    lanes = column_steps(z, z.early_step)
 
     def third(k, raw):
-        col.norm[:, lanes[k]] = jnp.broadcast_to(out(lanes[k], raw), (8, z.col_step))
+        col.norm[:, lanes[k]] = jnp.broadcast_to(out(lanes[k], raw), (8, z.early_step))
         return first(lanes[k])
 
     def fourth(k, dots):
@@ -306,41 +294,46 @@
     column_features(z, columns_ref, col, win, w_stack, out_m)
 
 
-def far_kernel(z, columns_ref, w_stack_ref, out_m_ref, out_k_ref, *refs):
+def far_kernel(z, columns_ref, w_stack_ref, out_m_ref, *refs):
     n, c = len(z.windows()), len(z.columns())
     win, col = Refs(z.windows(), refs[:n]), Refs(z.columns(), refs[n : n + c])
-    pack_ref, sums_ref = refs[n + c :]
+    sums_ref = refs[n + c]
     sums_ref[...] = win.sums[...]
     win.sums = sums_ref
     column_features(z, columns_ref, col, win, w_stack_ref[...], out_m_ref[...])
+
+
+def late_kernel(z, windows_ref, w_stack_ref, out_m_ref, out_k_ref, *refs):
+    w, c = len(z.windows()), len(z.columns())
+    near = Refs(z.windows(), refs[:w])
+    cols = [Refs(z.columns(), refs[w : w + c]), Refs(z.columns(), refs[w + c : w + 2 * c])]
+    near.sums, col_grad_ref, pack_ref = refs[w + 2 * c : w + 2 * c + 3]
+    win = Refs(z.windows(), refs[w + 2 * c + 3 :])
+    out_k = out_k_ref[...]
     pack_ref[...] = jnp.zeros(pack_ref.shape, F32)
-    window_backprop(z, win, out_k_ref[...], pack_ref)
-
-
-def late_kernel(z, windows_ref, w_stack_ref, out_m_ref, out_k_ref, *refs):
-    c = len(z.columns())
-    cols = [Refs(z.columns(), refs[:c]), Refs(z.columns(), refs[c : 2 * c])]
-    early_pack_ref, col_grad_ref, pack_ref = refs[2 * c : 2 * c + 3]
-    win = Refs(z.windows(), refs[2 * c + 3 :])
-    pack_ref[...] = early_pack_ref[...]
-    window_features(z, windows_ref, win, w_stack_ref[...], out_m_ref[...])
-    out_k = out_k_ref[...]
-    work = [(col, lanes) for col in cols for lanes in column_steps(z)]
+    rows = [pl.ds(i * z.win_step, z.win_step) for i in range(z.wide // z.win_step)]
+
+    def backward(work, totals):
+        stages = [backprop(z, s, out_k, pack_ref) for s, _ in work]
+        first = [lambda k=k: stages[k][0](work[k][1], totals[k]()) for k in range(len(work))]
+        second = [lambda g, k=k: stages[k][1](work[k][1], g) for k in range(len(work))]
+        return first, second
+
+    first, second = backward([(near, r) for r in rows], [functools.partial(window_total, z, near, r) for r in rows])
+    window_features(z, windows_ref, win, w_stack_ref[...], out_m_ref[...], list(zip(first, second)))
+    work = [(col, lanes) for col in cols for lanes in column_steps(z, z.col_step)]
     totals = []
 
     def total(k, dots):
         col, lanes = work[k]
-        sums = col.sums[:, lanes] + tile(z, win, col)[1](lanes, dots)
+        sums = col.sums[:, lanes] + tile(z, win, col, z.col_step)[1](lanes, dots)
         totals.append(total_of(z, col.m[:, lanes], sums))
 
-    flow(len(work), lambda k, _: tile(z, win, work[k][0])[0](work[k][1]), total)
+    flow(len(work), lambda k, _: tile(z, win, work[k][0], z.col_step)[0](work[k][1]), total)
     col_grad_ref[...] = totals[0][:, : z.own]
-    for i in range(z.wide // z.win_step):
-        rows = pl.ds(i * z.win_step, z.win_step)
-        work.append((win, rows))
-        totals.append(window_total(z, win, rows))
-    stages = [backprop(z, s, out_k, pack_ref) for s, _ in work]
-    flow(len(work), lambda k, _: stages[k][0](work[k][1], totals[k]), lambda k, g: stages[k][1](work[k][1], g))
+    totals = [lambda t=t: t for t in totals] + [functools.partial(window_total, z, win, r) for r in rows]
+    first, second = backward(work + [(win, r) for r in rows], totals)
+    flow(len(first), lambda k, _: first[k](), lambda k, g: second[k](g))
 
 
 def finish_kernel(z, mine_ref, theirs_ref, own_ref, col_grad_ref, grad_in_ref, grad_bias_ref, grad_out_ref):
@@ -376,7 +369,8 @@
     depth, own = protocols.shape
     z = Sizes(depth, solved.shape[0], w_out.shape[0], w_out.shape[1], own, n_row)
     bits = bits_of(n_col)
-    shared, joined = bits[:-1], bits[-1]
+    joined = bits[1]
+    shared = [bit for bit in bits if bit != joined]
     limit = 12 if n_row <= 4 else 48
     f32 = functools.partial(jax.ShapeDtypeStruct, dtype=F32)
 
@@ -406,19 +400,19 @@
         ),
         (w_in[None], b_in.reshape(1, -1), w_out.T),
     )
-    for bit in shared[1:]:
-        window = nearer(bit, window, swap(window, "col", n_col, bit))
-    columns = jnp.concatenate([columns, swap(columns, "col", n_col, joined)])
-    window, columns, w_stack, out_m, out_k = lax.optimization_barrier((window, columns, w_stack, out_m, out_k))
+    got = swap(jnp.concatenate([window, columns]), "col", n_col, joined)
+    window = nearer(joined, window, got[: z.part])
+    columns = jnp.concatenate([columns, got[z.part :]])
+    window, w_stack, out_m, out_k = lax.optimization_barrier((window, w_stack, out_m, out_k))
     for bit in reversed(bits_of(n_row)[1:]):
         columns = jnp.concatenate([columns, swap(columns, "row", n_row, bit)])
     far_columns = swap(columns, "row", n_row, 1)
-    window = nearer(joined, window, swap(window, "col", n_col, joined))
+    for bit in shared[1:]:
+        window = nearer(bit, window, swap(window, "col", n_col, bit))
     for bit in reversed(bits_of(n_row)[1:]):
         window = jnp.concatenate([window, swap(window, "row", n_row, bit)])
     far_window = swap(window, "row", n_row, 1)
 
-    pack_shape = f32((z.feats + z.ins, z.hid))
     near = call(
         functools.partial(near_kernel, z),
         "near",
@@ -428,20 +422,19 @@
         cost=10,
     )
     windows, near = near[: len(z.windows())], near[len(z.windows()) :]
-    *far, early_pack = call(
+    *far, sums = call(
         functools.partial(far_kernel, z),
         "far",
-        (*shapes(z.columns()), pack_shape),
-        (far_columns, w_stack, out_m, out_k, *windows),
-        [VMEM(*z.windows()["sums"])],
+        (*shapes(z.columns()), jax.ShapeDtypeStruct(*z.windows()["sums"])),
+        (far_columns, w_stack, out_m, *windows),
         limit=limit,
         cost=10,
     )
     col_grad, pack = call(
         functools.partial(late_kernel, z),
         "late",
-        (f32((z.feats, own)), pack_shape),
-        (far_window, w_stack, out_m, out_k, *near, *far, early_pack),
+        (f32((z.feats, own)), f32((z.feats + z.ins, z.hid))),
+        (far_window, w_stack, out_m, out_k, *windows, *near, *far, sums),
         [VMEM(*v) for v in z.windows().values()],
         limit=limit,
         cost=20,

time: 31.2 us -> 30.3 us (0.971)
  starting transfers between devices: 15.6 us -> 14.9 us
  Pallas kernels: 6.55 us -> 6.03 us
  waiting for transfers between devices: 7.27 us -> 7.62 us
    ppermute x11 -> x10, starting transfers between devices: 15.6 us -> 14.9 us  [swap(): return lax.ppermute(value, axis, [(i, i ^ bit) for i in range(size)])]
    pallas_call x7, Pallas kernels: 6.55 us -> 6.03 us  [call(): pl.pallas_call(kernel, out_shape=tuple(outs), in_specs=[pl.BlockSpec(memo...]
    ppermute x11 -> x10, waiting for transfers between devices: 7.27 us -> 7.62 us  [swap(): return lax.ppermute(value, axis, [(i, i ^ bit) for i in range(size)])]
    unnamed x7 -> x6, local copies, waits for them, and re-layouts: 0.69 us -> 0.68 us
  transfers between devices with their start and end apart: 11 -> 10, of which waited for: 5 -> 7; matrix products, arithmetic and copies ran while one was open for 0% -> 0% of each run, Pallas kernels for 12% -> 10%
where the time goes in v5:
time: 30.3 us; the launch traced here: 30 us
  starting transfers between devices  14.9 us (49%)
  waiting for transfers between devices  7.62 us (25%)
  Pallas kernels  6.03 us (20%)
  between operations  0.73 us (2%)
  local copies, waits for them, and re-layouts  0.68 us (2%)
    ppermute x10, starting transfers between devices, swap(): return lax.ppermute(value, axis, [(i, i ^ bit) for i in range(size)])  14.9 us
    ppermute x10, waiting for transfers between devices, swap(): return lax.ppermute(value, axis, [(i, i ^ bit) for i in range(size)])  7.62 us
    pallas_call x7, Pallas kernels, call(): pl.pallas_call(kernel, out_shape=tuple(outs), in_specs=[pl.BlockSpec(memo...  6.03 us
    unnamed x6, local copies, waits for them, and re-layouts  0.68 us
  transfers between devices with their start and end apart: 10, of which 7 were waited for; matrix products, arithmetic and copies ran while one was open for 0% of the time, Pallas kernels for 10%

profile of v5, /device:TPU:0, one launch (start us, length us, event | category | flops | bytes accessed | tf_op | source)
XLA Modules:
  0.0 30.0 jit_solution(15610765903097869380)
XLA Ops:
  0.6 0.5 %collective-permute-start.1 = (f32[32,128]{1,0:T(8,128)}, f32[32,128]{1,0:T(8,128)S(1)}, u32[]{:S(2)}, u32[]{:S(2)}) collective-permute-start(f32[32,128]{1,0:T(8,128)} %vec_hbm.1), channel_id=1, source_target_pairs={{0,1},{1,0},{2,3},{3,2},{4,5},{5,4},{6,7},{7,6},{8,9},{9,8},{10,11... | collective-permute-start | bytes 49160 | tf_op jit(solution)/shard_map/ppermute | solution.py:15
  1.1 0.1 collective-permute-start
  1.2 0.8 %prepare.1 = (f32[56,128]{1,0:T(8,128)S(1)}, f32[56,128]{1,0:T(8,128)S(1)}, s32[8,128]{1,0:T(8,128)S(1)}) custom-call(s32[4]{0:T(128)} %blocks_hbm.1, f32[20,128]{1,0:T(8,128)} %in_hbm.1, f32[32,128]{1,0:T(8,128)} %vec_hbm.1, f32[32,128]{1,0:T(8,128)} %probes_hbm.1), custom_call_target="tpu_custom_call" | custom-call | flops 100000000 | bytes 1000000 | tf_op jit(solution)/shard_map/prepare/pallas_call | solution.py:356
  2.0 0.5 %collective-permute-done.far_in = f32[20,128]{1,0:T(8,128)S(1)} collective-permute-done((f32[20,128]{1,0:T(8,128)}, f32[20,128]{1,0:T(8,128)S(1)}, u32[]{:S(2)}, u32[]{:S(2)}) %collective-permute-start) | collective-permute-done | bytes 10272 | tf_op jit(solution)/shard_map/ppermute | solution.py:15
  2.5 0.0 collective-permute-done.1.far_vec
  2.6 0.0 copy-start
  2.6 0.0 copy-start.1
  2.6 2.7 %collective-permute-start.2 = (f32[112,128]{1,0:T(8,128)S(1)}, f32[112,128]{1,0:T(8,128)S(1)}, u32[]{:S(2)}, u32[]{:S(2)}) collective-permute-start(f32[112,128]{1,0:T(8,128)S(1)} %pad_maximum_fusion.1), channel_id=1, source_target_pairs={{0,2},{1,3},{2,0},{3,1},{4,6},{5,7},{6,4},{7,5},{8,10},{9,11},{10,... | collective-permute-start | bytes 172040 | tf_op jit(solution)/shard_map/ppermute | solution.py:15
  5.3 0.0 copy-start.2
  5.3 0.0 copy-done
  5.3 0.0 copy-done.1
  5.3 0.7 %copy-done.2 = f32[256]{0:T(256)S(1)} copy-done((f32[256]{0:T(256)S(1)}, f32[256]{0:T(256)}, u32[]{:S(2)}) %copy-start.2) | copy-done | bytes 1048
  6.0 0.1 weights.1
  6.1 1.6 %collective-permute-done.2 = f32[112,128]{1,0:T(8,128)S(1)} collective-permute-done((f32[112,128]{1,0:T(8,128)S(1)}, f32[112,128]{1,0:T(8,128)S(1)}, u32[]{:S(2)}, u32[]{:S(2)}) %collective-permute-start.2) | collective-permute-done | bytes 57376 | tf_op jit(solution)/shard_map/ppermute | solution.py:15
  7.7 1.8 %collective-permute-start.3 = (f32[56,128]{1,0:T(8,128)S(1)}, f32[56,128]{1,0:T(8,128)S(1)}, u32[]{:S(2)}, u32[]{:S(2)}) collective-permute-start(f32[56,128]{1,0:T(8,128)S(1)} %get-tuple-element.57), channel_id=1, source_target_pairs={{0,4},{1,5},{2,6},{3,7},{4,0},{5,1},{6,2},{7,3},{8,12},{9,13},{10,... | collective-permute-start | bytes 86024 | tf_op jit(solution)/shard_map/ppermute | solution.py:15
  9.5 2.6 %collective-permute-start.6 = (f32[112,128]{1,0:T(8,128)S(1)}, f32[112,128]{1,0:T(8,128)S(1)}, u32[]{:S(2)}, u32[]{:S(2)}) collective-permute-start(f32[112,128]{1,0:T(8,128)S(1)} %pad_maximum_fusion.3), channel_id=1, source_target_pairs={{0,16},{8,24},{16,0},{24,8},{1,17},{9,25},{17,1},{25,9},{2,18},{10... | collective-permute-start | bytes 172040 | tf_op jit(solution)/shard_map/ppermute | solution.py:15
  12.1 0.0 collective-permute-done.3
  12.1 2.3 %collective-permute-start.4 = (f32[56,128]{1,0:T(8,128)S(1)}, f32[56,128]{1,0:T(8,128)S(1)}, u32[]{:S(2)}, u32[]{:S(2)}) collective-permute-start(f32[56,128]{1,0:T(8,128)S(1)} %broadcast_select_fusion), channel_id=1, source_target_pairs={{0,16},{8,24},{16,0},{24,8},{1,17},{9,25},{17,1},{25,9},{2,18},{10... | collective-permute-start | bytes 86024 | tf_op jit(solution)/shard_map/ppermute | solution.py:15
  14.5 0.4 %collective-permute-done.6 = f32[112,128]{1,0:T(8,128)S(1)} collective-permute-done((f32[112,128]{1,0:T(8,128)S(1)}, f32[112,128]{1,0:T(8,128)S(1)}, u32[]{:S(2)}, u32[]{:S(2)}) %collective-permute-start.6) | collective-permute-done | bytes 57376 | tf_op jit(solution)/shard_map/ppermute | solution.py:15
  14.9 1.6 %collective-permute-start.7 = (f32[224,128]{1,0:T(8,128)S(1)}, f32[224,128]{1,0:T(8,128)S(1)}, u32[]{:S(2)}, u32[]{:S(2)}) collective-permute-start(f32[224,128]{1,0:T(8,128)S(1)} %pad_maximum_fusion.columns_ref), channel_id=1, source_target_pairs={{0,8},{8,0},{16,24},{24,16},{1,9},{9,1},{17,25},{25,17},{2,10},{10... | collective-permute-start | bytes 344072 | tf_op jit(solution)/shard_map/ppermute | solution.py:15
  16.5 0.4 %collective-permute-done.4 = f32[56,128]{1,0:T(8,128)S(1)} collective-permute-done((f32[56,128]{1,0:T(8,128)S(1)}, f32[56,128]{1,0:T(8,128)S(1)}, u32[]{:S(2)}, u32[]{:S(2)}) %collective-permute-start.4) | collective-permute-done | bytes 28704 | tf_op jit(solution)/shard_map/ppermute | solution.py:15
  17.0 1.9 %collective-permute-start.5 = (f32[112,128]{1,0:T(8,128)S(1)}, f32[112,128]{1,0:T(8,128)S(1)}, u32[]{:S(2)}, u32[]{:S(2)}) collective-permute-start(f32[112,128]{1,0:T(8,128)S(1)} %pad_maximum_fusion.2.windows_ref), channel_id=1, source_target_pairs={{0,8},{8,0},{16,24},{24,16},{1,9},{9,1},{17,25},{25,17},{2,10},{10... | collective-permute-start | bytes 172040 | tf_op jit(solution)/shard_map/ppermute | solution.py:15
  18.9 1.1 %near.1 = (f32[24,256]{1,0:T(8,128)S(1)}, bf16[256,256]{1,0:T(8,128)(2,1)S(1)}, bf16[256,256]{1,0:T(8,128)(2,1)S(1)}, bf16[144,256]{1,0:T(8,128)(2,1)S(1)}, bf16...) custom-call(f32[112,128]{1,0:T(8,128)S(1)} %pad_maximum_fusion.2.win, ...), custom_call_target="tpu_custom_call" | custom-call | flops 1000000000 | bytes 1000000 | tf_op jit(solution)/shard_map/near/pallas_call | solution.py:356
  20.0 0.0 collective-permute-done.7.columns_ref
  20.0 1.0 %far.1 = (f32[24,512]{1,0:T(8,128)S(1)}, bf16[256,512]{1,0:T(8,128)(2,1)S(1)}, bf16[256,512]{1,0:T(8,128)(2,1)S(1)}, bf16[144,512]{1,0:T(8,128)(2,1)S(1)}, bf16[...) custom-call(f32[224,128]{1,0:T(8,128)S(1)} %collective-permute-done.7.columns_r, ...), custom_call_target="tpu_custom_call" | custom-call | flops 1000000000 | bytes 1000000 | tf_op jit(solution)/shard_map/far/pallas_call | solution.py:356
  21.1 0.1 collective-permute-done.5.windows_ref
  21.1 2.3 %late.1 = (f32[64,128]{1,0:T(8,128)S(1)}, f32[88,256]{1,0:T(8,128)S(1)}) custom-call(f32[112,128]{1,0:T(8,128)S(1)} %collective-permute-done.5.windows_ref, bf16[256,144]{1,0:T(8,128)(2,1)S(1)} %get-tuple-element.58.w_stack_ref, bf16[128,256]{1,0:T(8,128)(2,1)S(1)} %get-tuple-element.59.out_m_ref, bf16[256,256]{1,0:T(8,128)(2,1)S(1)} %get-tuple-element.60.out_k_ref, ...), custom_call_target="tpu_custom_call" | custom-call | flops 2000000000 | bytes 1000000 | tf_op jit(solution)/shard_map/late/pallas_call | solution.py:356
  23.4 1.3 %collective-permute-start.8 = (f32[88,256]{1,0:T(8,128)S(1)}, f32[88,256]{1,0:T(8,128)S(1)}, u32[]{:S(2)}, u32[]{:S(2)}) collective-permute-start(f32[88,256]{1,0:T(8,128)S(1)} %get-tuple-element.84), channel_id=1, source_target_pairs={{0,4},{1,5},{2,6},{3,7},{4,0},{5,1},{6,2},{7,3},{8,12},{9,13},{10,... | collective-permute-start | bytes 270344 | tf_op jit(solution)/shard_map/ppermute | solution.py:15
  24.7 3.3 %collective-permute-done.8 = f32[88,256]{1,0:T(8,128)S(1)} collective-permute-done((f32[88,256]{1,0:T(8,128)S(1)}, f32[88,256]{1,0:T(8,128)S(1)}, u32[]{:S(2)}, u32[]{:S(2)}) %collective-permute-start.8) | collective-permute-done | bytes 90144 | tf_op jit(solution)/shard_map/ppermute | solution.py:15
  28.0 0.1 collective-permute-start.9
  28.1 1.3 %collective-permute-done.9.theirs_ref = f32[88,256]{1,0:T(8,128)S(1)} collective-permute-done((f32[88,256]{1,0:T(8,128)S(1)}, f32[88,256]{1,0:T(8,128)S(1)}, u32[]{:S(2)}, u32[]{:S(2)}) %collective-permute-start.9) | collective-permute-done | bytes 90144 | tf_op jit(solution)/shard_map/ppermute | solution.py:15
  29.4 0.7 %finish.1 = (f32[64,128]{1,0:T(8,128)}, f32[20,256]{1,0:T(8,128)}, f32[1,256]{1,0:T(1,128)}, f32[64,256]{1,0:T(8,128)}) custom-call(f32[88,256]{1,0:T(8,128)S(1)} %add.3.mine_ref, f32[88,256]{1,0:T(8,128)S(1)} %collective-permute-done.9.theirs_ref, f32[64,128]{1,0:T(8,128)S(1)} %get-tuple-element.85.own_ref), custom_call_target="tpu_custom_call" | custom-call | flops 100000000 | bytes 1000000 | tf_op jit(solution)/shard_map/finish/pallas_call | solution.py:356
  (9 shorter events, 0.1 us)
Async XLA Ops:
  0.6 1.9 %collective-permute-start.1 = (f32[32,128]{1,0:T(8,128)}, f32[32,128]{1,0:T(8,128)S(1)}, u32[]{:S(2)}, u32[]{:S(2)}) collective-permute-start(f32[32,128]{1,0:T(8,128)} %vec_hbm.1), channel_id=1, source_target_pairs={{0,1},{1,0},{2,3},{3,2},{4,5},{5,4},{6,7},{7,6},{8,9},{9,8},{10,11... | collective-permute-start | bytes 49160 | tf_op jit(solution)/shard_map/ppermute | solution.py:15
  1.1 1.4 %collective-permute-start = (f32[20,128]{1,0:T(8,128)}, f32[20,128]{1,0:T(8,128)S(1)}, u32[]{:S(2)}, u32[]{:S(2)}) collective-permute-start(f32[20,128]{1,0:T(8,128)} %in_hbm.1), channel_id=1, source_target_pairs={{0,1},{1,0},{2,3},{3,2},{4,5},{5,4},{6,7},{7,6},{8,9},{9,8},{10,11... | collective-permute-start | bytes 30728 | tf_op jit(solution)/shard_map/ppermute | solution.py:15
  2.6 2.8 %copy-start = (f32[256,64]{0,1:T(8,128)S(1)}, f32[256,64]{0,1:T(8,128)}, u32[]{:S(2)}) copy-start(f32[256,64]{0,1:T(8,128)} %param.10) | copy-start | bytes 196612
  2.6 2.8 %copy-start.1 = (f32[20,256]{1,0:T(8,128)S(1)}, f32[20,256]{1,0:T(8,128)}, u32[]{:S(2)}) copy-start(f32[20,256]{1,0:T(8,128)} %param.8) | copy-start | bytes 61444
  2.6 5.1 %collective-permute-start.2 = (f32[112,128]{1,0:T(8,128)S(1)}, f32[112,128]{1,0:T(8,128)S(1)}, u32[]{:S(2)}, u32[]{:S(2)}) collective-permute-start(f32[112,128]{1,0:T(8,128)S(1)} %pad_maximum_fusion.1), channel_id=1, source_target_pairs={{0,2},{1,3},{2,0},{3,1},{4,6},{5,7},{6,4},{7,5},{8,10},{9,11},{10,... | collective-permute-start | bytes 172040 | tf_op jit(solution)/shard_map/ppermute | solution.py:15
  5.3 0.7 %copy-start.2 = (f32[256]{0:T(256)S(1)}, f32[256]{0:T(256)}, u32[]{:S(2)}) copy-start(f32[256]{0:T(256)} %param.9) | copy-start | bytes 3076
  7.7 4.4 %collective-permute-start.3 = (f32[56,128]{1,0:T(8,128)S(1)}, f32[56,128]{1,0:T(8,128)S(1)}, u32[]{:S(2)}, u32[]{:S(2)}) collective-permute-start(f32[56,128]{1,0:T(8,128)S(1)} %get-tuple-element.57), channel_id=1, source_target_pairs={{0,4},{1,5},{2,6},{3,7},{4,0},{5,1},{6,2},{7,3},{8,12},{9,13},{10,... | collective-permute-start | bytes 86024 | tf_op jit(solution)/shard_map/ppermute | solution.py:15
  9.5 5.4 %collective-permute-start.6 = (f32[112,128]{1,0:T(8,128)S(1)}, f32[112,128]{1,0:T(8,128)S(1)}, u32[]{:S(2)}, u32[]{:S(2)}) collective-permute-start(f32[112,128]{1,0:T(8,128)S(1)} %pad_maximum_fusion.3), channel_id=1, source_target_pairs={{0,16},{8,24},{16,0},{24,8},{1,17},{9,25},{17,1},{25,9},{2,18},{10... | collective-permute-start | bytes 172040 | tf_op jit(solution)/shard_map/ppermute | solution.py:15
  12.1 4.8 %collective-permute-start.4 = (f32[56,128]{1,0:T(8,128)S(1)}, f32[56,128]{1,0:T(8,128)S(1)}, u32[]{:S(2)}, u32[]{:S(2)}) collective-permute-start(f32[56,128]{1,0:T(8,128)S(1)} %broadcast_select_fusion), channel_id=1, source_target_pairs={{0,16},{8,24},{16,0},{24,8},{1,17},{9,25},{17,1},{25,9},{2,18},{10... | collective-permute-start | bytes 86024 | tf_op jit(solution)/shard_map/ppermute | solution.py:15
  14.9 5.1 %collective-permute-start.7 = (f32[224,128]{1,0:T(8,128)S(1)}, f32[224,128]{1,0:T(8,128)S(1)}, u32[]{:S(2)}, u32[]{:S(2)}) collective-permute-start(f32[224,128]{1,0:T(8,128)S(1)} %pad_maximum_fusion.columns_ref), channel_id=1, source_target_pairs={{0,8},{8,0},{16,24},{24,16},{1,9},{9,1},{17,25},{25,17},{2,10},{10... | collective-permute-start | bytes 344072 | tf_op jit(solution)/shard_map/ppermute | solution.py:15
  17.0 4.2 %collective-permute-start.5 = (f32[112,128]{1,0:T(8,128)S(1)}, f32[112,128]{1,0:T(8,128)S(1)}, u32[]{:S(2)}, u32[]{:S(2)}) collective-permute-start(f32[112,128]{1,0:T(8,128)S(1)} %pad_maximum_fusion.2.windows_ref), channel_id=1, source_target_pairs={{0,8},{8,0},{16,24},{24,16},{1,9},{9,1},{17,25},{25,17},{2,10},{10... | collective-permute-start | bytes 172040 | tf_op jit(solution)/shard_map/ppermute | solution.py:15
  23.4 4.6 %collective-permute-start.8 = (f32[88,256]{1,0:T(8,128)S(1)}, f32[88,256]{1,0:T(8,128)S(1)}, u32[]{:S(2)}, u32[]{:S(2)}) collective-permute-start(f32[88,256]{1,0:T(8,128)S(1)} %get-tuple-element.84), channel_id=1, source_target_pairs={{0,4},{1,5},{2,6},{3,7},{4,0},{5,1},{6,2},{7,3},{8,12},{9,13},{10,... | collective-permute-start | bytes 270344 | tf_op jit(solution)/shard_map/ppermute | solution.py:15
  28.0 1.4 %collective-permute-start.9 = (f32[88,256]{1,0:T(8,128)S(1)}, f32[88,256]{1,0:T(8,128)S(1)}, u32[]{:S(2)}, u32[]{:S(2)}) collective-permute-start(f32[88,256]{1,0:T(8,128)S(1)} %add.3.mine_ref), channel_id=1, source_target_pairs={{0,1},{1,0},{2,3},{3,2},{4,5},{5,4},{6,7},{7,6},{8,9},{9,8},{10,11... | collective-permute-start | bytes 270344 | tf_op jit(solution)/shard_map/ppermute | solution.py:15

commit v6 on v5

--- a/solution.py
+++ b/solution.py
@@ -38,10 +38,6 @@
 
 def mm_nt(a, b):
     return lax.dot_general(a, b, (((1,), (1,)), ((), ())), preferred_element_type=F32)
-
-
-def mm_tn(a, b):
-    return lax.dot_general(a, b, (((0,), (0,)), ((), ())), preferred_element_type=F32)
 
 
 def each(count, step):
@@ -77,26 +73,35 @@
         self.col_step = min(512, self.cols)
         self.early_step = min(256, self.cols)
 
-    def network(self, lanes):
-        return dict(
-            x=((self.ins, lanes), F32),
-            h1=((self.hid, lanes), BF),
-            h2=((self.hid, lanes), BF),
-            m=((self.rows, lanes), BF),
-        )
-
     def windows(self):
         w = self.wide
-        return self.network(w) | dict(
-            key=((w, 4 * self.feats), BF),
-            vec=((w, 4 * self.vecs), BF),
-            norm=((w, self.own), F32),
-            sums=((w, self.rows), F32),
+        return dict(
+            x=((self.ins, w), F32),
+            h1=((self.hid, w), BF),
+            h2=((self.hid, w), BF),
+            m=((self.rows, w), BF),
+            right=((w, self.rows), BF),
+            vec=((4 * self.vecs, w), BF),
+            norm=((8, w), F32),
+            sums=((self.rows, w), F32),
         )
 
     def columns(self):
         c = self.cols
-        return self.network(c) | dict(vec=((4 * self.vecs, c), BF), norm=((8, c), F32), sums=((self.rows, c), F32))
+        return dict(
+            x=((self.ins, c), F32),
+            h1=((c, self.hid), BF),
+            h2=((c, self.hid), BF),
+            slope=((c, self.hid), F32),
+            pair=((c, 2 * self.feats), BF),
+            m=((self.rows, c), BF),
+            vec=((c, 4 * self.vecs), BF),
+            norm=((c, self.own), F32),
+            sums=((c, self.rows), F32),
+        )
+
+
+WEIGHTS = ("into", "out", "back")
 
 
 class Refs:
@@ -135,54 +140,90 @@
     window_ref[ins:] = nearer(own_ref[ins:], far_vec[...])
 
 
-def weights_kernel(z, w_in, b_in, w_out, w_stack_ref, out_m_ref, out_k_ref):
+def weights_kernel(z, w_in, b_in, w_out, *refs):
+    col, win = Refs(WEIGHTS, refs[:3]), Refs(WEIGHTS, refs[3:])
     w_all = jnp.concatenate([w_in[0], b_in[...], jnp.zeros((z.ins - z.depth - 1, z.hid), F32)], 0)
     w1, w2, w3 = split(w_all, 3)
-    w_stack_ref[...] = stack([w1, w1, w2, w2, w1, w3]).T
+    w_stack = stack([w1, w1, w2, w2, w1, w3])
+    col.into[...] = w_stack
+    win.into[...] = w_stack.T
     o1, o2 = split(w_out[...])
-    out_m_ref[...] = stack([o1, o2])
-    out_k_ref[...] = stack([o1, o1, o2, o2]).T
-
-
-def network(z, s, w_stack, out_m):
+    out = stack([o1, o2])
+    win.out[...] = out
+    col.out[...] = jnp.concatenate([out.T, out.T], 0)
+    back = stack([o1, o1, o2, o2])
+    col.back[...] = back
+    win.back[...] = back.T
+
+
+def beside(parts):
+    return jnp.concatenate(parts, 1)
+
+
+def both_halves(value):
+    return value + pltpu.roll(value, value.shape[1] // 2, 1)
+
+
+def paired(value):
+    high = value.astype(BF).astype(F32)
+    first = lax.broadcasted_iota(jnp.int32, value.shape, 1) < value.shape[1] // 2
+    return jnp.where(first, high, value - high).astype(BF)
+
+
+def column_network(z, s, w):
+    def into(here):
+        x1, x2, x3 = split(s.x[:, here], 3)
+        return mm(stack([x1, x2, x1, x2, x3, x1]).T, w.into[...])
+
+    def middle(here, pre):
+        h = jnp.tanh(pre)
+        h1 = h.astype(BF)
+        h2 = (h - h1.astype(F32)).astype(BF)
+        s.h1[here, :], s.h2[here, :] = h1, h2
+        s.slope[here, :] = 1.0 - h * h
+        return mm(beside([h1, h2]), w.out[...])
+
+    def out(here, raw):
+        pair = paired(both_halves(raw))
+        s.pair[here, :] = pair
+        s.m[: 2 * z.feats, here] = pair.T
+        s.m[2 * z.feats :, here] = jnp.ones((16, raw.shape[0]), BF)
+        return pair
+
+    return into, middle, out
+
+
+def window_network(z, s, w):
     def into(lanes):
         x1, x2, x3 = split(s.x[:, lanes], 3)
-        return mm(w_stack, stack([x1, x2, x1, x2, x3, x1]))
+        return mm(w.into[...], stack([x1, x2, x1, x2, x3, x1]))
 
     def middle(lanes, pre):
         h = jnp.tanh(pre)
         h1 = h.astype(BF)
         h2 = (h - h1.astype(F32)).astype(BF)
         s.h1[:, lanes], s.h2[:, lanes] = h1, h2
-        return mm(out_m, h1) + mm(out_m, h2)
+        return mm(w.out[...], h1) + mm(w.out[...], h2)
 
     def out(lanes, raw):
+        count = raw.shape[1]
         f1, f2 = split(raw[: z.feats] + raw[z.feats :])
-        s.m[:, lanes] = stack([f1, f2, jnp.ones((16, raw.shape[1]), F32)])
+        m = stack([f1, f2, jnp.ones((16, count), F32)])
+        s.m[:, lanes] = m
+        s.right[lanes, :] = m.T
         exact = f1 + f2
-        return 0.5 * jnp.sum(exact * exact, 0, keepdims=True)
+        s.norm[:, lanes] = jnp.broadcast_to(0.5 * jnp.sum(exact * exact, 0, keepdims=True), (8, count))
 
     return into, middle, out
 
 
-def window_features(z, blocks_ref, s, w_stack, out_m, others=()):
-    own, part, step = z.own, z.part, z.win_step
+def window_blocks(z, blocks_ref, s):
+    own, part = z.own, z.part
     for r in range(z.wide // own):
         here = pl.ds(r * own, own)
         s.x[:, here] = blocks_ref[r * part : r * part + z.ins]
         v1, v2 = split(blocks_ref[r * part + z.ins : (r + 1) * part])
-        s.vec[here, :] = stack([v1, v2, v1, v2]).T
-    into, middle, out = network(z, s, w_stack, out_m)
-    for i in range(z.wide // step):
-        rows = pl.ds(i * step, step)
-        value = into(rows)
-        other = others[i][0]() if others else None
-        value = middle(rows, value)
-        if others:
-            others[i][1](other)
-        norm = out(rows, value)
-        s.key[rows, :] = jnp.concatenate([s.m[: 2 * z.feats, rows]] * 2, 0).T
-        s.norm[rows, :] = jnp.broadcast_to(norm, (own, step)).T
+        s.vec[:, here] = stack([v1, v2, v1, v2])
     s.sums[...] = jnp.zeros(s.sums.shape, F32)
 
 
@@ -191,11 +232,7 @@
         here = pl.ds(r * z.own, z.own)
         s.x[:, here] = blocks_ref[r * z.part : r * z.part + z.ins]
         v1, v2 = split(blocks_ref[r * z.part + z.ins : (r + 1) * z.part])
-        s.vec[:, here] = stack([v1, v1, v2, v2])
-
-
-def beside(parts):
-    return jnp.concatenate(parts, 1)
+        s.vec[here, :] = stack([v1, v1, v2, v2]).T
 
 
 def tile(z, win, col, width):
@@ -203,21 +240,22 @@
     single = z.wide == step
 
     def products(lanes, rows):
-        m = col.m[: 2 * feats, lanes]
+        m = win.m[: 2 * feats, rows]
         f1, f2 = m[:feats], m[feats:]
-        cross = mm(win.key[rows, :], jnp.concatenate([f1, f1, f2, f2], 0))
-        return cross, mm(win.vec[rows, :], col.vec[:, lanes])
+        pair = col.pair[lanes, :]
+        cross = mm(beside([pair, pair]), jnp.concatenate([f1, f1, f2, f2], 0))
+        return cross, mm(col.vec[lanes, :], win.vec[:, rows])
 
     def weighed(lanes, rows, dots):
-        far = beside([win.norm[rows, :]] * (width // z.own))
-        weigh = jnp.exp(dots[0] - far - col.norm[:1, lanes]) * dots[1]
+        own_norm = beside([col.norm[lanes, :]] * (step // z.own))
+        weigh = jnp.exp(dots[0] - own_norm - win.norm[:1, rows]) * dots[1]
         g1 = weigh.astype(BF)
         g2 = (weigh - g1.astype(F32)).astype(BF)
         both = jnp.concatenate([g1, g2], 0)
-        mine = win.m[:, rows]
-        part = mm_nt(both, col.m[:, lanes])
-        win.sums[rows, :] += part[:step] + part[step:]
-        return mm(beside([mine, mine]), both)
+        part = mm(both, win.right[rows, :])
+        m = col.m[:, lanes]
+        win.sums[:, rows] += mm(beside([m, m]), both)
+        return part[:width] + part[width:]
 
     def first(lanes):
         return products(lanes, pl.ds(0, step)) if single else None
@@ -230,22 +268,50 @@
             rows = pl.ds(k * step, step)
             return sums + weighed(lanes, rows, products(lanes, rows))
 
-        return lax.fori_loop(0, z.wide // step, add, jnp.zeros((z.rows, width), F32))
+        return lax.fori_loop(0, z.wide // step, add, jnp.zeros((width, z.rows), F32))
 
     return first, second
 
 
-def total_of(z, m, sums):
+def window_terms(z, s, rows):
     feats = z.feats
-    m = m[: 2 * feats].astype(F32)
-    return sums[:feats] + sums[feats : 2 * feats] - (m[:feats] + m[feats:]) * sums[2 * feats : 2 * feats + 1]
-
-
-def backprop(z, s, out_k, pack_ref):
-    def first(lanes, total):
-        t1, t2 = split(total)
-        t_stack = stack([t1, t2])
-        g = mm(out_k, jnp.concatenate([t_stack, t_stack], 0))
+    m, sums = s.m[: 2 * feats, rows].astype(F32), s.sums[:, rows]
+    total = sums[:feats] + sums[feats : 2 * feats] - (m[:feats] + m[feats:]) * sums[2 * feats : 2 * feats + 1]
+    return stack(split(total))
+
+
+def column_total(z, s, here, sums):
+    wide = 2 * z.feats
+    return both_halves(sums[:, :wide]) - both_halves(s.pair[here, :].astype(F32)) * sums[:, wide : wide + 1]
+
+
+def column_terms(total):
+    pair = paired(total)
+    return pair.T, pair
+
+
+def column_backprop(z, s, w, pack_ref):
+    def first(here, terms):
+        t_stack, pair = terms
+        g = mm(beside([pair, pair]), w.back[...])
+        both = mm(beside([t_stack, t_stack]), jnp.concatenate([s.h1[here, :], s.h2[here, :]], 0))
+        pack_ref[: z.feats] += both[: z.feats] + both[z.feats :]
+        return g
+
+    def second(here, g):
+        g = g * s.slope[here, :]
+        x_stack = stack(split(s.x[:, here]))
+        g1 = g.astype(BF)
+        g2 = (g - g1.astype(F32)).astype(BF)
+        both = mm(beside([x_stack, x_stack]), jnp.concatenate([g1, g2], 0))
+        pack_ref[z.feats :] += both[: z.ins] + both[z.ins :]
+
+    return first, second
+
+
+def window_backprop(z, s, w, pack_ref):
+    def first(lanes, t_stack):
+        g = mm(w.back[...], jnp.concatenate([t_stack, t_stack], 0))
         both = mm_nt(beside([t_stack, t_stack]), beside([s.h1[:, lanes], s.h2[:, lanes]]))
         pack_ref[: z.feats] += both[: z.feats] + both[z.feats :]
         return g
@@ -262,78 +328,102 @@
     return first, second
 
 
-def window_total(z, s, rows):
-    return total_of(z, s.m[:, rows], s.sums[rows, :].T)
-
-
 def column_steps(z, step):
     return [pl.ds(k * step, step) for k in range(z.cols // step)]
 
 
-def column_features(z, blocks_ref, col, win, w_stack, out_m):
+def window_steps(z):
+    return [pl.ds(k * z.win_step, z.win_step) for k in range(z.wide // z.win_step)]
+
+
+def column_features(z, blocks_ref, col, win, w, w_win=None):
     column_blocks(z, blocks_ref, col)
-    into, middle, out = network(z, col, w_stack, out_m)
+    into, middle, out = column_network(z, col, w)
     first, second = tile(z, win, col, z.early_step)
     lanes = column_steps(z, z.early_step)
-
-    def third(k, raw):
-        col.norm[:, lanes[k]] = jnp.broadcast_to(out(lanes[k], raw), (8, z.early_step))
-        return first(lanes[k])
-
-    def fourth(k, dots):
-        col.sums[:, lanes[k]] = second(lanes[k], dots)
-
-    flow(len(lanes), lambda k, _: into(lanes[k]), lambda k, pre: middle(lanes[k], pre), third, fourth)
-
-
-def near_kernel(z, windows_ref, columns_ref, w_stack_ref, out_m_ref, *refs):
+    rows = window_steps(z) if w_win else []
+    stages = window_network(z, win, w_win) if w_win else ()
+
+    def third(here, raw):
+        out(here, raw)
+        exact = both_halves(col.pair[here, :].astype(F32))
+        norm = 0.25 * jnp.sum(exact * exact, 1, keepdims=True)
+        col.norm[here, :] = jnp.broadcast_to(norm, (z.early_step, z.own))
+        return first(here)
+
+    def fourth(here, dots):
+        col.sums[here, :] = second(here, dots)
+
+    def stage(depth):
+        def do(k, value):
+            if k >= len(rows):
+                here = lanes[k - len(rows)]
+                return into(here) if depth == 0 else (middle, third, fourth)[depth - 1](here, value)
+            if depth < 3:
+                return stages[0](rows[k]) if depth == 0 else stages[depth](rows[k], value)
+
+        return do
+
+    flow(len(rows) + len(lanes), *[stage(depth) for depth in range(4)])
+
+
+def near_kernel(z, windows_ref, columns_ref, *refs):
     n = len(z.windows())
+    w_col, w_win, refs = Refs(WEIGHTS, refs[:3]), Refs(WEIGHTS, refs[3:6]), refs[6:]
     win, col = Refs(z.windows(), refs[:n]), Refs(z.columns(), refs[n:])
-    w_stack, out_m = w_stack_ref[...], out_m_ref[...]
-    window_features(z, windows_ref, win, w_stack, out_m)
-    column_features(z, columns_ref, col, win, w_stack, out_m)
-
-
-def far_kernel(z, columns_ref, w_stack_ref, out_m_ref, *refs):
+    window_blocks(z, windows_ref, win)
+    column_features(z, columns_ref, col, win, w_col, w_win)
+
+
+def far_kernel(z, columns_ref, *refs):
     n, c = len(z.windows()), len(z.columns())
+    w_col, refs = Refs(WEIGHTS, refs[:3]), refs[3:]
     win, col = Refs(z.windows(), refs[:n]), Refs(z.columns(), refs[n : n + c])
     sums_ref = refs[n + c]
     sums_ref[...] = win.sums[...]
     win.sums = sums_ref
-    column_features(z, columns_ref, col, win, w_stack_ref[...], out_m_ref[...])
-
-
-def late_kernel(z, windows_ref, w_stack_ref, out_m_ref, out_k_ref, *refs):
-    w, c = len(z.windows()), len(z.columns())
-    near = Refs(z.windows(), refs[:w])
-    cols = [Refs(z.columns(), refs[w : w + c]), Refs(z.columns(), refs[w + c : w + 2 * c])]
-    near.sums, col_grad_ref, pack_ref = refs[w + 2 * c : w + 2 * c + 3]
-    win = Refs(z.windows(), refs[w + 2 * c + 3 :])
-    out_k = out_k_ref[...]
+    column_features(z, columns_ref, col, win, w_col)
+
+
+def late_kernel(z, windows_ref, *refs):
+    n, c = len(z.windows()), len(z.columns())
+    w_col, w_win, refs = Refs(WEIGHTS, refs[:3]), Refs(WEIGHTS, refs[3:6]), refs[6:]
+    near = Refs(z.windows(), refs[:n])
+    cols = [Refs(z.columns(), refs[n : n + c]), Refs(z.columns(), refs[n + c : n + 2 * c])]
+    near.sums, col_grad_ref, pack_ref = refs[n + 2 * c : n + 2 * c + 3]
+    win = Refs(z.windows(), refs[n + 2 * c + 3 :])
     pack_ref[...] = jnp.zeros(pack_ref.shape, F32)
-    rows = [pl.ds(i * z.win_step, z.win_step) for i in range(z.wide // z.win_step)]
-
-    def backward(work, totals):
-        stages = [backprop(z, s, out_k, pack_ref) for s, _ in work]
-        first = [lambda k=k: stages[k][0](work[k][1], totals[k]()) for k in range(len(work))]
-        second = [lambda g, k=k: stages[k][1](work[k][1], g) for k in range(len(work))]
-        return first, second
-
-    first, second = backward([(near, r) for r in rows], [functools.partial(window_total, z, near, r) for r in rows])
-    window_features(z, windows_ref, win, w_stack_ref[...], out_m_ref[...], list(zip(first, second)))
+    rows = window_steps(z)
+
+    def of_window(s, here):
+        first, second = window_backprop(z, s, w_win, pack_ref)
+        return lambda: first(here, window_terms(z, s, here)), lambda g: second(here, g)
+
+    def of_columns(s, here, total):
+        first, second = column_backprop(z, s, w_col, pack_ref)
+        return lambda: first(here, column_terms(total)), lambda g: second(here, g)
+
+    window_blocks(z, windows_ref, win)
+    into, middle, out = window_network(z, win, w_win)
+    for here in rows:
+        first, second = of_window(near, here)
+        value = into(here)
+        other = first()
+        value = middle(here, value)
+        second(other)
+        out(here, value)
     work = [(col, lanes) for col in cols for lanes in column_steps(z, z.col_step)]
     totals = []
 
     def total(k, dots):
         col, lanes = work[k]
-        sums = col.sums[:, lanes] + tile(z, win, col, z.col_step)[1](lanes, dots)
-        totals.append(total_of(z, col.m[:, lanes], sums))
+        sums = col.sums[lanes, :] + tile(z, win, col, z.col_step)[1](lanes, dots)
+        totals.append(column_total(z, col, lanes, sums))
 
     flow(len(work), lambda k, _: tile(z, win, work[k][0], z.col_step)[0](work[k][1]), total)
-    col_grad_ref[...] = totals[0][:, : z.own]
-    totals = [lambda t=t: t for t in totals] + [functools.partial(window_total, z, win, r) for r in rows]
-    first, second = backward(work + [(win, r) for r in rows], totals)
-    flow(len(first), lambda k, _: first[k](), lambda k, g: second[k](g))
+    col_grad_ref[...] = totals[0][: z.own].T[: z.feats]
+    stages = [of_columns(*item, t) for item, t in zip(work, totals)] + [of_window(win, here) for here in rows]
+    flow(len(stages), lambda k, _: stages[k][0](), lambda k, g: stages[k][1](g))
 
 
 def finish_kernel(z, mine_ref, theirs_ref, own_ref, col_grad_ref, grad_in_ref, grad_bias_ref, grad_out_ref):
@@ -390,20 +480,18 @@
         return jnp.where((apart[:1] & bit) == 0, mine, theirs)
 
     window, w_in, b_in, w_out = lax.optimization_barrier((window, w_in, b_in, w_out))
-    w_stack, out_m, out_k = call(
+    forms = ((6 * z.ins, z.hid), (2 * z.hid, 2 * z.feats), (4 * z.feats, z.hid))
+    forms += ((z.hid, 6 * z.ins), (2 * z.feats, z.hid), (z.hid, 4 * z.feats))
+    weights = call(
         functools.partial(weights_kernel, z),
         "weights",
-        (
-            jax.ShapeDtypeStruct((z.hid, 6 * z.ins), BF),
-            jax.ShapeDtypeStruct((2 * z.feats, z.hid), BF),
-            jax.ShapeDtypeStruct((z.hid, 4 * z.feats), BF),
-        ),
+        [jax.ShapeDtypeStruct(form, BF) for form in forms],
         (w_in[None], b_in.reshape(1, -1), w_out.T),
     )
     got = swap(jnp.concatenate([window, columns]), "col", n_col, joined)
     window = nearer(joined, window, got[: z.part])
     columns = jnp.concatenate([columns, got[z.part :]])
-    window, w_stack, out_m, out_k = lax.optimization_barrier((window, w_stack, out_m, out_k))
+    window, *weights = lax.optimization_barrier((window, *weights))
     for bit in reversed(bits_of(n_row)[1:]):
         columns = jnp.concatenate([columns, swap(columns, "row", n_row, bit)])
     far_columns = swap(columns, "row", n_row, 1)
@@ -417,7 +505,7 @@
         functools.partial(near_kernel, z),
         "near",
         (*shapes(z.windows()), *shapes(z.columns())),
-        (window, columns, w_stack, out_m),
+        (window, columns, *weights),
         limit=limit,
         cost=10,
     )
@@ -426,7 +514,7 @@
         functools.partial(far_kernel, z),
         "far",
         (*shapes(z.columns()), jax.ShapeDtypeStruct(*z.windows()["sums"])),
-        (far_columns, w_stack, out_m, *windows),
+        (far_columns, *weights[:3], *windows),
         limit=limit,
         cost=10,
     )
@@ -434,7 +522,7 @@
         functools.partial(late_kernel, z),
         "late",
         (f32((z.feats, own)), f32((z.feats + z.ins, z.hid))),
-        (far_window, w_stack, out_m, out_k, *windows, *near, *far, sums),
+        (far_window, *weights, *windows, *near, *far, sums),
         [VMEM(*v) for v in z.windows().values()],
         limit=limit,
         cost=20,

time: 30.3 us -> 30.2 us (level)
  transfers between devices with their start and end apart: 10 -> 10, of which waited for: 7 -> 6; matrix products, arithmetic and copies ran while one was open for 0% -> 0% of each run, Pallas kernels for 10% -> 11%
where the time goes in v6:
time: 30.2 us; the launch traced here: 29.9 us
  starting transfers between devices  14.8 us (49%)
  waiting for transfers between devices  7.59 us (25%)
  Pallas kernels  6.04 us (20%)
  between operations  0.74 us (2%)
  local copies, waits for them, and re-layouts  0.68 us (2%)
    ppermute x10, starting transfers between devices, swap(): return lax.ppermute(value, axis, [(i, i ^ bit) for i in range(size)])  14.8 us
    ppermute x10, waiting for transfers between devices, swap(): return lax.ppermute(value, axis, [(i, i ^ bit) for i in range(size)])  7.59 us
    pallas_call x7, Pallas kernels, call(): pl.pallas_call(kernel, out_shape=tuple(outs), in_specs=[pl.BlockSpec(memo...  6.04 us
    unnamed x6, local copies, waits for them, and re-layouts  0.68 us
  transfers between devices with their start and end apart: 10, of which 6 were waited for; matrix products, arithmetic and copies ran while one was open for 0% of the time, Pallas kernels for 11%

profile of v6, /device:TPU:0, one launch (start us, length us, event | category | flops | bytes accessed | tf_op | source)
XLA Modules:
  0.0 29.9 jit_solution(5818378978253939722)
XLA Ops:
  0.6 0.5 %collective-permute-start.1 = (f32[32,128]{1,0:T(8,128)}, f32[32,128]{1,0:T(8,128)S(1)}, u32[]{:S(2)}, u32[]{:S(2)}) collective-permute-start(f32[32,128]{1,0:T(8,128)} %vec_hbm.1), channel_id=1, source_target_pairs={{0,1},{1,0},{2,3},{3,2},{4,5},{5,4},{6,7},{7,6},{8,9},{9,8},{10,11... | collective-permute-start | bytes 49160 | tf_op jit(solution)/shard_map/ppermute | solution.py:15
  1.1 0.1 collective-permute-start
  1.2 0.8 %prepare.1 = (f32[56,128]{1,0:T(8,128)S(1)}, f32[56,128]{1,0:T(8,128)S(1)}, s32[8,128]{1,0:T(8,128)S(1)}) custom-call(s32[4]{0:T(128)} %blocks_hbm.1, f32[20,128]{1,0:T(8,128)} %in_hbm.1, f32[32,128]{1,0:T(8,128)} %vec_hbm.1, f32[32,128]{1,0:T(8,128)} %probes_hbm.1), custom_call_target="tpu_custom_call" | custom-call | flops 100000000 | bytes 1000000 | tf_op jit(solution)/shard_map/prepare/pallas_call | solution.py:446
  2.0 0.5 %collective-permute-done.far_in = f32[20,128]{1,0:T(8,128)S(1)} collective-permute-done((f32[20,128]{1,0:T(8,128)}, f32[20,128]{1,0:T(8,128)S(1)}, u32[]{:S(2)}, u32[]{:S(2)}) %collective-permute-start) | collective-permute-done | bytes 10272 | tf_op jit(solution)/shard_map/ppermute | solution.py:15
  2.5 0.0 collective-permute-done.1.far_vec
  2.6 0.0 copy-start
  2.6 0.0 copy-start.1
  2.6 2.7 %collective-permute-start.2 = (f32[112,128]{1,0:T(8,128)S(1)}, f32[112,128]{1,0:T(8,128)S(1)}, u32[]{:S(2)}, u32[]{:S(2)}) collective-permute-start(f32[112,128]{1,0:T(8,128)S(1)} %pad_maximum_fusion.1), channel_id=1, source_target_pairs={{0,2},{1,3},{2,0},{3,1},{4,6},{5,7},{6,4},{7,5},{8,10},{9,11},{10,... | collective-permute-start | bytes 172040 | tf_op jit(solution)/shard_map/ppermute | solution.py:15
  5.3 0.0 copy-start.2
  5.3 0.0 copy-done
  5.3 0.0 copy-done.1
  5.3 0.7 %copy-done.2 = f32[256]{0:T(256)S(1)} copy-done((f32[256]{0:T(256)S(1)}, f32[256]{0:T(256)}, u32[]{:S(2)}) %copy-start.2) | copy-done | bytes 1048
  6.0 0.1 weights.1
  6.1 1.6 %collective-permute-done.2 = f32[112,128]{1,0:T(8,128)S(1)} collective-permute-done((f32[112,128]{1,0:T(8,128)S(1)}, f32[112,128]{1,0:T(8,128)S(1)}, u32[]{:S(2)}, u32[]{:S(2)}) %collective-permute-start.2) | collective-permute-done | bytes 57376 | tf_op jit(solution)/shard_map/ppermute | solution.py:15
  7.7 1.8 %collective-permute-start.3 = (f32[56,128]{1,0:T(8,128)S(1)}, f32[56,128]{1,0:T(8,128)S(1)}, u32[]{:S(2)}, u32[]{:S(2)}) collective-permute-start(f32[56,128]{1,0:T(8,128)S(1)} %get-tuple-element.70), channel_id=1, source_target_pairs={{0,4},{1,5},{2,6},{3,7},{4,0},{5,1},{6,2},{7,3},{8,12},{9,13},{10,... | collective-permute-start | bytes 86024 | tf_op jit(solution)/shard_map/ppermute | solution.py:15
  9.5 2.6 %collective-permute-start.6 = (f32[112,128]{1,0:T(8,128)S(1)}, f32[112,128]{1,0:T(8,128)S(1)}, u32[]{:S(2)}, u32[]{:S(2)}) collective-permute-start(f32[112,128]{1,0:T(8,128)S(1)} %pad_maximum_fusion.3), channel_id=1, source_target_pairs={{0,16},{8,24},{16,0},{24,8},{1,17},{9,25},{17,1},{25,9},{2,18},{10... | collective-permute-start | bytes 172040 | tf_op jit(solution)/shard_map/ppermute | solution.py:15
  12.1 0.0 collective-permute-done.3
  12.1 2.3 %collective-permute-start.4 = (f32[56,128]{1,0:T(8,128)S(1)}, f32[56,128]{1,0:T(8,128)S(1)}, u32[]{:S(2)}, u32[]{:S(2)}) collective-permute-start(f32[56,128]{1,0:T(8,128)S(1)} %broadcast_select_fusion), channel_id=1, source_target_pairs={{0,16},{8,24},{16,0},{24,8},{1,17},{9,25},{17,1},{25,9},{2,18},{10... | collective-permute-start | bytes 86024 | tf_op jit(solution)/shard_map/ppermute | solution.py:15
  14.5 0.4 %collective-permute-done.6 = f32[112,128]{1,0:T(8,128)S(1)} collective-permute-done((f32[112,128]{1,0:T(8,128)S(1)}, f32[112,128]{1,0:T(8,128)S(1)}, u32[]{:S(2)}, u32[]{:S(2)}) %collective-permute-start.6) | collective-permute-done | bytes 57376 | tf_op jit(solution)/shard_map/ppermute | solution.py:15
  14.9 1.6 %collective-permute-start.7 = (f32[224,128]{1,0:T(8,128)S(1)}, f32[224,128]{1,0:T(8,128)S(1)}, u32[]{:S(2)}, u32[]{:S(2)}) collective-permute-start(f32[224,128]{1,0:T(8,128)S(1)} %pad_maximum_fusion.columns_ref), channel_id=1, source_target_pairs={{0,8},{8,0},{16,24},{24,16},{1,9},{9,1},{17,25},{25,17},{2,10},{10... | collective-permute-start | bytes 344072 | tf_op jit(solution)/shard_map/ppermute | solution.py:15
  16.5 0.4 %collective-permute-done.4 = f32[56,128]{1,0:T(8,128)S(1)} collective-permute-done((f32[56,128]{1,0:T(8,128)S(1)}, f32[56,128]{1,0:T(8,128)S(1)}, u32[]{:S(2)}, u32[]{:S(2)}) %collective-permute-start.4) | collective-permute-done | bytes 28704 | tf_op jit(solution)/shard_map/ppermute | solution.py:15
  17.0 1.9 %collective-permute-start.5 = (f32[112,128]{1,0:T(8,128)S(1)}, f32[112,128]{1,0:T(8,128)S(1)}, u32[]{:S(2)}, u32[]{:S(2)}) collective-permute-start(f32[112,128]{1,0:T(8,128)S(1)} %pad_maximum_fusion.2.windows_ref), channel_id=1, source_target_pairs={{0,8},{8,0},{16,24},{24,16},{1,9},{9,1},{17,25},{25,17},{2,10},{10... | collective-permute-start | bytes 172040 | tf_op jit(solution)/shard_map/ppermute | solution.py:15
  18.9 1.2 %near.1 = (f32[24,256]{1,0:T(8,128)S(1)}, bf16[256,256]{1,0:T(8,128)(2,1)S(1)}, bf16[256,256]{1,0:T(8,128)(2,1)S(1)}, bf16[144,256]{1,0:T(8,128)(2,1)S(1)}, bf16...) custom-call(f32[112,128]{1,0:T(8,128)S(1)} %pad_maximum_fusion.2.win, ...), custom_call_target="tpu_custom_call" | custom-call | flops 1000000000 | bytes 1000000 | tf_op jit(solution)/shard_map/near/pallas_call | solution.py:446
  20.0 0.0 collective-permute-done.7.columns_ref
  20.1 1.2 %far.1 = (f32[24,512]{1,0:T(8,128)S(1)}, bf16[512,256]{1,0:T(8,128)(2,1)S(1)}, bf16[512,256]{1,0:T(8,128)(2,1)S(1)}, f32[512,256]{1,0:T(8,128)S(1)}, bf16[512,12...) custom-call(f32[224,128]{1,0:T(8,128)S(1)} %collective-permute-done., ...), custom_call_target="tpu_custom_call" | custom-call | flops 1000000000 | bytes 1000000 | tf_op jit(solution)/shard_map/far/pallas_call | solution.py:446
  21.2 0.0 collective-permute-done.5.windows_ref
  21.2 2.1 %late.1 = (f32[64,128]{1,0:T(8,128)S(1)}, f32[88,256]{1,0:T(8,128)S(1)}) custom-call(f32[112,128]{1,0:T(8,128)S(1)} %collective-permute-done.5.windows_ref, bf16[144,256]{1,0:T(8,128)(2,1)S(1)} %get-tuple-element.71.refs_0_, bf16[512,128]{1,0:T(8,128)(2,1)S(1)} %get-tuple-element.72.refs_1_, bf16[256,256]{1,0:T(8,128)(2,1)S(1)} %get-tuple-element.73.refs_2_, ...), custom_call_target="tpu_custom_call" | custom-call | flops 2000000000 | bytes 1000000 | tf_op jit(solution)/shard_map/late/pallas_call | solution.py:446
  23.3 1.2 %collective-permute-start.8 = (f32[88,256]{1,0:T(8,128)S(1)}, f32[88,256]{1,0:T(8,128)S(1)}, u32[]{:S(2)}, u32[]{:S(2)}) collective-permute-start(f32[88,256]{1,0:T(8,128)S(1)} %get-tuple-element.104), channel_id=1, source_target_pairs={{0,4},{1,5},{2,6},{3,7},{4,0},{5,1},{6,2},{7,3},{8,12},{9,13},{10,... | collective-permute-start | bytes 270344 | tf_op jit(solution)/shard_map/ppermute | solution.py:15
  24.5 3.4 %collective-permute-done.8 = f32[88,256]{1,0:T(8,128)S(1)} collective-permute-done((f32[88,256]{1,0:T(8,128)S(1)}, f32[88,256]{1,0:T(8,128)S(1)}, u32[]{:S(2)}, u32[]{:S(2)}) %collective-permute-start.8) | collective-permute-done | bytes 90144 | tf_op jit(solution)/shard_map/ppermute | solution.py:15
  27.9 0.1 collective-permute-start.9
  28.0 1.3 %collective-permute-done.9.theirs_ref = f32[88,256]{1,0:T(8,128)S(1)} collective-permute-done((f32[88,256]{1,0:T(8,128)S(1)}, f32[88,256]{1,0:T(8,128)S(1)}, u32[]{:S(2)}, u32[]{:S(2)}) %collective-permute-start.9) | collective-permute-done | bytes 90144 | tf_op jit(solution)/shard_map/ppermute | solution.py:15
  29.3 0.7 %finish.1 = (f32[64,128]{1,0:T(8,128)}, f32[20,256]{1,0:T(8,128)}, f32[1,256]{1,0:T(1,128)}, f32[64,256]{1,0:T(8,128)}) custom-call(f32[88,256]{1,0:T(8,128)S(1)} %add.3.mine_ref, f32[88,256]{1,0:T(8,128)S(1)} %collective-permute-done.9.theirs_ref, f32[64,128]{1,0:T(8,128)S(1)} %get-tuple-element.105.own_ref), custom_call_target="tpu_custom_call" | custom-call | flops 100000000 | bytes 1000000 | tf_op jit(solution)/shard_map/finish/pallas_call | solution.py:446
  (9 shorter events, 0.1 us)
Async XLA Ops:
  0.6 1.9 %collective-permute-start.1 = (f32[32,128]{1,0:T(8,128)}, f32[32,128]{1,0:T(8,128)S(1)}, u32[]{:S(2)}, u32[]{:S(2)}) collective-permute-start(f32[32,128]{1,0:T(8,128)} %vec_hbm.1), channel_id=1, source_target_pairs={{0,1},{1,0},{2,3},{3,2},{4,5},{5,4},{6,7},{7,6},{8,9},{9,8},{10,11... | collective-permute-start | bytes 49160 | tf_op jit(solution)/shard_map/ppermute | solution.py:15
  1.1 1.4 %collective-permute-start = (f32[20,128]{1,0:T(8,128)}, f32[20,128]{1,0:T(8,128)S(1)}, u32[]{:S(2)}, u32[]{:S(2)}) collective-permute-start(f32[20,128]{1,0:T(8,128)} %in_hbm.1), channel_id=1, source_target_pairs={{0,1},{1,0},{2,3},{3,2},{4,5},{5,4},{6,7},{7,6},{8,9},{9,8},{10,11... | collective-permute-start | bytes 30728 | tf_op jit(solution)/shard_map/ppermute | solution.py:15
  2.6 2.8 %copy-start = (f32[256,64]{0,1:T(8,128)S(1)}, f32[256,64]{0,1:T(8,128)}, u32[]{:S(2)}) copy-start(f32[256,64]{0,1:T(8,128)} %param.10) | copy-start | bytes 196612
  2.6 2.8 %copy-start.1 = (f32[20,256]{1,0:T(8,128)S(1)}, f32[20,256]{1,0:T(8,128)}, u32[]{:S(2)}) copy-start(f32[20,256]{1,0:T(8,128)} %param.8) | copy-start | bytes 61444
  2.6 5.1 %collective-permute-start.2 = (f32[112,128]{1,0:T(8,128)S(1)}, f32[112,128]{1,0:T(8,128)S(1)}, u32[]{:S(2)}, u32[]{:S(2)}) collective-permute-start(f32[112,128]{1,0:T(8,128)S(1)} %pad_maximum_fusion.1), channel_id=1, source_target_pairs={{0,2},{1,3},{2,0},{3,1},{4,6},{5,7},{6,4},{7,5},{8,10},{9,11},{10,... | collective-permute-start | bytes 172040 | tf_op jit(solution)/shard_map/ppermute | solution.py:15
  5.3 0.7 %copy-start.2 = (f32[256]{0:T(256)S(1)}, f32[256]{0:T(256)}, u32[]{:S(2)}) copy-start(f32[256]{0:T(256)} %param.9) | copy-start | bytes 3076
  7.7 4.4 %collective-permute-start.3 = (f32[56,128]{1,0:T(8,128)S(1)}, f32[56,128]{1,0:T(8,128)S(1)}, u32[]{:S(2)}, u32[]{:S(2)}) collective-permute-start(f32[56,128]{1,0:T(8,128)S(1)} %get-tuple-element.70), channel_id=1, source_target_pairs={{0,4},{1,5},{2,6},{3,7},{4,0},{5,1},{6,2},{7,3},{8,12},{9,13},{10,... | collective-permute-start | bytes 86024 | tf_op jit(solution)/shard_map/ppermute | solution.py:15
  9.5 5.4 %collective-permute-start.6 = (f32[112,128]{1,0:T(8,128)S(1)}, f32[112,128]{1,0:T(8,128)S(1)}, u32[]{:S(2)}, u32[]{:S(2)}) collective-permute-start(f32[112,128]{1,0:T(8,128)S(1)} %pad_maximum_fusion.3), channel_id=1, source_target_pairs={{0,16},{8,24},{16,0},{24,8},{1,17},{9,25},{17,1},{25,9},{2,18},{10... | collective-permute-start | bytes 172040 | tf_op jit(solution)/shard_map/ppermute | solution.py:15
  12.1 4.8 %collective-permute-start.4 = (f32[56,128]{1,0:T(8,128)S(1)}, f32[56,128]{1,0:T(8,128)S(1)}, u32[]{:S(2)}, u32[]{:S(2)}) collective-permute-start(f32[56,128]{1,0:T(8,128)S(1)} %broadcast_select_fusion), channel_id=1, source_target_pairs={{0,16},{8,24},{16,0},{24,8},{1,17},{9,25},{17,1},{25,9},{2,18},{10... | collective-permute-start | bytes 86024 | tf_op jit(solution)/shard_map/ppermute | solution.py:15
  14.9 5.2 %collective-permute-start.7 = (f32[224,128]{1,0:T(8,128)S(1)}, f32[224,128]{1,0:T(8,128)S(1)}, u32[]{:S(2)}, u32[]{:S(2)}) collective-permute-start(f32[224,128]{1,0:T(8,128)S(1)} %pad_maximum_fusion.columns_ref), channel_id=1, source_target_pairs={{0,8},{8,0},{16,24},{24,16},{1,9},{9,1},{17,25},{25,17},{2,10},{10... | collective-permute-start | bytes 344072 | tf_op jit(solution)/shard_map/ppermute | solution.py:15
  17.0 4.2 %collective-permute-start.5 = (f32[112,128]{1,0:T(8,128)S(1)}, f32[112,128]{1,0:T(8,128)S(1)}, u32[]{:S(2)}, u32[]{:S(2)}) collective-permute-start(f32[112,128]{1,0:T(8,128)S(1)} %pad_maximum_fusion.2.windows_ref), channel_id=1, source_target_pairs={{0,8},{8,0},{16,24},{24,16},{1,9},{9,1},{17,25},{25,17},{2,10},{10... | collective-permute-start | bytes 172040 | tf_op jit(solution)/shard_map/ppermute | solution.py:15
  23.3 4.6 %collective-permute-start.8 = (f32[88,256]{1,0:T(8,128)S(1)}, f32[88,256]{1,0:T(8,128)S(1)}, u32[]{:S(2)}, u32[]{:S(2)}) collective-permute-start(f32[88,256]{1,0:T(8,128)S(1)} %get-tuple-element.104), channel_id=1, source_target_pairs={{0,4},{1,5},{2,6},{3,7},{4,0},{5,1},{6,2},{7,3},{8,12},{9,13},{10,... | collective-permute-start | bytes 270344 | tf_op jit(solution)/shard_map/ppermute | solution.py:15
  27.9 1.4 %collective-permute-start.9 = (f32[88,256]{1,0:T(8,128)S(1)}, f32[88,256]{1,0:T(8,128)S(1)}, u32[]{:S(2)}, u32[]{:S(2)}) collective-permute-start(f32[88,256]{1,0:T(8,128)S(1)} %add.3.mine_ref), channel_id=1, source_target_pairs={{0,1},{1,0},{2,3},{3,2},{4,5},{5,4},{6,7},{7,6},{8,9},{9,8},{10,11... | collective-permute-start | bytes 270344 | tf_op jit(solution)/shard_map/ppermute | solution.py:15

commit v7 on v6

--- a/solution.py
+++ b/solution.py
@@ -426,8 +426,11 @@
     flow(len(stages), lambda k, _: stages[k][0](), lambda k, g: stages[k][1](g))
 
 
-def finish_kernel(z, mine_ref, theirs_ref, own_ref, col_grad_ref, grad_in_ref, grad_bias_ref, grad_out_ref):
+def emit_kernel(own_ref, col_grad_ref):
     col_grad_ref[...] = own_ref[...]
+
+
+def finish_kernel(z, mine_ref, theirs_ref, grad_in_ref, grad_bias_ref, grad_out_ref):
     both = mine_ref[...] + theirs_ref[...]
     grad_out_ref[...] = both[: z.feats]
     grad_in_ref[...] = both[z.feats : z.feats + z.depth]
@@ -529,11 +532,12 @@
     )
     for bit in reversed(shared[1:]):
         pack = pack + swap(pack, "col", n_col, bit)
-    col_grad, grad_in, grad_bias, grad_out = call(
+    (col_grad,) = call(emit_kernel, "emit", (f32((z.feats, own)),), (col_grad,))
+    grad_in, grad_bias, grad_out = call(
         functools.partial(finish_kernel, z),
         "finish",
-        (f32((z.feats, own)), f32((depth, z.hid)), f32((1, z.hid)), f32((z.feats, z.hid))),
-        (pack, swap(pack, "col", n_col, shared[0]), col_grad),
+        (f32((depth, z.hid)), f32((1, z.hid)), f32((z.feats, z.hid))),
+        (pack, swap(pack, "col", n_col, shared[0])),
     )
     return (col_grad, grad_in, grad_bias.reshape(-1), grad_out.T)
 

time: 30.2 us -> 30.2 us (level)
  waiting for transfers between devices: 7.59 us -> 6.97 us
  Pallas kernels: 6.04 us -> 6.64 us
    ppermute x10, waiting for transfers between devices: 7.59 us -> 6.97 us  [swap(): return lax.ppermute(value, axis, [(i, i ^ bit) for i in range(size)])]
    pallas_call x7 -> x8, Pallas kernels: 6.04 us -> 6.64 us  [call(): pl.pallas_call(kernel, out_shape=tuple(outs), in_specs=[pl.BlockSpec(memo...]
  transfers between devices with their start and end apart: 10 -> 10, of which waited for: 6 -> 6; matrix products, arithmetic and copies ran while one was open for 0% -> 0% of each run, Pallas kernels for 11% -> 13%
where the time goes in v7:
time: 30.2 us; the launch traced here: 29.9 us
  starting transfers between devices  14.8 us (49%)
  waiting for transfers between devices  6.97 us (23%)
  Pallas kernels  6.64 us (22%)
  between operations  0.74 us (2%)
  local copies, waits for them, and re-layouts  0.68 us (2%)
    ppermute x10, starting transfers between devices, swap(): return lax.ppermute(value, axis, [(i, i ^ bit) for i in range(size)])  14.8 us
    ppermute x10, waiting for transfers between devices, swap(): return lax.ppermute(value, axis, [(i, i ^ bit) for i in range(size)])  6.97 us
    pallas_call x8, Pallas kernels, call(): pl.pallas_call(kernel, out_shape=tuple(outs), in_specs=[pl.BlockSpec(memo...  6.64 us
    unnamed x6, local copies, waits for them, and re-layouts  0.68 us
  transfers between devices with their start and end apart: 10, of which 6 were waited for; matrix products, arithmetic and copies ran while one was open for 0% of the time, Pallas kernels for 13%

profile of v7, /device:TPU:0, one launch (start us, length us, event | category | flops | bytes accessed | tf_op | source)
XLA Modules:
  0.0 29.9 jit_solution(9533432655720400595)
XLA Ops:
  0.6 0.5 %collective-permute-start.1 = (f32[32,128]{1,0:T(8,128)}, f32[32,128]{1,0:T(8,128)S(1)}, u32[]{:S(2)}, u32[]{:S(2)}) collective-permute-start(f32[32,128]{1,0:T(8,128)} %vec_hbm.1), channel_id=1, source_target_pairs={{0,1},{1,0},{2,3},{3,2},{4,5},{5,4},{6,7},{7,6},{8,9},{9,8},{10,11... | collective-permute-start | bytes 49160 | tf_op jit(solution)/shard_map/ppermute | solution.py:15
  1.1 0.1 collective-permute-start
  1.2 0.8 %prepare.1 = (f32[56,128]{1,0:T(8,128)S(1)}, f32[56,128]{1,0:T(8,128)S(1)}, s32[8,128]{1,0:T(8,128)S(1)}) custom-call(s32[4]{0:T(128)} %blocks_hbm.1, f32[20,128]{1,0:T(8,128)} %in_hbm.1, f32[32,128]{1,0:T(8,128)} %vec_hbm.1, f32[32,128]{1,0:T(8,128)} %probes_hbm.1), custom_call_target="tpu_custom_call" | custom-call | flops 100000000 | bytes 1000000 | tf_op jit(solution)/shard_map/prepare/pallas_call | solution.py:449
  2.0 0.5 %collective-permute-done.far_in = f32[20,128]{1,0:T(8,128)S(1)} collective-permute-done((f32[20,128]{1,0:T(8,128)}, f32[20,128]{1,0:T(8,128)S(1)}, u32[]{:S(2)}, u32[]{:S(2)}) %collective-permute-start) | collective-permute-done | bytes 10272 | tf_op jit(solution)/shard_map/ppermute | solution.py:15
  2.5 0.0 collective-permute-done.1.far_vec
  2.6 0.0 copy-start
  2.6 0.0 copy-start.1
  2.6 2.7 %collective-permute-start.2 = (f32[112,128]{1,0:T(8,128)S(1)}, f32[112,128]{1,0:T(8,128)S(1)}, u32[]{:S(2)}, u32[]{:S(2)}) collective-permute-start(f32[112,128]{1,0:T(8,128)S(1)} %pad_maximum_fusion.1), channel_id=1, source_target_pairs={{0,2},{1,3},{2,0},{3,1},{4,6},{5,7},{6,4},{7,5},{8,10},{9,11},{10,... | collective-permute-start | bytes 172040 | tf_op jit(solution)/shard_map/ppermute | solution.py:15
  5.3 0.0 copy-start.2
  5.3 0.0 copy-done
  5.3 0.0 copy-done.1
  5.3 0.7 %copy-done.2 = f32[256]{0:T(256)S(1)} copy-done((f32[256]{0:T(256)S(1)}, f32[256]{0:T(256)}, u32[]{:S(2)}) %copy-start.2) | copy-done | bytes 1048
  6.0 0.1 weights.1
  6.1 1.6 %collective-permute-done.2 = f32[112,128]{1,0:T(8,128)S(1)} collective-permute-done((f32[112,128]{1,0:T(8,128)S(1)}, f32[112,128]{1,0:T(8,128)S(1)}, u32[]{:S(2)}, u32[]{:S(2)}) %collective-permute-start.2) | collective-permute-done | bytes 57376 | tf_op jit(solution)/shard_map/ppermute | solution.py:15
  7.7 1.8 %collective-permute-start.3 = (f32[56,128]{1,0:T(8,128)S(1)}, f32[56,128]{1,0:T(8,128)S(1)}, u32[]{:S(2)}, u32[]{:S(2)}) collective-permute-start(f32[56,128]{1,0:T(8,128)S(1)} %get-tuple-element.69), channel_id=1, source_target_pairs={{0,4},{1,5},{2,6},{3,7},{4,0},{5,1},{6,2},{7,3},{8,12},{9,13},{10,... | collective-permute-start | bytes 86024 | tf_op jit(solution)/shard_map/ppermute | solution.py:15
  9.5 2.6 %collective-permute-start.6 = (f32[112,128]{1,0:T(8,128)S(1)}, f32[112,128]{1,0:T(8,128)S(1)}, u32[]{:S(2)}, u32[]{:S(2)}) collective-permute-start(f32[112,128]{1,0:T(8,128)S(1)} %pad_maximum_fusion.3), channel_id=1, source_target_pairs={{0,16},{8,24},{16,0},{24,8},{1,17},{9,25},{17,1},{25,9},{2,18},{10... | collective-permute-start | bytes 172040 | tf_op jit(solution)/shard_map/ppermute | solution.py:15
  12.1 0.0 collective-permute-done.3
  12.1 2.3 %collective-permute-start.4 = (f32[56,128]{1,0:T(8,128)S(1)}, f32[56,128]{1,0:T(8,128)S(1)}, u32[]{:S(2)}, u32[]{:S(2)}) collective-permute-start(f32[56,128]{1,0:T(8,128)S(1)} %broadcast_select_fusion), channel_id=1, source_target_pairs={{0,16},{8,24},{16,0},{24,8},{1,17},{9,25},{17,1},{25,9},{2,18},{10... | collective-permute-start | bytes 86024 | tf_op jit(solution)/shard_map/ppermute | solution.py:15
  14.5 0.4 %collective-permute-done.6 = f32[112,128]{1,0:T(8,128)S(1)} collective-permute-done((f32[112,128]{1,0:T(8,128)S(1)}, f32[112,128]{1,0:T(8,128)S(1)}, u32[]{:S(2)}, u32[]{:S(2)}) %collective-permute-start.6) | collective-permute-done | bytes 57376 | tf_op jit(solution)/shard_map/ppermute | solution.py:15
  14.9 1.6 %collective-permute-start.7 = (f32[224,128]{1,0:T(8,128)S(1)}, f32[224,128]{1,0:T(8,128)S(1)}, u32[]{:S(2)}, u32[]{:S(2)}) collective-permute-start(f32[224,128]{1,0:T(8,128)S(1)} %pad_maximum_fusion.columns_ref), channel_id=1, source_target_pairs={{0,8},{8,0},{16,24},{24,16},{1,9},{9,1},{17,25},{25,17},{2,10},{10... | collective-permute-start | bytes 344072 | tf_op jit(solution)/shard_map/ppermute | solution.py:15
  16.5 0.4 %collective-permute-done.4 = f32[56,128]{1,0:T(8,128)S(1)} collective-permute-done((f32[56,128]{1,0:T(8,128)S(1)}, f32[56,128]{1,0:T(8,128)S(1)}, u32[]{:S(2)}, u32[]{:S(2)}) %collective-permute-start.4) | collective-permute-done | bytes 28704 | tf_op jit(solution)/shard_map/ppermute | solution.py:15
  17.0 1.9 %collective-permute-start.5 = (f32[112,128]{1,0:T(8,128)S(1)}, f32[112,128]{1,0:T(8,128)S(1)}, u32[]{:S(2)}, u32[]{:S(2)}) collective-permute-start(f32[112,128]{1,0:T(8,128)S(1)} %pad_maximum_fusion.2.windows_ref), channel_id=1, source_target_pairs={{0,8},{8,0},{16,24},{24,16},{1,9},{9,1},{17,25},{25,17},{2,10},{10... | collective-permute-start | bytes 172040 | tf_op jit(solution)/shard_map/ppermute | solution.py:15
  18.9 1.2 %near.1 = (f32[24,256]{1,0:T(8,128)S(1)}, bf16[256,256]{1,0:T(8,128)(2,1)S(1)}, bf16[256,256]{1,0:T(8,128)(2,1)S(1)}, bf16[144,256]{1,0:T(8,128)(2,1)S(1)}, bf16...) custom-call(f32[112,128]{1,0:T(8,128)S(1)} %pad_maximum_fusion.2.win, ...), custom_call_target="tpu_custom_call" | custom-call | flops 1000000000 | bytes 1000000 | tf_op jit(solution)/shard_map/near/pallas_call | solution.py:449
  20.0 0.0 collective-permute-done.7.columns_ref
  20.1 1.2 %far.1 = (f32[24,512]{1,0:T(8,128)S(1)}, bf16[512,256]{1,0:T(8,128)(2,1)S(1)}, bf16[512,256]{1,0:T(8,128)(2,1)S(1)}, f32[512,256]{1,0:T(8,128)S(1)}, bf16[512,12...) custom-call(f32[224,128]{1,0:T(8,128)S(1)} %collective-permute-done., ...), custom_call_target="tpu_custom_call" | custom-call | flops 1000000000 | bytes 1000000 | tf_op jit(solution)/shard_map/far/pallas_call | solution.py:449
  21.2 0.0 collective-permute-done.5.windows_ref
  21.2 2.1 %late.1 = (f32[64,128]{1,0:T(8,128)S(1)}, f32[88,256]{1,0:T(8,128)S(1)}) custom-call(f32[112,128]{1,0:T(8,128)S(1)} %collective-permute-done.5.windows_ref, bf16[144,256]{1,0:T(8,128)(2,1)S(1)} %get-tuple-element.70.refs_0_, bf16[512,128]{1,0:T(8,128)(2,1)S(1)} %get-tuple-element.71.refs_1_, bf16[256,256]{1,0:T(8,128)(2,1)S(1)} %get-tuple-element.72.refs_2_, ...), custom_call_target="tpu_custom_call" | custom-call | flops 2000000000 | bytes 1000000 | tf_op jit(solution)/shard_map/late/pallas_call | solution.py:449
  23.3 1.2 %collective-permute-start.8 = (f32[88,256]{1,0:T(8,128)S(1)}, f32[88,256]{1,0:T(8,128)S(1)}, u32[]{:S(2)}, u32[]{:S(2)}) collective-permute-start(f32[88,256]{1,0:T(8,128)S(1)} %get-tuple-element.104), channel_id=1, source_target_pairs={{0,4},{1,5},{2,6},{3,7},{4,0},{5,1},{6,2},{7,3},{8,12},{9,13},{10,... | collective-permute-start | bytes 270344 | tf_op jit(solution)/shard_map/ppermute | solution.py:15
  24.5 3.4 %collective-permute-done.8 = f32[88,256]{1,0:T(8,128)S(1)} collective-permute-done((f32[88,256]{1,0:T(8,128)S(1)}, f32[88,256]{1,0:T(8,128)S(1)}, u32[]{:S(2)}, u32[]{:S(2)}) %collective-permute-start.8) | collective-permute-done | bytes 90144 | tf_op jit(solution)/shard_map/ppermute | solution.py:15
  27.9 0.1 collective-permute-start.9
  28.0 0.6 %emit.1 = f32[64,128]{1,0:T(8,128)} custom-call(f32[64,128]{1,0:T(8,128)S(1)} %get-tuple-element.103.own_ref), custom_call_target="tpu_custom_call" | custom-call | flops 100000000 | bytes 1000000 | tf_op jit(solution)/shard_map/emit/pallas_call | solution.py:449
  28.6 0.7 %collective-permute-done.9.theirs_ref = f32[88,256]{1,0:T(8,128)S(1)} collective-permute-done((f32[88,256]{1,0:T(8,128)S(1)}, f32[88,256]{1,0:T(8,128)S(1)}, u32[]{:S(2)}, u32[]{:S(2)}) %collective-permute-start.9) | collective-permute-done | bytes 90144 | tf_op jit(solution)/shard_map/ppermute | solution.py:15
  29.3 0.6 %finish.1 = (f32[20,256]{1,0:T(8,128)}, f32[1,256]{1,0:T(1,128)}, f32[64,256]{1,0:T(8,128)}) custom-call(f32[88,256]{1,0:T(8,128)S(1)} %add.3.mine_ref, f32[88,256]{1,0:T(8,128)S(1)} %collective-permute-done.9.theirs_ref), custom_call_target="tpu_custom_call" | custom-call | flops 100000000 | bytes 1000000 | tf_op jit(solution)/shard_map/finish/pallas_call | solution.py:449
  (9 shorter events, 0.1 us)
Async XLA Ops:
  0.6 1.9 %collective-permute-start.1 = (f32[32,128]{1,0:T(8,128)}, f32[32,128]{1,0:T(8,128)S(1)}, u32[]{:S(2)}, u32[]{:S(2)}) collective-permute-start(f32[32,128]{1,0:T(8,128)} %vec_hbm.1), channel_id=1, source_target_pairs={{0,1},{1,0},{2,3},{3,2},{4,5},{5,4},{6,7},{7,6},{8,9},{9,8},{10,11... | collective-permute-start | bytes 49160 | tf_op jit(solution)/shard_map/ppermute | solution.py:15
  1.1 1.4 %collective-permute-start = (f32[20,128]{1,0:T(8,128)}, f32[20,128]{1,0:T(8,128)S(1)}, u32[]{:S(2)}, u32[]{:S(2)}) collective-permute-start(f32[20,128]{1,0:T(8,128)} %in_hbm.1), channel_id=1, source_target_pairs={{0,1},{1,0},{2,3},{3,2},{4,5},{5,4},{6,7},{7,6},{8,9},{9,8},{10,11... | collective-permute-start | bytes 30728 | tf_op jit(solution)/shard_map/ppermute | solution.py:15
  2.6 2.8 %copy-start = (f32[256,64]{0,1:T(8,128)S(1)}, f32[256,64]{0,1:T(8,128)}, u32[]{:S(2)}) copy-start(f32[256,64]{0,1:T(8,128)} %param.10) | copy-start | bytes 196612
  2.6 2.8 %copy-start.1 = (f32[20,256]{1,0:T(8,128)S(1)}, f32[20,256]{1,0:T(8,128)}, u32[]{:S(2)}) copy-start(f32[20,256]{1,0:T(8,128)} %param.8) | copy-start | bytes 61444
  2.6 5.1 %collective-permute-start.2 = (f32[112,128]{1,0:T(8,128)S(1)}, f32[112,128]{1,0:T(8,128)S(1)}, u32[]{:S(2)}, u32[]{:S(2)}) collective-permute-start(f32[112,128]{1,0:T(8,128)S(1)} %pad_maximum_fusion.1), channel_id=1, source_target_pairs={{0,2},{1,3},{2,0},{3,1},{4,6},{5,7},{6,4},{7,5},{8,10},{9,11},{10,... | collective-permute-start | bytes 172040 | tf_op jit(solution)/shard_map/ppermute | solution.py:15
  5.3 0.7 %copy-start.2 = (f32[256]{0:T(256)S(1)}, f32[256]{0:T(256)}, u32[]{:S(2)}) copy-start(f32[256]{0:T(256)} %param.9) | copy-start | bytes 3076
  7.7 4.4 %collective-permute-start.3 = (f32[56,128]{1,0:T(8,128)S(1)}, f32[56,128]{1,0:T(8,128)S(1)}, u32[]{:S(2)}, u32[]{:S(2)}) collective-permute-start(f32[56,128]{1,0:T(8,128)S(1)} %get-tuple-element.69), channel_id=1, source_target_pairs={{0,4},{1,5},{2,6},{3,7},{4,0},{5,1},{6,2},{7,3},{8,12},{9,13},{10,... | collective-permute-start | bytes 86024 | tf_op jit(solution)/shard_map/ppermute | solution.py:15
  9.5 5.4 %collective-permute-start.6 = (f32[112,128]{1,0:T(8,128)S(1)}, f32[112,128]{1,0:T(8,128)S(1)}, u32[]{:S(2)}, u32[]{:S(2)}) collective-permute-start(f32[112,128]{1,0:T(8,128)S(1)} %pad_maximum_fusion.3), channel_id=1, source_target_pairs={{0,16},{8,24},{16,0},{24,8},{1,17},{9,25},{17,1},{25,9},{2,18},{10... | collective-permute-start | bytes 172040 | tf_op jit(solution)/shard_map/ppermute | solution.py:15
  12.1 4.8 %collective-permute-start.4 = (f32[56,128]{1,0:T(8,128)S(1)}, f32[56,128]{1,0:T(8,128)S(1)}, u32[]{:S(2)}, u32[]{:S(2)}) collective-permute-start(f32[56,128]{1,0:T(8,128)S(1)} %broadcast_select_fusion), channel_id=1, source_target_pairs={{0,16},{8,24},{16,0},{24,8},{1,17},{9,25},{17,1},{25,9},{2,18},{10... | collective-permute-start | bytes 86024 | tf_op jit(solution)/shard_map/ppermute | solution.py:15
  14.9 5.1 %collective-permute-start.7 = (f32[224,128]{1,0:T(8,128)S(1)}, f32[224,128]{1,0:T(8,128)S(1)}, u32[]{:S(2)}, u32[]{:S(2)}) collective-permute-start(f32[224,128]{1,0:T(8,128)S(1)} %pad_maximum_fusion.columns_ref), channel_id=1, source_target_pairs={{0,8},{8,0},{16,24},{24,16},{1,9},{9,1},{17,25},{25,17},{2,10},{10... | collective-permute-start | bytes 344072 | tf_op jit(solution)/shard_map/ppermute | solution.py:15
  17.0 4.2 %collective-permute-start.5 = (f32[112,128]{1,0:T(8,128)S(1)}, f32[112,128]{1,0:T(8,128)S(1)}, u32[]{:S(2)}, u32[]{:S(2)}) collective-permute-start(f32[112,128]{1,0:T(8,128)S(1)} %pad_maximum_fusion.2.windows_ref), channel_id=1, source_target_pairs={{0,8},{8,0},{16,24},{24,16},{1,9},{9,1},{17,25},{25,17},{2,10},{10... | collective-permute-start | bytes 172040 | tf_op jit(solution)/shard_map/ppermute | solution.py:15
  23.3 4.6 %collective-permute-start.8 = (f32[88,256]{1,0:T(8,128)S(1)}, f32[88,256]{1,0:T(8,128)S(1)}, u32[]{:S(2)}, u32[]{:S(2)}) collective-permute-start(f32[88,256]{1,0:T(8,128)S(1)} %get-tuple-element.104), channel_id=1, source_target_pairs={{0,4},{1,5},{2,6},{3,7},{4,0},{5,1},{6,2},{7,3},{8,12},{9,13},{10,... | collective-permute-start | bytes 270344 | tf_op jit(solution)/shard_map/ppermute | solution.py:15
  27.9 1.4 %collective-permute-start.9 = (f32[88,256]{1,0:T(8,128)S(1)}, f32[88,256]{1,0:T(8,128)S(1)}, u32[]{:S(2)}, u32[]{:S(2)}) collective-permute-start(f32[88,256]{1,0:T(8,128)S(1)} %add.3.mine_ref), channel_id=1, source_target_pairs={{0,1},{1,0},{2,3},{3,2},{4,5},{5,4},{6,7},{7,6},{8,9},{9,8},{10,11... | collective-permute-start | bytes 270344 | tf_op jit(solution)/shard_map/ppermute | solution.py:15

commit v8 on v7

--- a/solution.py
+++ b/solution.py
@@ -294,8 +294,8 @@
     def first(here, terms):
         t_stack, pair = terms
         g = mm(beside([pair, pair]), w.back[...])
-        both = mm(beside([t_stack, t_stack]), jnp.concatenate([s.h1[here, :], s.h2[here, :]], 0))
-        pack_ref[: z.feats] += both[: z.feats] + both[z.feats :]
+        both = mm(t_stack, s.h1[here, :])
+        pack_ref[: z.feats] += both[: z.feats] + both[z.feats :] + mm(t_stack[: z.feats], s.h2[here, :])
         return g
 
     def second(here, g):

time: 30.2 us -> 30.2 us (level)
  no operation moved by 1% of the time
where the time goes in v8:
time: 30.2 us; the launch traced here: 29.9 us
  starting transfers between devices  14.8 us (49%)
  waiting for transfers between devices  6.97 us (23%)
  Pallas kernels  6.63 us (22%)
  between operations  0.74 us (2%)
  local copies, waits for them, and re-layouts  0.68 us (2%)
    ppermute x10, starting transfers between devices, swap(): return lax.ppermute(value, axis, [(i, i ^ bit) for i in range(size)])  14.8 us
    ppermute x10, waiting for transfers between devices, swap(): return lax.ppermute(value, axis, [(i, i ^ bit) for i in range(size)])  6.97 us
    pallas_call x8, Pallas kernels, call(): pl.pallas_call(kernel, out_shape=tuple(outs), in_specs=[pl.BlockSpec(memo...  6.63 us
    unnamed x6, local copies, waits for them, and re-layouts  0.68 us
  transfers between devices with their start and end apart: 10, of which 6 were waited for; matrix products, arithmetic and copies ran while one was open for 0% of the time, Pallas kernels for 13%

profile of v8, /device:TPU:0, one launch (start us, length us, event | category | flops | bytes accessed | tf_op | source)
XLA Modules:
  0.0 29.9 jit_solution(14124064143676922164)
XLA Ops:
  0.6 0.5 %collective-permute-start.1 = (f32[32,128]{1,0:T(8,128)}, f32[32,128]{1,0:T(8,128)S(1)}, u32[]{:S(2)}, u32[]{:S(2)}) collective-permute-start(f32[32,128]{1,0:T(8,128)} %vec_hbm.1), channel_id=1, source_target_pairs={{0,1},{1,0},{2,3},{3,2},{4,5},{5,4},{6,7},{7,6},{8,9},{9,8},{10,11... | collective-permute-start | bytes 49160 | tf_op jit(solution)/shard_map/ppermute | solution.py:15
  1.1 0.1 collective-permute-start
  1.2 0.8 %prepare.1 = (f32[56,128]{1,0:T(8,128)S(1)}, f32[56,128]{1,0:T(8,128)S(1)}, s32[8,128]{1,0:T(8,128)S(1)}) custom-call(s32[4]{0:T(128)} %blocks_hbm.1, f32[20,128]{1,0:T(8,128)} %in_hbm.1, f32[32,128]{1,0:T(8,128)} %vec_hbm.1, f32[32,128]{1,0:T(8,128)} %probes_hbm.1), custom_call_target="tpu_custom_call" | custom-call | flops 100000000 | bytes 1000000 | tf_op jit(solution)/shard_map/prepare/pallas_call | solution.py:449
  2.0 0.5 %collective-permute-done.far_in = f32[20,128]{1,0:T(8,128)S(1)} collective-permute-done((f32[20,128]{1,0:T(8,128)}, f32[20,128]{1,0:T(8,128)S(1)}, u32[]{:S(2)}, u32[]{:S(2)}) %collective-permute-start) | collective-permute-done | bytes 10272 | tf_op jit(solution)/shard_map/ppermute | solution.py:15
  2.5 0.0 collective-permute-done.1.far_vec
  2.6 0.0 copy-start
  2.6 0.0 copy-start.1
  2.6 2.7 %collective-permute-start.2 = (f32[112,128]{1,0:T(8,128)S(1)}, f32[112,128]{1,0:T(8,128)S(1)}, u32[]{:S(2)}, u32[]{:S(2)}) collective-permute-start(f32[112,128]{1,0:T(8,128)S(1)} %pad_maximum_fusion.1), channel_id=1, source_target_pairs={{0,2},{1,3},{2,0},{3,1},{4,6},{5,7},{6,4},{7,5},{8,10},{9,11},{10,... | collective-permute-start | bytes 172040 | tf_op jit(solution)/shard_map/ppermute | solution.py:15
  5.3 0.0 copy-start.2
  5.3 0.0 copy-done
  5.3 0.0 copy-done.1
  5.3 0.7 %copy-done.2 = f32[256]{0:T(256)S(1)} copy-done((f32[256]{0:T(256)S(1)}, f32[256]{0:T(256)}, u32[]{:S(2)}) %copy-start.2) | copy-done | bytes 1048
  6.0 0.1 weights.1
  6.1 1.6 %collective-permute-done.2 = f32[112,128]{1,0:T(8,128)S(1)} collective-permute-done((f32[112,128]{1,0:T(8,128)S(1)}, f32[112,128]{1,0:T(8,128)S(1)}, u32[]{:S(2)}, u32[]{:S(2)}) %collective-permute-start.2) | collective-permute-done | bytes 57376 | tf_op jit(solution)/shard_map/ppermute | solution.py:15
  7.7 1.8 %collective-permute-start.3 = (f32[56,128]{1,0:T(8,128)S(1)}, f32[56,128]{1,0:T(8,128)S(1)}, u32[]{:S(2)}, u32[]{:S(2)}) collective-permute-start(f32[56,128]{1,0:T(8,128)S(1)} %get-tuple-element.69), channel_id=1, source_target_pairs={{0,4},{1,5},{2,6},{3,7},{4,0},{5,1},{6,2},{7,3},{8,12},{9,13},{10,... | collective-permute-start | bytes 86024 | tf_op jit(solution)/shard_map/ppermute | solution.py:15
  9.5 2.6 %collective-permute-start.6 = (f32[112,128]{1,0:T(8,128)S(1)}, f32[112,128]{1,0:T(8,128)S(1)}, u32[]{:S(2)}, u32[]{:S(2)}) collective-permute-start(f32[112,128]{1,0:T(8,128)S(1)} %pad_maximum_fusion.3), channel_id=1, source_target_pairs={{0,16},{8,24},{16,0},{24,8},{1,17},{9,25},{17,1},{25,9},{2,18},{10... | collective-permute-start | bytes 172040 | tf_op jit(solution)/shard_map/ppermute | solution.py:15
  12.1 0.0 collective-permute-done.3
  12.1 2.3 %collective-permute-start.4 = (f32[56,128]{1,0:T(8,128)S(1)}, f32[56,128]{1,0:T(8,128)S(1)}, u32[]{:S(2)}, u32[]{:S(2)}) collective-permute-start(f32[56,128]{1,0:T(8,128)S(1)} %broadcast_select_fusion), channel_id=1, source_target_pairs={{0,16},{8,24},{16,0},{24,8},{1,17},{9,25},{17,1},{25,9},{2,18},{10... | collective-permute-start | bytes 86024 | tf_op jit(solution)/shard_map/ppermute | solution.py:15
  14.5 0.4 %collective-permute-done.6 = f32[112,128]{1,0:T(8,128)S(1)} collective-permute-done((f32[112,128]{1,0:T(8,128)S(1)}, f32[112,128]{1,0:T(8,128)S(1)}, u32[]{:S(2)}, u32[]{:S(2)}) %collective-permute-start.6) | collective-permute-done | bytes 57376 | tf_op jit(solution)/shard_map/ppermute | solution.py:15
  14.9 1.6 %collective-permute-start.7 = (f32[224,128]{1,0:T(8,128)S(1)}, f32[224,128]{1,0:T(8,128)S(1)}, u32[]{:S(2)}, u32[]{:S(2)}) collective-permute-start(f32[224,128]{1,0:T(8,128)S(1)} %pad_maximum_fusion.columns_ref), channel_id=1, source_target_pairs={{0,8},{8,0},{16,24},{24,16},{1,9},{9,1},{17,25},{25,17},{2,10},{10... | collective-permute-start | bytes 344072 | tf_op jit(solution)/shard_map/ppermute | solution.py:15
  16.5 0.4 %collective-permute-done.4 = f32[56,128]{1,0:T(8,128)S(1)} collective-permute-done((f32[56,128]{1,0:T(8,128)S(1)}, f32[56,128]{1,0:T(8,128)S(1)}, u32[]{:S(2)}, u32[]{:S(2)}) %collective-permute-start.4) | collective-permute-done | bytes 28704 | tf_op jit(solution)/shard_map/ppermute | solution.py:15
  17.0 1.9 %collective-permute-start.5 = (f32[112,128]{1,0:T(8,128)S(1)}, f32[112,128]{1,0:T(8,128)S(1)}, u32[]{:S(2)}, u32[]{:S(2)}) collective-permute-start(f32[112,128]{1,0:T(8,128)S(1)} %pad_maximum_fusion.2.windows_ref), channel_id=1, source_target_pairs={{0,8},{8,0},{16,24},{24,16},{1,9},{9,1},{17,25},{25,17},{2,10},{10... | collective-permute-start | bytes 172040 | tf_op jit(solution)/shard_map/ppermute | solution.py:15
  18.9 1.2 %near.1 = (f32[24,256]{1,0:T(8,128)S(1)}, bf16[256,256]{1,0:T(8,128)(2,1)S(1)}, bf16[256,256]{1,0:T(8,128)(2,1)S(1)}, bf16[144,256]{1,0:T(8,128)(2,1)S(1)}, bf16...) custom-call(f32[112,128]{1,0:T(8,128)S(1)} %pad_maximum_fusion.2.win, ...), custom_call_target="tpu_custom_call" | custom-call | flops 1000000000 | bytes 1000000 | tf_op jit(solution)/shard_map/near/pallas_call | solution.py:449
  20.0 0.0 collective-permute-done.7.columns_ref
  20.1 1.2 %far.1 = (f32[24,512]{1,0:T(8,128)S(1)}, bf16[512,256]{1,0:T(8,128)(2,1)S(1)}, bf16[512,256]{1,0:T(8,128)(2,1)S(1)}, f32[512,256]{1,0:T(8,128)S(1)}, bf16[512,12...) custom-call(f32[224,128]{1,0:T(8,128)S(1)} %collective-permute-done., ...), custom_call_target="tpu_custom_call" | custom-call | flops 1000000000 | bytes 1000000 | tf_op jit(solution)/shard_map/far/pallas_call | solution.py:449
  21.2 0.0 collective-permute-done.5.windows_ref
  21.2 2.1 %late.1 = (f32[64,128]{1,0:T(8,128)S(1)}, f32[88,256]{1,0:T(8,128)S(1)}) custom-call(f32[112,128]{1,0:T(8,128)S(1)} %collective-permute-done.5.windows_ref, bf16[144,256]{1,0:T(8,128)(2,1)S(1)} %get-tuple-element.70.refs_0_, bf16[512,128]{1,0:T(8,128)(2,1)S(1)} %get-tuple-element.71.refs_1_, bf16[256,256]{1,0:T(8,128)(2,1)S(1)} %get-tuple-element.72.refs_2_, ...), custom_call_target="tpu_custom_call" | custom-call | flops 2000000000 | bytes 1000000 | tf_op jit(solution)/shard_map/late/pallas_call | solution.py:449
  23.3 1.2 %collective-permute-start.8 = (f32[88,256]{1,0:T(8,128)S(1)}, f32[88,256]{1,0:T(8,128)S(1)}, u32[]{:S(2)}, u32[]{:S(2)}) collective-permute-start(f32[88,256]{1,0:T(8,128)S(1)} %get-tuple-element.104), channel_id=1, source_target_pairs={{0,4},{1,5},{2,6},{3,7},{4,0},{5,1},{6,2},{7,3},{8,12},{9,13},{10,... | collective-permute-start | bytes 270344 | tf_op jit(solution)/shard_map/ppermute | solution.py:15
  24.5 3.4 %collective-permute-done.8 = f32[88,256]{1,0:T(8,128)S(1)} collective-permute-done((f32[88,256]{1,0:T(8,128)S(1)}, f32[88,256]{1,0:T(8,128)S(1)}, u32[]{:S(2)}, u32[]{:S(2)}) %collective-permute-start.8) | collective-permute-done | bytes 90144 | tf_op jit(solution)/shard_map/ppermute | solution.py:15
  27.9 0.1 collective-permute-start.9
  28.0 0.6 %emit.1 = f32[64,128]{1,0:T(8,128)} custom-call(f32[64,128]{1,0:T(8,128)S(1)} %get-tuple-element.103.own_ref), custom_call_target="tpu_custom_call" | custom-call | flops 100000000 | bytes 1000000 | tf_op jit(solution)/shard_map/emit/pallas_call | solution.py:449
  28.6 0.7 %collective-permute-done.9.theirs_ref = f32[88,256]{1,0:T(8,128)S(1)} collective-permute-done((f32[88,256]{1,0:T(8,128)S(1)}, f32[88,256]{1,0:T(8,128)S(1)}, u32[]{:S(2)}, u32[]{:S(2)}) %collective-permute-start.9) | collective-permute-done | bytes 90144 | tf_op jit(solution)/shard_map/ppermute | solution.py:15
  29.3 0.6 %finish.1 = (f32[20,256]{1,0:T(8,128)}, f32[1,256]{1,0:T(1,128)}, f32[64,256]{1,0:T(8,128)}) custom-call(f32[88,256]{1,0:T(8,128)S(1)} %add.3.mine_ref, f32[88,256]{1,0:T(8,128)S(1)} %collective-permute-done.9.theirs_ref), custom_call_target="tpu_custom_call" | custom-call | flops 100000000 | bytes 1000000 | tf_op jit(solution)/shard_map/finish/pallas_call | solution.py:449
  (9 shorter events, 0.1 us)
Async XLA Ops:
  0.6 1.9 %collective-permute-start.1 = (f32[32,128]{1,0:T(8,128)}, f32[32,128]{1,0:T(8,128)S(1)}, u32[]{:S(2)}, u32[]{:S(2)}) collective-permute-start(f32[32,128]{1,0:T(8,128)} %vec_hbm.1), channel_id=1, source_target_pairs={{0,1},{1,0},{2,3},{3,2},{4,5},{5,4},{6,7},{7,6},{8,9},{9,8},{10,11... | collective-permute-start | bytes 49160 | tf_op jit(solution)/shard_map/ppermute | solution.py:15
  1.1 1.4 %collective-permute-start = (f32[20,128]{1,0:T(8,128)}, f32[20,128]{1,0:T(8,128)S(1)}, u32[]{:S(2)}, u32[]{:S(2)}) collective-permute-start(f32[20,128]{1,0:T(8,128)} %in_hbm.1), channel_id=1, source_target_pairs={{0,1},{1,0},{2,3},{3,2},{4,5},{5,4},{6,7},{7,6},{8,9},{9,8},{10,11... | collective-permute-start | bytes 30728 | tf_op jit(solution)/shard_map/ppermute | solution.py:15
  2.6 2.8 %copy-start = (f32[256,64]{0,1:T(8,128)S(1)}, f32[256,64]{0,1:T(8,128)}, u32[]{:S(2)}) copy-start(f32[256,64]{0,1:T(8,128)} %param.10) | copy-start | bytes 196612
  2.6 2.8 %copy-start.1 = (f32[20,256]{1,0:T(8,128)S(1)}, f32[20,256]{1,0:T(8,128)}, u32[]{:S(2)}) copy-start(f32[20,256]{1,0:T(8,128)} %param.8) | copy-start | bytes 61444
  2.6 5.1 %collective-permute-start.2 = (f32[112,128]{1,0:T(8,128)S(1)}, f32[112,128]{1,0:T(8,128)S(1)}, u32[]{:S(2)}, u32[]{:S(2)}) collective-permute-start(f32[112,128]{1,0:T(8,128)S(1)} %pad_maximum_fusion.1), channel_id=1, source_target_pairs={{0,2},{1,3},{2,0},{3,1},{4,6},{5,7},{6,4},{7,5},{8,10},{9,11},{10,... | collective-permute-start | bytes 172040 | tf_op jit(solution)/shard_map/ppermute | solution.py:15
  5.3 0.7 %copy-start.2 = (f32[256]{0:T(256)S(1)}, f32[256]{0:T(256)}, u32[]{:S(2)}) copy-start(f32[256]{0:T(256)} %param.9) | copy-start | bytes 3076
  7.7 4.4 %collective-permute-start.3 = (f32[56,128]{1,0:T(8,128)S(1)}, f32[56,128]{1,0:T(8,128)S(1)}, u32[]{:S(2)}, u32[]{:S(2)}) collective-permute-start(f32[56,128]{1,0:T(8,128)S(1)} %get-tuple-element.69), channel_id=1, source_target_pairs={{0,4},{1,5},{2,6},{3,7},{4,0},{5,1},{6,2},{7,3},{8,12},{9,13},{10,... | collective-permute-start | bytes 86024 | tf_op jit(solution)/shard_map/ppermute | solution.py:15
  9.5 5.4 %collective-permute-start.6 = (f32[112,128]{1,0:T(8,128)S(1)}, f32[112,128]{1,0:T(8,128)S(1)}, u32[]{:S(2)}, u32[]{:S(2)}) collective-permute-start(f32[112,128]{1,0:T(8,128)S(1)} %pad_maximum_fusion.3), channel_id=1, source_target_pairs={{0,16},{8,24},{16,0},{24,8},{1,17},{9,25},{17,1},{25,9},{2,18},{10... | collective-permute-start | bytes 172040 | tf_op jit(solution)/shard_map/ppermute | solution.py:15
  12.1 4.8 %collective-permute-start.4 = (f32[56,128]{1,0:T(8,128)S(1)}, f32[56,128]{1,0:T(8,128)S(1)}, u32[]{:S(2)}, u32[]{:S(2)}) collective-permute-start(f32[56,128]{1,0:T(8,128)S(1)} %broadcast_select_fusion), channel_id=1, source_target_pairs={{0,16},{8,24},{16,0},{24,8},{1,17},{9,25},{17,1},{25,9},{2,18},{10... | collective-permute-start | bytes 86024 | tf_op jit(solution)/shard_map/ppermute | solution.py:15
  14.9 5.1 %collective-permute-start.7 = (f32[224,128]{1,0:T(8,128)S(1)}, f32[224,128]{1,0:T(8,128)S(1)}, u32[]{:S(2)}, u32[]{:S(2)}) collective-permute-start(f32[224,128]{1,0:T(8,128)S(1)} %pad_maximum_fusion.columns_ref), channel_id=1, source_target_pairs={{0,8},{8,0},{16,24},{24,16},{1,9},{9,1},{17,25},{25,17},{2,10},{10... | collective-permute-start | bytes 344072 | tf_op jit(solution)/shard_map/ppermute | solution.py:15
  17.0 4.2 %collective-permute-start.5 = (f32[112,128]{1,0:T(8,128)S(1)}, f32[112,128]{1,0:T(8,128)S(1)}, u32[]{:S(2)}, u32[]{:S(2)}) collective-permute-start(f32[112,128]{1,0:T(8,128)S(1)} %pad_maximum_fusion.2.windows_ref), channel_id=1, source_target_pairs={{0,8},{8,0},{16,24},{24,16},{1,9},{9,1},{17,25},{25,17},{2,10},{10... | collective-permute-start | bytes 172040 | tf_op jit(solution)/shard_map/ppermute | solution.py:15
  23.3 4.6 %collective-permute-start.8 = (f32[88,256]{1,0:T(8,128)S(1)}, f32[88,256]{1,0:T(8,128)S(1)}, u32[]{:S(2)}, u32[]{:S(2)}) collective-permute-start(f32[88,256]{1,0:T(8,128)S(1)} %get-tuple-element.104), channel_id=1, source_target_pairs={{0,4},{1,5},{2,6},{3,7},{4,0},{5,1},{6,2},{7,3},{8,12},{9,13},{10,... | collective-permute-start | bytes 270344 | tf_op jit(solution)/shard_map/ppermute | solution.py:15
  27.9 1.4 %collective-permute-start.9 = (f32[88,256]{1,0:T(8,128)S(1)}, f32[88,256]{1,0:T(8,128)S(1)}, u32[]{:S(2)}, u32[]{:S(2)}) collective-permute-start(f32[88,256]{1,0:T(8,128)S(1)} %add.3.mine_ref), channel_id=1, source_target_pairs={{0,1},{1,0},{2,3},{3,2},{4,5},{5,4},{6,7},{7,6},{8,9},{9,8},{10,11... | collective-permute-start | bytes 270344 | tf_op jit(solution)/shard_map/ppermute | solution.py:15

commit v9 on v7

--- a/solution.py
+++ b/solution.py
@@ -462,7 +462,7 @@
     depth, own = protocols.shape
     z = Sizes(depth, solved.shape[0], w_out.shape[0], w_out.shape[1], own, n_row)
     bits = bits_of(n_col)
-    joined = bits[1]
+    joined = bits[-1]
     shared = [bit for bit in bits if bit != joined]
     limit = 12 if n_row <= 4 else 48
     f32 = functools.partial(jax.ShapeDtypeStruct, dtype=F32)

time: 30.2 us -> 30.2 us (level)
  no operation moved by 1% of the time
where the time goes in v9:
time: 30.2 us; the launch traced here: 29.9 us
  starting transfers between devices  14.9 us (49%)
  waiting for transfers between devices  6.91 us (23%)
  Pallas kernels  6.64 us (22%)
  between operations  0.74 us (2%)
  local copies, waits for them, and re-layouts  0.68 us (2%)
    ppermute x10, starting transfers between devices, swap(): return lax.ppermute(value, axis, [(i, i ^ bit) for i in range(size)])  14.9 us
    ppermute x10, waiting for transfers between devices, swap(): return lax.ppermute(value, axis, [(i, i ^ bit) for i in range(size)])  6.91 us
    pallas_call x8, Pallas kernels, call(): pl.pallas_call(kernel, out_shape=tuple(outs), in_specs=[pl.BlockSpec(memo...  6.64 us
    unnamed x6, local copies, waits for them, and re-layouts  0.68 us
  transfers between devices with their start and end apart: 10, of which 6 were waited for; matrix products, arithmetic and copies ran while one was open for 0% of the time, Pallas kernels for 13%

profile of v9, /device:TPU:0, one launch (start us, length us, event | category | flops | bytes accessed | tf_op | source)
XLA Modules:
  0.0 29.9 jit_solution(8954997671183978339)
XLA Ops:
  0.6 0.5 %collective-permute-start.1 = (f32[32,128]{1,0:T(8,128)}, f32[32,128]{1,0:T(8,128)S(1)}, u32[]{:S(2)}, u32[]{:S(2)}) collective-permute-start(f32[32,128]{1,0:T(8,128)} %vec_hbm.1), channel_id=1, source_target_pairs={{0,1},{1,0},{2,3},{3,2},{4,5},{5,4},{6,7},{7,6},{8,9},{9,8},{10,11... | collective-permute-start | bytes 49160 | tf_op jit(solution)/shard_map/ppermute | solution.py:15
  1.1 0.1 collective-permute-start
  1.2 0.8 %prepare.1 = (f32[56,128]{1,0:T(8,128)S(1)}, f32[56,128]{1,0:T(8,128)S(1)}, s32[8,128]{1,0:T(8,128)S(1)}) custom-call(s32[4]{0:T(128)} %blocks_hbm.1, f32[20,128]{1,0:T(8,128)} %in_hbm.1, f32[32,128]{1,0:T(8,128)} %vec_hbm.1, f32[32,128]{1,0:T(8,128)} %probes_hbm.1), custom_call_target="tpu_custom_call" | custom-call | flops 100000000 | bytes 1000000 | tf_op jit(solution)/shard_map/prepare/pallas_call | solution.py:449
  2.0 0.5 %collective-permute-done.far_in = f32[20,128]{1,0:T(8,128)S(1)} collective-permute-done((f32[20,128]{1,0:T(8,128)}, f32[20,128]{1,0:T(8,128)S(1)}, u32[]{:S(2)}, u32[]{:S(2)}) %collective-permute-start) | collective-permute-done | bytes 10272 | tf_op jit(solution)/shard_map/ppermute | solution.py:15
  2.5 0.0 collective-permute-done.1.far_vec
  2.6 0.0 copy-start
  2.6 0.0 copy-start.1
  2.6 2.7 %collective-permute-start.2 = (f32[112,128]{1,0:T(8,128)S(1)}, f32[112,128]{1,0:T(8,128)S(1)}, u32[]{:S(2)}, u32[]{:S(2)}) collective-permute-start(f32[112,128]{1,0:T(8,128)S(1)} %pad_maximum_fusion.1), channel_id=1, source_target_pairs={{0,4},{1,5},{2,6},{3,7},{4,0},{5,1},{6,2},{7,3},{8,12},{9,13},{10,... | collective-permute-start | bytes 172040 | tf_op jit(solution)/shard_map/ppermute | solution.py:15
  5.3 0.0 copy-start.2
  5.3 0.0 copy-done
  5.3 0.0 copy-done.1
  5.4 0.7 %copy-done.2 = f32[256]{0:T(256)S(1)} copy-done((f32[256]{0:T(256)S(1)}, f32[256]{0:T(256)}, u32[]{:S(2)}) %copy-start.2) | copy-done | bytes 1048
  6.0 0.1 weights.1
  6.2 1.6 %collective-permute-done.2 = f32[112,128]{1,0:T(8,128)S(1)} collective-permute-done((f32[112,128]{1,0:T(8,128)S(1)}, f32[112,128]{1,0:T(8,128)S(1)}, u32[]{:S(2)}, u32[]{:S(2)}) %collective-permute-start.2) | collective-permute-done | bytes 57376 | tf_op jit(solution)/shard_map/ppermute | solution.py:15
  7.8 1.7 %collective-permute-start.3 = (f32[56,128]{1,0:T(8,128)S(1)}, f32[56,128]{1,0:T(8,128)S(1)}, u32[]{:S(2)}, u32[]{:S(2)}) collective-permute-start(f32[56,128]{1,0:T(8,128)S(1)} %get-tuple-element.69), channel_id=1, source_target_pairs={{0,2},{1,3},{2,0},{3,1},{4,6},{5,7},{6,4},{7,5},{8,10},{9,11},{10,... | collective-permute-start | bytes 86024 | tf_op jit(solution)/shard_map/ppermute | solution.py:15
  9.5 2.6 %collective-permute-start.6 = (f32[112,128]{1,0:T(8,128)S(1)}, f32[112,128]{1,0:T(8,128)S(1)}, u32[]{:S(2)}, u32[]{:S(2)}) collective-permute-start(f32[112,128]{1,0:T(8,128)S(1)} %pad_maximum_fusion.3), channel_id=1, source_target_pairs={{0,16},{8,24},{16,0},{24,8},{1,17},{9,25},{17,1},{25,9},{2,18},{10... | collective-permute-start | bytes 172040 | tf_op jit(solution)/shard_map/ppermute | solution.py:15
  12.1 0.0 collective-permute-done.3
  12.1 2.4 %collective-permute-start.4 = (f32[56,128]{1,0:T(8,128)S(1)}, f32[56,128]{1,0:T(8,128)S(1)}, u32[]{:S(2)}, u32[]{:S(2)}) collective-permute-start(f32[56,128]{1,0:T(8,128)S(1)} %broadcast_select_fusion), channel_id=1, source_target_pairs={{0,16},{8,24},{16,0},{24,8},{1,17},{9,25},{17,1},{25,9},{2,18},{10... | collective-permute-start | bytes 86024 | tf_op jit(solution)/shard_map/ppermute | solution.py:15
  14.5 0.4 %collective-permute-done.6 = f32[112,128]{1,0:T(8,128)S(1)} collective-permute-done((f32[112,128]{1,0:T(8,128)S(1)}, f32[112,128]{1,0:T(8,128)S(1)}, u32[]{:S(2)}, u32[]{:S(2)}) %collective-permute-start.6) | collective-permute-done | bytes 57376 | tf_op jit(solution)/shard_map/ppermute | solution.py:15
  14.9 1.6 %collective-permute-start.7 = (f32[224,128]{1,0:T(8,128)S(1)}, f32[224,128]{1,0:T(8,128)S(1)}, u32[]{:S(2)}, u32[]{:S(2)}) collective-permute-start(f32[224,128]{1,0:T(8,128)S(1)} %pad_maximum_fusion.columns_ref), channel_id=1, source_target_pairs={{0,8},{8,0},{16,24},{24,16},{1,9},{9,1},{17,25},{25,17},{2,10},{10... | collective-permute-start | bytes 344072 | tf_op jit(solution)/shard_map/ppermute | solution.py:15
  16.5 0.4 %collective-permute-done.4 = f32[56,128]{1,0:T(8,128)S(1)} collective-permute-done((f32[56,128]{1,0:T(8,128)S(1)}, f32[56,128]{1,0:T(8,128)S(1)}, u32[]{:S(2)}, u32[]{:S(2)}) %collective-permute-start.4) | collective-permute-done | bytes 28704 | tf_op jit(solution)/shard_map/ppermute | solution.py:15
  16.9 1.9 %collective-permute-start.5 = (f32[112,128]{1,0:T(8,128)S(1)}, f32[112,128]{1,0:T(8,128)S(1)}, u32[]{:S(2)}, u32[]{:S(2)}) collective-permute-start(f32[112,128]{1,0:T(8,128)S(1)} %pad_maximum_fusion.2.windows_ref), channel_id=1, source_target_pairs={{0,8},{8,0},{16,24},{24,16},{1,9},{9,1},{17,25},{25,17},{2,10},{10... | collective-permute-start | bytes 172040 | tf_op jit(solution)/shard_map/ppermute | solution.py:15
  18.8 1.2 %near.1 = (f32[24,256]{1,0:T(8,128)S(1)}, bf16[256,256]{1,0:T(8,128)(2,1)S(1)}, bf16[256,256]{1,0:T(8,128)(2,1)S(1)}, bf16[144,256]{1,0:T(8,128)(2,1)S(1)}, bf16...) custom-call(f32[112,128]{1,0:T(8,128)S(1)} %pad_maximum_fusion.2.win, ...), custom_call_target="tpu_custom_call" | custom-call | flops 1000000000 | bytes 1000000 | tf_op jit(solution)/shard_map/near/pallas_call | solution.py:449
  20.0 0.0 collective-permute-done.7.columns_ref
  20.0 1.2 %far.1 = (f32[24,512]{1,0:T(8,128)S(1)}, bf16[512,256]{1,0:T(8,128)(2,1)S(1)}, bf16[512,256]{1,0:T(8,128)(2,1)S(1)}, f32[512,256]{1,0:T(8,128)S(1)}, bf16[512,12...) custom-call(f32[224,128]{1,0:T(8,128)S(1)} %collective-permute-done., ...), custom_call_target="tpu_custom_call" | custom-call | flops 1000000000 | bytes 1000000 | tf_op jit(solution)/shard_map/far/pallas_call | solution.py:449
  21.2 0.0 collective-permute-done.5.windows_ref
  21.2 2.1 %late.1 = (f32[64,128]{1,0:T(8,128)S(1)}, f32[88,256]{1,0:T(8,128)S(1)}) custom-call(f32[112,128]{1,0:T(8,128)S(1)} %collective-permute-done.5.windows_ref, bf16[144,256]{1,0:T(8,128)(2,1)S(1)} %get-tuple-element.70.refs_0_, bf16[512,128]{1,0:T(8,128)(2,1)S(1)} %get-tuple-element.71.refs_1_, bf16[256,256]{1,0:T(8,128)(2,1)S(1)} %get-tuple-element.72.refs_2_, ...), custom_call_target="tpu_custom_call" | custom-call | flops 2000000000 | bytes 1000000 | tf_op jit(solution)/shard_map/late/pallas_call | solution.py:449
  23.3 1.3 %collective-permute-start.8 = (f32[88,256]{1,0:T(8,128)S(1)}, f32[88,256]{1,0:T(8,128)S(1)}, u32[]{:S(2)}, u32[]{:S(2)}) collective-permute-start(f32[88,256]{1,0:T(8,128)S(1)} %get-tuple-element.104), channel_id=1, source_target_pairs={{0,2},{1,3},{2,0},{3,1},{4,6},{5,7},{6,4},{7,5},{8,10},{9,11},{10,... | collective-permute-start | bytes 270344 | tf_op jit(solution)/shard_map/ppermute | solution.py:15
  24.6 3.3 %collective-permute-done.8 = f32[88,256]{1,0:T(8,128)S(1)} collective-permute-done((f32[88,256]{1,0:T(8,128)S(1)}, f32[88,256]{1,0:T(8,128)S(1)}, u32[]{:S(2)}, u32[]{:S(2)}) %collective-permute-start.8) | collective-permute-done | bytes 90144 | tf_op jit(solution)/shard_map/ppermute | solution.py:15
  27.9 0.1 collective-permute-start.9
  28.0 0.6 %emit.1 = f32[64,128]{1,0:T(8,128)} custom-call(f32[64,128]{1,0:T(8,128)S(1)} %get-tuple-element.103.own_ref), custom_call_target="tpu_custom_call" | custom-call | flops 100000000 | bytes 1000000 | tf_op jit(solution)/shard_map/emit/pallas_call | solution.py:449
  28.6 0.7 %collective-permute-done.9.theirs_ref = f32[88,256]{1,0:T(8,128)S(1)} collective-permute-done((f32[88,256]{1,0:T(8,128)S(1)}, f32[88,256]{1,0:T(8,128)S(1)}, u32[]{:S(2)}, u32[]{:S(2)}) %collective-permute-start.9) | collective-permute-done | bytes 90144 | tf_op jit(solution)/shard_map/ppermute | solution.py:15
  29.3 0.6 %finish.1 = (f32[20,256]{1,0:T(8,128)}, f32[1,256]{1,0:T(1,128)}, f32[64,256]{1,0:T(8,128)}) custom-call(f32[88,256]{1,0:T(8,128)S(1)} %add.3.mine_ref, f32[88,256]{1,0:T(8,128)S(1)} %collective-permute-done.9.theirs_ref), custom_call_target="tpu_custom_call" | custom-call | flops 100000000 | bytes 1000000 | tf_op jit(solution)/shard_map/finish/pallas_call | solution.py:449
  (9 shorter events, 0.1 us)
Async XLA Ops:
  0.6 1.9 %collective-permute-start.1 = (f32[32,128]{1,0:T(8,128)}, f32[32,128]{1,0:T(8,128)S(1)}, u32[]{:S(2)}, u32[]{:S(2)}) collective-permute-start(f32[32,128]{1,0:T(8,128)} %vec_hbm.1), channel_id=1, source_target_pairs={{0,1},{1,0},{2,3},{3,2},{4,5},{5,4},{6,7},{7,6},{8,9},{9,8},{10,11... | collective-permute-start | bytes 49160 | tf_op jit(solution)/shard_map/ppermute | solution.py:15
  1.1 1.4 %collective-permute-start = (f32[20,128]{1,0:T(8,128)}, f32[20,128]{1,0:T(8,128)S(1)}, u32[]{:S(2)}, u32[]{:S(2)}) collective-permute-start(f32[20,128]{1,0:T(8,128)} %in_hbm.1), channel_id=1, source_target_pairs={{0,1},{1,0},{2,3},{3,2},{4,5},{5,4},{6,7},{7,6},{8,9},{9,8},{10,11... | collective-permute-start | bytes 30728 | tf_op jit(solution)/shard_map/ppermute | solution.py:15
  2.6 2.8 %copy-start = (f32[256,64]{0,1:T(8,128)S(1)}, f32[256,64]{0,1:T(8,128)}, u32[]{:S(2)}) copy-start(f32[256,64]{0,1:T(8,128)} %param.10) | copy-start | bytes 196612
  2.6 2.8 %copy-start.1 = (f32[20,256]{1,0:T(8,128)S(1)}, f32[20,256]{1,0:T(8,128)}, u32[]{:S(2)}) copy-start(f32[20,256]{1,0:T(8,128)} %param.8) | copy-start | bytes 61444
  2.6 5.2 %collective-permute-start.2 = (f32[112,128]{1,0:T(8,128)S(1)}, f32[112,128]{1,0:T(8,128)S(1)}, u32[]{:S(2)}, u32[]{:S(2)}) collective-permute-start(f32[112,128]{1,0:T(8,128)S(1)} %pad_maximum_fusion.1), channel_id=1, source_target_pairs={{0,4},{1,5},{2,6},{3,7},{4,0},{5,1},{6,2},{7,3},{8,12},{9,13},{10,... | collective-permute-start | bytes 172040 | tf_op jit(solution)/shard_map/ppermute | solution.py:15
  5.3 0.7 %copy-start.2 = (f32[256]{0:T(256)S(1)}, f32[256]{0:T(256)}, u32[]{:S(2)}) copy-start(f32[256]{0:T(256)} %param.9) | copy-start | bytes 3076
  7.8 4.3 %collective-permute-start.3 = (f32[56,128]{1,0:T(8,128)S(1)}, f32[56,128]{1,0:T(8,128)S(1)}, u32[]{:S(2)}, u32[]{:S(2)}) collective-permute-start(f32[56,128]{1,0:T(8,128)S(1)} %get-tuple-element.69), channel_id=1, source_target_pairs={{0,2},{1,3},{2,0},{3,1},{4,6},{5,7},{6,4},{7,5},{8,10},{9,11},{10,... | collective-permute-start | bytes 86024 | tf_op jit(solution)/shard_map/ppermute | solution.py:15
  9.5 5.4 %collective-permute-start.6 = (f32[112,128]{1,0:T(8,128)S(1)}, f32[112,128]{1,0:T(8,128)S(1)}, u32[]{:S(2)}, u32[]{:S(2)}) collective-permute-start(f32[112,128]{1,0:T(8,128)S(1)} %pad_maximum_fusion.3), channel_id=1, source_target_pairs={{0,16},{8,24},{16,0},{24,8},{1,17},{9,25},{17,1},{25,9},{2,18},{10... | collective-permute-start | bytes 172040 | tf_op jit(solution)/shard_map/ppermute | solution.py:15
  12.1 4.8 %collective-permute-start.4 = (f32[56,128]{1,0:T(8,128)S(1)}, f32[56,128]{1,0:T(8,128)S(1)}, u32[]{:S(2)}, u32[]{:S(2)}) collective-permute-start(f32[56,128]{1,0:T(8,128)S(1)} %broadcast_select_fusion), channel_id=1, source_target_pairs={{0,16},{8,24},{16,0},{24,8},{1,17},{9,25},{17,1},{25,9},{2,18},{10... | collective-permute-start | bytes 86024 | tf_op jit(solution)/shard_map/ppermute | solution.py:15
  14.9 5.1 %collective-permute-start.7 = (f32[224,128]{1,0:T(8,128)S(1)}, f32[224,128]{1,0:T(8,128)S(1)}, u32[]{:S(2)}, u32[]{:S(2)}) collective-permute-start(f32[224,128]{1,0:T(8,128)S(1)} %pad_maximum_fusion.columns_ref), channel_id=1, source_target_pairs={{0,8},{8,0},{16,24},{24,16},{1,9},{9,1},{17,25},{25,17},{2,10},{10... | collective-permute-start | bytes 344072 | tf_op jit(solution)/shard_map/ppermute | solution.py:15
  16.9 4.2 %collective-permute-start.5 = (f32[112,128]{1,0:T(8,128)S(1)}, f32[112,128]{1,0:T(8,128)S(1)}, u32[]{:S(2)}, u32[]{:S(2)}) collective-permute-start(f32[112,128]{1,0:T(8,128)S(1)} %pad_maximum_fusion.2.windows_ref), channel_id=1, source_target_pairs={{0,8},{8,0},{16,24},{24,16},{1,9},{9,1},{17,25},{25,17},{2,10},{10... | collective-permute-start | bytes 172040 | tf_op jit(solution)/shard_map/ppermute | solution.py:15
  23.3 4.6 %collective-permute-start.8 = (f32[88,256]{1,0:T(8,128)S(1)}, f32[88,256]{1,0:T(8,128)S(1)}, u32[]{:S(2)}, u32[]{:S(2)}) collective-permute-start(f32[88,256]{1,0:T(8,128)S(1)} %get-tuple-element.104), channel_id=1, source_target_pairs={{0,2},{1,3},{2,0},{3,1},{4,6},{5,7},{6,4},{7,5},{8,10},{9,11},{10,... | collective-permute-start | bytes 270344 | tf_op jit(solution)/shard_map/ppermute | solution.py:15
  27.9 1.4 %collective-permute-start.9 = (f32[88,256]{1,0:T(8,128)S(1)}, f32[88,256]{1,0:T(8,128)S(1)}, u32[]{:S(2)}, u32[]{:S(2)}) collective-permute-start(f32[88,256]{1,0:T(8,128)S(1)} %add.3.mine_ref), channel_id=1, source_target_pairs={{0,1},{1,0},{2,3},{3,2},{4,5},{5,4},{6,7},{7,6},{8,9},{9,8},{10,11... | collective-permute-start | bytes 270344 | tf_op jit(solution)/shard_map/ppermute | solution.py:15
